TPU v7x, 32 devices: a whole 2x2x4 slice. The times are simulated.
32 devices in a mesh: dp: 4 (over y, core), expert: 8 (over z, x).
Axes of the slice: x: 2, y: 2, z: 4, core: 2. Of those that a mesh axis runs over, the one named last changes fastest.
Arguments:
- frames: bfloat16 [4096, 1024], P(('dp', 'expert')), may hold values from -6 to 6
- cotangent: bfloat16 [4096, 1024], P(('dp', 'expert')), may hold values from -6 to 6
- expert_ids: int32 [4096, 1], P(('dp', 'expert')), may hold values from 0 to 7; in each aligned block of 128 rows (0 to 127, 128 to 255, ...) at most 32 rows name the same one
- conv_weight: float32 [32, 1024], replicated, may hold values from -1 to 1
- up_master: float32 [8, 1024, 2048], P('expert', 'dp'), may hold values from -0.1875 to 0.1875
- down_master: float32 [8, 2048, 1024], P('expert', 'dp'), may hold values from -0.125 to 0.125
- up_mean_code: bfloat16 [8, 1024, 2048], P('expert', 'dp'), may hold values from -1 to 1
- up_mean_scale: float32 [8, 1024, 16], P('expert', 'dp'), may hold values from 0.5 to 5
- up_square_code: bfloat16 [8, 1024, 2048], P('expert', 'dp'), may hold values from 0.049804688 to 1
- up_square_scale: float32 [8, 1024, 16], P('expert', 'dp'), may hold values from 20 to 200
- down_mean_code: bfloat16 [8, 2048, 1024], P('expert', 'dp'), may hold values from -1 to 1
- down_mean_scale: float32 [8, 2048, 8], P('expert', 'dp'), may hold values from 0.5 to 5
- down_square_code: bfloat16 [8, 2048, 1024], P('expert', 'dp'), may hold values from 0.049804688 to 1
- down_square_scale: float32 [8, 2048, 8], P('expert', 'dp'), may hold values from 20 to 200
Outputs:
- grad_frames: bfloat16 [4096, 1024], P(('dp', 'expert'))
- conv_grad: float32 [32, 1024], replicated
- up_next: float32 [8, 1024, 2048], P('expert', 'dp')
- up_mean_next: bfloat16 [8, 1024, 2048], P('expert', 'dp')
- up_mean_scale_next: float32 [8, 1024, 16], P('expert', 'dp')
- up_square_next: bfloat16 [8, 1024, 2048], P('expert', 'dp')
- up_square_scale_next: float32 [8, 1024, 16], P('expert', 'dp')
- down_next: float32 [8, 2048, 1024], P('expert', 'dp')
- down_mean_next: bfloat16 [8, 2048, 1024], P('expert', 'dp')
- down_mean_scale_next: float32 [8, 2048, 8], P('expert', 'dp')
- down_square_next: bfloat16 [8, 2048, 1024], P('expert', 'dp')
- down_square_scale_next: float32 [8, 2048, 8], P('expert', 'dp')
Inputs may be any that keep to these rules, and one draw needn't show every extreme that they name: `expert_ids`: within each device's aligned block of 128 frames no expert is chosen by more than 32 frames, and some expert is chosen by exactly 32 frames.
All inputs are finite; a program needn't handle non-finite values. Where the computation divides by a largest or mean magnitude, that divisor is 1e-20 or more.
Results may differ from a plain program's by a relative error of at most 0.017.
Values may be sent and summed in bfloat16 or wider, within the bound.
No kernel may reach another device: no remote copies, remote signals or barrier semaphores. Data moves between devices by JAX's collectives and lax.ppermute only.
A program may use at most 128 MiB of HBM per device.

v0:
```python
import jax
import jax.numpy as jnp
from jax import lax
from jax.sharding import PartitionSpec as P

beta_one = 0.9
beta_two = 0.95
bias_one = 1.0 - beta_one**10
bias_two = 1.0 - beta_two**10
learn_rate = 0.001
adam_eps = 1e-08
scale_eps = 1e-06


def with_halo(cells, sides, width):
    for axis, dim in sides:
        count = lax.axis_size(axis)
        ends = count - 1
        head = lax.slice_in_dim(cells, 0, width, axis=dim)
        tail = lax.slice_in_dim(cells, cells.shape[dim] - width, cells.shape[dim], axis=dim)
        cells = jnp.concatenate(
            [
                lax.ppermute(tail, axis, [(i, (i + 1) % count) for i in range(ends)]),
                cells,
                lax.ppermute(head, axis, [((i + 1) % count, i) for i in range(ends)]),
            ],
            axis=dim,
        )
    return cells


def swish_parts(values):
    gate_value = jax.nn.sigmoid(values)
    return (values * gate_value, gate_value * (1.0 + values * (1.0 - gate_value)))


def adam_block(master, gradient, mean_code, mean_scale, square_code, square_scale):
    full_shape = master.shape
    block_count = mean_scale.shape[-1]
    blocked = full_shape[:-1] + (block_count, full_shape[-1] // block_count)
    mean_old = mean_code.astype(jnp.float32).reshape(blocked) * mean_scale[..., None]
    square_old = square_code.astype(jnp.float32).reshape(blocked) * square_scale[..., None]
    grad_blocks = gradient.reshape(blocked)
    mean_new = beta_one * mean_old + (1.0 - beta_one) * grad_blocks
    square_new = beta_two * square_old + (1.0 - beta_two) * grad_blocks * grad_blocks
    update = mean_new / bias_one / (jnp.sqrt(square_new / bias_two) + adam_eps)
    master_new = master - learn_rate * update.reshape(full_shape)
    mean_top = jnp.max(jnp.abs(mean_new), axis=-1) + scale_eps
    square_top = jnp.max(square_new, axis=-1) + scale_eps
    mean_codes = (mean_new / mean_top[..., None]).reshape(full_shape).astype(jnp.bfloat16)
    square_codes = (square_new / square_top[..., None]).reshape(full_shape).astype(jnp.bfloat16)
    return (master_new, mean_codes, mean_top, square_codes, square_top)


def body(
    frames,
    cotangent,
    expert_ids,
    conv_weight,
    up_master,
    down_master,
    up_mean_code,
    up_mean_scale,
    up_square_code,
    up_square_scale,
    down_mean_code,
    down_mean_scale,
    down_square_code,
    down_square_scale,
):
    length = frames.shape[0]
    model_width = frames.shape[1]
    tap_count = conv_weight.shape[0]
    half_taps = tap_count // 2
    experts = lax.axis_size("expert")
    capacity = 2 * length // experts
    padded = with_halo(frames, ((("dp", "expert"), 0),), half_taps).astype(jnp.float32)
    convolved = jnp.zeros((length, model_width), jnp.float32)
    for tap_index in range(tap_count):
        convolved = convolved + conv_weight[tap_index] * padded[tap_index : tap_index + length]
    activated, conv_slope = swish_parts(convolved)
    features = activated.astype(jnp.bfloat16)
    chosen = expert_ids[:, 0]
    one_hot = (chosen[:, None] == jnp.arange(experts, dtype=jnp.int32)[None, :]).astype(jnp.int32)
    ranks = jnp.cumsum(one_hot, axis=0) - one_hot
    slot_index = jnp.sum(ranks * one_hot, axis=1)
    position = chosen * capacity + slot_index
    empty_rows = jnp.zeros((experts * capacity, model_width), jnp.bfloat16)
    send_rows = empty_rows.at[position].set(features).reshape(experts, capacity, model_width)
    send_grads = empty_rows.at[position].set(cotangent).reshape(experts, capacity, model_width)
    recv_rows, recv_grads = (
        lax.all_to_all(send_rows, "expert", split_axis=0, concat_axis=0, tiled=True),
        lax.all_to_all(send_grads, "expert", split_axis=0, concat_axis=0, tiled=True),
    )
    rows_in = recv_rows.reshape(-1, model_width)
    grads_in = recv_grads.reshape(-1, model_width)
    up_full, down_full = (
        lax.all_gather(up_master.astype(jnp.bfloat16), "dp", axis=1, tiled=True),
        lax.all_gather(down_master.astype(jnp.bfloat16), "dp", axis=1, tiled=True),
    )
    up_weight = up_full[0]
    down_weight = down_full[0]
    pre_act = jnp.dot(rows_in, up_weight, preferred_element_type=jnp.float32)
    hidden_act, hidden_slope = swish_parts(pre_act)
    hidden = hidden_act.astype(jnp.bfloat16)
    down_part = jnp.einsum("rh,rd->hd", hidden, grads_in, preferred_element_type=jnp.float32)
    grad_hidden = jnp.einsum("rd,hd->rh", grads_in, down_weight, preferred_element_type=jnp.float32)
    grad_pre = (grad_hidden * hidden_slope).astype(jnp.bfloat16)
    up_part = jnp.einsum("rd,rh->dh", rows_in, grad_pre, preferred_element_type=jnp.float32)
    grad_rows = jnp.einsum("rh,dh->rd", grad_pre, up_weight, preferred_element_type=jnp.float32)
    grad_rows = grad_rows.astype(jnp.bfloat16).reshape(experts, capacity, model_width)
    returned = lax.all_to_all(grad_rows, "expert", split_axis=0, concat_axis=0, tiled=True)
    grad_features = returned.reshape(-1, model_width)[position]
    grad_conv = (grad_features.astype(jnp.float32) * conv_slope).astype(jnp.bfloat16)
    grad_padded = with_halo(grad_conv, ((("dp", "expert"), 0),), half_taps).astype(jnp.float32)
    grad_total = cotangent.astype(jnp.float32)
    for tap_index in range(tap_count):
        start = tap_count - tap_index
        grad_total = grad_total + conv_weight[tap_index] * grad_padded[start : start + length]
    grad_local = grad_padded[half_taps : half_taps + length]
    conv_terms = jnp.stack(
        [
            jnp.sum(grad_local * padded[tap_index : tap_index + length], axis=0)
            for tap_index in range(tap_count)
        ]
    )
    conv_total = lax.psum(conv_terms, ("dp", "expert"))
    share_up, share_down = (
        lax.psum_scatter(
            up_part[None].astype(jnp.bfloat16), "dp", scatter_dimension=1, tiled=True
        ).astype(jnp.float32),
        lax.psum_scatter(
            down_part[None].astype(jnp.bfloat16), "dp", scatter_dimension=1, tiled=True
        ).astype(jnp.float32),
    )
    up_next, up_mean_next, up_mean_scale_next, up_square_next, up_square_scale_next = adam_block(
        up_master, share_up, up_mean_code, up_mean_scale, up_square_code, up_square_scale
    )
    down_next, down_mean_next, down_mean_scale_next, down_square_next, down_square_scale_next = (
        adam_block(
            down_master,
            share_down,
            down_mean_code,
            down_mean_scale,
            down_square_code,
            down_square_scale,
        )
    )
    return (
        grad_total.astype(jnp.bfloat16),
        conv_total,
        up_next,
        up_mean_next,
        up_mean_scale_next,
        up_square_next,
        up_square_scale_next,
        down_next,
        down_mean_next,
        down_mean_scale_next,
        down_square_next,
        down_square_scale_next,
    )


def solution(mesh):
    return jax.shard_map(
        body,
        mesh=mesh,
        in_specs=(
            P(("dp", "expert"), None),
            P(("dp", "expert"), None),
            P(("dp", "expert"), None),
            P(),
            P("expert", "dp", None),
            P("expert", "dp", None),
            P("expert", "dp", None),
            P("expert", "dp", None),
            P("expert", "dp", None),
            P("expert", "dp", None),
            P("expert", "dp", None),
            P("expert", "dp", None),
            P("expert", "dp", None),
            P("expert", "dp", None),
        ),
        out_specs=(
            P(("dp", "expert"), None),
            P(),
            P("expert", "dp", None),
            P("expert", "dp", None),
            P("expert", "dp", None),
            P("expert", "dp", None),
            P("expert", "dp", None),
            P("expert", "dp", None),
            P("expert", "dp", None),
            P("expert", "dp", None),
            P("expert", "dp", None),
            P("expert", "dp", None),
        ),
        check_vma=False,
    )
```

profile of v0, /device:TPU:0, one launch (start us, length us, event | category | flops | bytes accessed | tf_op | source)
XLA Modules:
  0.0 395.1 jit_solution(14302484131352905360)
XLA Ops:
  7.3 2.8 convert_element_type.94
  11.4 5.5 %collective-permute-start = (bf16[16,1024]{1,0:T(8,128)(2,1)S(1)}, bf16[16,1024]{1,0:T(8,128)(2,1)S(1)}, u32[]{:S(2)}, u32[]{:S(2)}) collective-permute-start(bf16[16,1024]{1,0:T(8,128)(2,1)S(1)} %get-tuple-element.78), channel_id=1, source_target_pairs={{0,1},{1,2},{2,3},{3,4},{4,5},{5,6},{6,7},{7,8},{8,9},{9,10},{10,1... | collective-permute-start | bytes 98312 | tf_op jit(solution)/shard_map/ppermute | solution.py:23
  18.5 4.1 %scatter_custom_fusion.1 = bf16[256,1024]{1,0:T(8,128)(2,1)} fusion(s32[128]{0:T(128)S(1)} %fusion.77, f32[]{:T(128)} %constant.20.clone.1, bf16[]{:T(256)} %constant.16.clone.1, f32[160,1024]{1,0:T(8,128)S(1)} %maximum_convert_fusion, f32[1024]{0:T(1024)S(1)} %bitcast.285, f32[1024]{0:T(1024)S(1)} %bitcast.288, f32[1024]{0:T(1024)S(1)} %bitcast.198, ...), kind=kCustom, calls=%fused_computation.171 | custom fusion | flops 8912896 | bytes 17432582 | tf_op jit(solution)/shard_map/scatter | solution.py:89
  22.9 8.9 %all-to-all-start.1 = ((bf16[8,32,1024]{2,1,0:T(8,128)(2,1)}), bf16[8,32,1024]{2,1,0:T(8,128)(2,1)S(1)}, u32[]{:S(2)}, u32[]{:S(2)}) async-start(bf16[8,32,1024]{2,1,0:T(8,128)(2,1)} %bitcast.38), calls=%async_computation.1 | async-start | bytes 1048576 | tf_op jit(solution)/shard_map/all_to_all | solution.py:92
  31.8 2.4 scatter_custom_fusion
  34.2 12.0 %all-to-all-done.1 = bf16[8,32,1024]{2,1,0:T(8,128)(2,1)S(1)} async-done(((bf16[8,32,1024]{2,1,0:T(8,128)(2,1)}), bf16[8,32,1024]{2,1,0:T(8,128)(2,1)S(1)}, u32[]{:S(2)}, u32[]{:S(2)}) %all-to-all-start.1) | async-done | bytes 524320 | tf_op jit(solution)/shard_map/all_to_all | solution.py:92
  46.2 5.1 %all-to-all-start = ((bf16[8,32,1024]{2,1,0:T(8,128)(2,1)}), bf16[8,32,1024]{2,1,0:T(8,128)(2,1)S(1)}, u32[]{:S(2)}, u32[]{:S(2)}) async-start(bf16[8,32,1024]{2,1,0:T(8,128)(2,1)} %bitcast.4), calls=%async_computation | async-start | bytes 1048576 | tf_op jit(solution)/shard_map/all_to_all | solution.py:93
  51.3 4.8 %fusion.2 = f32[256,2048]{1,0:T(8,128)} fusion(bf16[256,1024]{1,0:T(8,128)(2,1)S(1)} %bitcast.190, bf16[1,1024,2048]{2,1,0:T(8,128)(2,1)} %all-gather.5.cloned.1.call-done), kind=kOutput, calls=%fused_computation.5 | convolution fusion | flops 1073741824 | bytes 6815744 | tf_op jit(solution)/shard_map/dot_general | solution.py:103
  56.1 9.9 %all-to-all-done = bf16[8,32,1024]{2,1,0:T(8,128)(2,1)S(1)} async-done(((bf16[8,32,1024]{2,1,0:T(8,128)(2,1)}), bf16[8,32,1024]{2,1,0:T(8,128)(2,1)S(1)}, u32[]{:S(2)}, u32[]{:S(2)}) %all-to-all-start) | async-done | bytes 524320 | tf_op jit(solution)/shard_map/all_to_all | solution.py:93
  66.0 5.1 %convert_bitcast_fusion = bf16[1,2048,1024]{2,1,0:T(8,128)(2,1)} fusion(bf16[256,1024]{1,0:T(8,128)(2,1)S(1)} %bitcast.192, f32[256,2048]{1,0:T(8,128)} %fusion.2), kind=kOutput, calls=%fused_computation.9 | convolution fusion | flops 1078460416 | bytes 6815744 | tf_op jit(solution)/shard_map/rh,rd->hd/dot_general | solution.py:106
  73.1 1.8 copy.67
  75.1 1.8 copy.65
  76.9 1.9 mul.1262
  78.8 2.3 mul.1263
  81.0 2.9 mul.1253
  84.0 2.7 mul.1254
  86.7 29.6 %reduce-scatter.5.cloned.1.call-done = bf16[1,512,1024]{2,1,0:T(8,128)(2,1)} async-done(((bf16[1,2048,1024]{2,1,0:T(8,128)(2,1)}), bf16[1,512,1024]{2,1,0:T(8,128)(2,1)}) %reduce-scatter.5.cloned.1.call-update) | async-done | bytes 1048592 | tf_op jit(solution)/shard_map/reduce_scatter | solution.py:132
  116.3 1.5 convert_bitcast_fusion.2
  120.0 14.2 %fusion.23 = (f32[512,8]{1,0:T(8,128)S(1)}, f32[512,8]{1,0:T(8,128)S(1)}) fusion(f32[512,8]{1,0:T(8,128)S(1)} %copy.55, f32[512,8]{1,0:T(8,128)S(1)} %copy-done.9, f32[1,512,8,128]{3,2,1,0:T(8,128)S(1)} %bitcast.184, f32[1,512,8,128]{3,2,1,0:T(8,128)S(1)} %bitcast.186, f32[1,512,8,128]{3,2,1,0:T(8,128)S(1)} %bitcast.185), kind=kLoop, calls=%fused_computation.42 | loop fusion | flops 6283264 | bytes 6356992 | tf_op jit(solution)/shard_map/reduce_max | solution.py:49
  135.0 1.9 div.121
  137.0 2.7 div.122
  139.7 1.9 div.118
  141.6 2.7 div.119
  144.3 8.2 %divide_convert_fusion = (bf16[1,512,1024]{2,1,0:T(8,128)(2,1)}, f32[1,512,1024]{2,1,0:T(8,128)}, bf16[1,512,1024]{2,1,0:T(8,128)(2,1)}, bf16[1,512,1024]{2,1,0:T(8,128)(2,1)}) fusion(f32[1,512,1024]{2,1,0:T(8,128)} %div.122, bf16[1,512,1024]{2,1,0:T(8,128)(2,1)} %reduce-scatter.5.cloned.1.call-done, f32[1,512,1024]{2,1,0:T(8,128)S(1)} %mul.1263, ...), kind=kLoop, calls=%fused_computation.59 | loop fusion | flops 12058624 | bytes 18874368 | tf_op jit(solution)/shard_map/convert_element_type | solution.py:51
  152.9 34.4 %all-gather.3.cloned.1.call-done = bf16[1,2048,1024]{2,1,0:T(8,128)(2,1)} async-done(((bf16[1,512,1024]{2,1,0:T(8,128)(2,1)}), bf16[1,2048,1024]{2,1,0:T(8,128)(2,1)}) %all-gather.3.cloned.1.call-update) | async-done | bytes 4194320 | tf_op jit(solution)/shard_map/all_gather | solution.py:99
  187.2 4.5 %fusion.9 = bf16[256,2048]{1,0:T(8,128)(2,1)S(1)} fusion(bf16[256,1024]{1,0:T(8,128)(2,1)} %bitcast.193, bf16[1,2048,1024]{2,1,0:T(8,128)(2,1)} %all-gather.3.cloned.1.call-done, f32[256,2048]{1,0:T(8,128)} %fusion.2), kind=kOutput, calls=%fused_computation.30 | convolution fusion | flops 1078460416 | bytes 7864320 | tf_op jit(solution)/shard_map/rd,hd->rh/dot_general | solution.py:107
  192.7 3.2 convert_bitcast_fusion.1
  197.2 4.4 %fusion.34 = bf16[256,1024]{1,0:T(8,128)(2,1)} fusion(bf16[256,2048]{1,0:T(8,128)(2,1)S(1)} %copy-done.16, bf16[1,1024,2048]{2,1,0:T(8,128)(2,1)} %all-gather.5.cloned.1.call-done), kind=kOutput, calls=%fused_computation.67 | convolution fusion | flops 1074003968 | bytes 5767168 | tf_op jit(solution)/shard_map/rh,dh->rd/dot_general | solution.py:110
  201.5 5.5 %all-to-all-start.2 = ((bf16[8,32,1024]{2,1,0:T(8,128)(2,1)}), bf16[8,32,1024]{2,1,0:T(8,128)(2,1)S(1)}, u32[]{:S(2)}, u32[]{:S(2)}) async-start(bf16[8,32,1024]{2,1,0:T(8,128)(2,1)} %bitcast.194), calls=%async_computation.2 | async-start | bytes 1048576 | tf_op jit(solution)/shard_map/all_to_all | solution.py:112
  207.4 1.6 convert_bitcast_fusion.6
  209.0 13.0 %all-to-all-done.2 = bf16[8,32,1024]{2,1,0:T(8,128)(2,1)S(1)} async-done(((bf16[8,32,1024]{2,1,0:T(8,128)(2,1)}), bf16[8,32,1024]{2,1,0:T(8,128)(2,1)S(1)}, u32[]{:S(2)}, u32[]{:S(2)}) %all-to-all-start.2) | async-done | bytes 524320 | tf_op jit(solution)/shard_map/all_to_all | solution.py:112
  223.1 2.4 multiply_convert_fusion.2
  226.9 5.1 %collective-permute-start.2 = (bf16[16,1024]{1,0:T(8,128)(2,1)S(1)}, bf16[16,1024]{1,0:T(8,128)(2,1)}, u32[]{:S(2)}, u32[]{:S(2)}) collective-permute-start(bf16[16,1024]{1,0:T(8,128)(2,1)S(1)} %get-tuple-element.76), channel_id=1, source_target_pairs={{0,1},{1,2},{2,3},{3,4},{4,5},{5,6},{6,7},{7,8},{8,9},{9,10},{10,1... | collective-permute-start | bytes 98312 | tf_op jit(solution)/shard_map/ppermute | solution.py:23
  232.1 1.6 convert_bitcast_fusion.7
  233.9 2.2 copy.64
  236.2 1.7 copy.62
  237.9 1.9 mul.1229
  239.9 2.8 mul.1230
  242.7 2.0 mul.1221
  244.7 2.8 mul.1222
  254.4 5.5 %stack.131 = f32[32,1024]{1,0:T(8,128)} concatenate(f32[1,1024]{1,0:T(1,128)} %bitcast.300, f32[1,1024]{1,0:T(1,128)} %bitcast.301, f32[1,1024]{1,0:T(1,128)} %bitcast.302, f32[1,1024]{1,0:T(1,128)} %bitcast.303, f32[1,1024]{1,0:T(1,128)} %bitcast.304, f32[1,1024]{1,0:T(1,128)} %bitcast.317, f32[1,1024]{1,0:T(1,128)} %bitcast.316, f32[1,1024]{1,0:T(1,128)} %bitcast.315, ...), dimensions={0} | concatenate | bytes 262144 | tf_op jit(solution)/shard_map/stack | solution.py:121
  259.9 3.8 fusion.39
  266.8 7.0 %fusion.21 = (f32[256,16]{1,0:T(8,128)S(1)}, f32[256,16]{1,0:T(8,128)S(1)}) fusion(f32[256,16]{1,0:T(8,128)S(1)} %copy.51, f32[256,16]{1,0:T(8,128)S(1)} %copy-done.12, f32[1,256,16,128]{3,2,1,0:T(8,128)S(1)} %bitcast.187, f32[1,256,16,128]{3,2,1,0:T(8,128)S(1)} %bitcast.189, f32[1,256,16,128]{3,2,1,0:T(8,128)S(1)} %bitcast.188), kind=kLoop, calls=%fused_computation.40 | loop fusion | flops 6283264 | bytes 6356992 | tf_op jit(solution)/shard_map/reduce_max | solution.py:49
  276.0 1.9 div.107
  277.9 2.9 div.108
  280.8 6.7 %divide_convert_fusion.2 = (bf16[1,256,2048]{2,1,0:T(8,128)(2,1)}, f32[1,256,2048]{2,1,0:T(8,128)}, bf16[1,256,2048]{2,1,0:T(8,128)(2,1)}) fusion(f32[1,256,2048]{2,1,0:T(8,128)} %div.111, bf16[1,256,2048]{2,1,0:T(8,128)(2,1)} %reduce-scatter.3.cloned.1.call-done, f32[1,256,2048]{2,1,0:T(8,128)} %mul.1230, bf16[1,256,2048]{2,1,0:T(8,128)(2,1)} %param.22, ...), kind=kLoop, calls=%fused_computation.63 | loop fusion | flops 11534336 | bytes 17825792 | tf_op jit(solution)/shard_map/convert_element_type | solution.py:51
  288.8 98.2 %all-reduce.2.cloned.1.call-done = f32[32,1024]{1,0:T(8,128)} async-done(((f32[32,1024]{1,0:T(8,128)}), f32[32,1024]{1,0:T(8,128)}) %all-reduce.2.cloned.1.call-update) | async-done | bytes 131088 | tf_op jit(solution)/shard_map/psum | solution.py:127
  387.0 1.6 copy.69
  (219 shorter events, 26.8 us)
Async XLA Ops:
  7.2 9.7 %copy-start.81 = (s32[128,1]{0,1:T(1,128)S(1)}, s32[128,1]{0,1:T(1,128)}, u32[]{:S(2)}) copy-start(s32[128,1]{0,1:T(1,128)} %param.16) | copy-start | bytes 1540
  7.2 10.1 %copy-start.19 = (f32[32,1024]{1,0:T(8,128)S(1)}, f32[32,1024]{1,0:T(8,128)}, u32[]{:S(2)}) copy-start(f32[32,1024]{1,0:T(8,128)} %param.17) | copy-start | bytes 393220
  7.2 44.1 %all-gather.5.cloned.1.call-start = ((), (), s32[]{:S(2)}) async-start(), calls=%async_computation.6 | async-start | bytes 5242880 | tf_op jit(solution)/shard_map/all_gather | solution.py:98
  10.1 7.7 %collective-permute-start.1 = (bf16[16,1024]{1,0:T(8,128)(2,1)S(1)}, bf16[16,1024]{1,0:T(8,128)(2,1)S(1)}, u32[]{:S(2)}, u32[]{:S(2)}) collective-permute-start(bf16[16,1024]{1,0:T(8,128)(2,1)S(1)} %get-tuple-element.79), channel_id=1, source_target_pairs={{1,0},{2,1},{3,2},{4,3},{5,4},{6,5},{7,6},{8,7},{9,8},{10,9},{11,1... | collective-permute-start | bytes 98312 | tf_op jit(solution)/shard_map/ppermute | solution.py:25
  11.4 7.1 %collective-permute-start = (bf16[16,1024]{1,0:T(8,128)(2,1)S(1)}, bf16[16,1024]{1,0:T(8,128)(2,1)S(1)}, u32[]{:S(2)}, u32[]{:S(2)}) collective-permute-start(bf16[16,1024]{1,0:T(8,128)(2,1)S(1)} %get-tuple-element.78), channel_id=1, source_target_pairs={{0,1},{1,2},{2,3},{3,4},{4,5},{5,6},{6,7},{7,8},{8,9},{9,10},{10,1... | collective-permute-start | bytes 98312 | tf_op jit(solution)/shard_map/ppermute | solution.py:23
  17.7 14.0 %copy-start.82 = (s32[128]{0:T(128)}, s32[128]{0:T(128)S(1)}, u32[]{:S(2)}) copy-start(s32[128]{0:T(128)S(1)} %fusion.77) | copy-start | bytes 1540
  22.9 23.3 %all-to-all-start.1 = ((bf16[8,32,1024]{2,1,0:T(8,128)(2,1)}), bf16[8,32,1024]{2,1,0:T(8,128)(2,1)S(1)}, u32[]{:S(2)}, u32[]{:S(2)}) async-start(bf16[8,32,1024]{2,1,0:T(8,128)(2,1)} %bitcast.38), calls=%async_computation.1 | async-start | bytes 1048576 | tf_op jit(solution)/shard_map/all_to_all | solution.py:92
  46.2 19.8 %all-to-all-start = ((bf16[8,32,1024]{2,1,0:T(8,128)(2,1)}), bf16[8,32,1024]{2,1,0:T(8,128)(2,1)S(1)}, u32[]{:S(2)}, u32[]{:S(2)}) async-start(bf16[8,32,1024]{2,1,0:T(8,128)(2,1)} %bitcast.4), calls=%async_computation | async-start | bytes 1048576 | tf_op jit(solution)/shard_map/all_to_all | solution.py:93
  51.2 65.0 %reduce-scatter.5.cloned.1.call-start = ((), (), s32[]{:S(2)}) async-start(), calls=%async_computation.9 | async-start | bytes 5242880 | tf_op jit(solution)/shard_map/reduce_scatter | solution.py:132
  71.1 116.1 %all-gather.3.cloned.1.call-start = ((), (), s32[]{:S(2)}) async-start(), calls=%async_computation.5 | async-start | bytes 5242880 | tf_op jit(solution)/shard_map/all_gather | solution.py:99
  152.6 111.2 %reduce-scatter.3.cloned.1.call-start = ((), (), s32[]{:S(2)}) async-start(), calls=%async_computation.8 | async-start | bytes 5242880 | tf_op jit(solution)/shard_map/reduce_scatter | solution.py:129
  197.2 9.9 %copy-start.83 = (s32[128]{0:T(128)S(1)}, s32[128]{0:T(128)}, u32[]{:S(2)}) copy-start(s32[128]{0:T(128)} %copy-done.82) | copy-start | bytes 1540
  197.2 9.9 %copy-start.7 = (bf16[1,256,2048]{2,1,0:T(8,128)(2,1)S(1)}, bf16[1,256,2048]{2,1,0:T(8,128)(2,1)}, u32[]{:S(2)}) copy-start(bf16[1,256,2048]{2,1,0:T(8,128)(2,1)} %param.22) | copy-start | bytes 3145732
  201.5 20.4 %all-to-all-start.2 = ((bf16[8,32,1024]{2,1,0:T(8,128)(2,1)}), bf16[8,32,1024]{2,1,0:T(8,128)(2,1)S(1)}, u32[]{:S(2)}, u32[]{:S(2)}) async-start(bf16[8,32,1024]{2,1,0:T(8,128)(2,1)} %bitcast.194), calls=%async_computation.2 | async-start | bytes 1048576 | tf_op jit(solution)/shard_map/all_to_all | solution.py:112
  207.1 179.9 %all-reduce.2.cloned.1.call-start = ((), (), s32[]{:S(2)}) async-start(), calls=%async_computation.7 | async-start | bytes 262144 | tf_op jit(solution)/shard_map/psum | solution.py:127
  207.1 15.7 %copy-start.21 = (f32[1,1024]{1,0:T(1,128)S(1)}, f32[1,1024]{1,0:T(1,128)}, u32[]{:S(2)}) copy-start(f32[1,1024]{1,0:T(1,128)} %copy-done.20) | copy-start | bytes 12292
  207.1 15.7 %copy-start.23 = (f32[1,1024]{1,0:T(1,128)S(1)}, f32[1,1024]{1,0:T(1,128)}, u32[]{:S(2)}) copy-start(f32[1,1024]{1,0:T(1,128)} %copy-done.22) | copy-start | bytes 12292
  207.2 15.7 %copy-start.25 = (f32[1,1024]{1,0:T(1,128)S(1)}, f32[1,1024]{1,0:T(1,128)}, u32[]{:S(2)}) copy-start(f32[1,1024]{1,0:T(1,128)} %copy-done.24) | copy-start | bytes 12292
  207.2 15.7 %copy-start.27 = (f32[1,1024]{1,0:T(1,128)S(1)}, f32[1,1024]{1,0:T(1,128)}, u32[]{:S(2)}) copy-start(f32[1,1024]{1,0:T(1,128)} %copy-done.26) | copy-start | bytes 12292
  207.2 15.7 %copy-start.29 = (f32[1,1024]{1,0:T(1,128)S(1)}, f32[1,1024]{1,0:T(1,128)}, u32[]{:S(2)}) copy-start(f32[1,1024]{1,0:T(1,128)} %copy-done.28) | copy-start | bytes 12292
  207.2 15.7 %copy-start.31 = (f32[1,1024]{1,0:T(1,128)S(1)}, f32[1,1024]{1,0:T(1,128)}, u32[]{:S(2)}) copy-start(f32[1,1024]{1,0:T(1,128)} %copy-done.30) | copy-start | bytes 12292
  207.2 15.7 %copy-start.33 = (f32[1,1024]{1,0:T(1,128)S(1)}, f32[1,1024]{1,0:T(1,128)}, u32[]{:S(2)}) copy-start(f32[1,1024]{1,0:T(1,128)} %copy-done.32) | copy-start | bytes 12292
  207.2 15.7 %copy-start.35 = (f32[1,1024]{1,0:T(1,128)S(1)}, f32[1,1024]{1,0:T(1,128)}, u32[]{:S(2)}) copy-start(f32[1,1024]{1,0:T(1,128)} %copy-done.34) | copy-start | bytes 12292
  207.2 15.7 %copy-start.37 = (f32[1,1024]{1,0:T(1,128)S(1)}, f32[1,1024]{1,0:T(1,128)}, u32[]{:S(2)}) copy-start(f32[1,1024]{1,0:T(1,128)} %copy-done.36) | copy-start | bytes 12292
  207.2 15.7 %copy-start.39 = (f32[1,1024]{1,0:T(1,128)S(1)}, f32[1,1024]{1,0:T(1,128)}, u32[]{:S(2)}) copy-start(f32[1,1024]{1,0:T(1,128)} %copy-done.38) | copy-start | bytes 12292
  207.2 15.7 %copy-start.41 = (f32[1,1024]{1,0:T(1,128)S(1)}, f32[1,1024]{1,0:T(1,128)}, u32[]{:S(2)}) copy-start(f32[1,1024]{1,0:T(1,128)} %copy-done.40) | copy-start | bytes 12292
  207.2 15.7 %copy-start.43 = (f32[1,1024]{1,0:T(1,128)S(1)}, f32[1,1024]{1,0:T(1,128)}, u32[]{:S(2)}) copy-start(f32[1,1024]{1,0:T(1,128)} %copy-done.42) | copy-start | bytes 12292
  207.3 15.7 %copy-start.45 = (f32[1,1024]{1,0:T(1,128)S(1)}, f32[1,1024]{1,0:T(1,128)}, u32[]{:S(2)}) copy-start(f32[1,1024]{1,0:T(1,128)} %copy-done.44) | copy-start | bytes 12292
  207.3 15.7 %copy-start.47 = (f32[1,1024]{1,0:T(1,128)S(1)}, f32[1,1024]{1,0:T(1,128)}, u32[]{:S(2)}) copy-start(f32[1,1024]{1,0:T(1,128)} %copy-done.46) | copy-start | bytes 12292
  207.3 15.7 %copy-start.49 = (f32[1,1024]{1,0:T(1,128)S(1)}, f32[1,1024]{1,0:T(1,128)}, u32[]{:S(2)}) copy-start(f32[1,1024]{1,0:T(1,128)} %copy-done.48) | copy-start | bytes 12292
  207.3 15.7 %copy-start.51 = (f32[1,1024]{1,0:T(1,128)S(1)}, f32[1,1024]{1,0:T(1,128)}, u32[]{:S(2)}) copy-start(f32[1,1024]{1,0:T(1,128)} %copy-done.50) | copy-start | bytes 12292
  207.3 15.7 %copy-start.53 = (f32[1,1024]{1,0:T(1,128)S(1)}, f32[1,1024]{1,0:T(1,128)}, u32[]{:S(2)}) copy-start(f32[1,1024]{1,0:T(1,128)} %copy-done.52) | copy-start | bytes 12292
  207.3 15.7 %copy-start.55 = (f32[1,1024]{1,0:T(1,128)S(1)}, f32[1,1024]{1,0:T(1,128)}, u32[]{:S(2)}) copy-start(f32[1,1024]{1,0:T(1,128)} %copy-done.54) | copy-start | bytes 12292
  207.3 15.7 %copy-start.57 = (f32[1,1024]{1,0:T(1,128)S(1)}, f32[1,1024]{1,0:T(1,128)}, u32[]{:S(2)}) copy-start(f32[1,1024]{1,0:T(1,128)} %copy-done.56) | copy-start | bytes 12292
  207.3 15.7 %copy-start.59 = (f32[1,1024]{1,0:T(1,128)S(1)}, f32[1,1024]{1,0:T(1,128)}, u32[]{:S(2)}) copy-start(f32[1,1024]{1,0:T(1,128)} %copy-done.58) | copy-start | bytes 12292
  207.3 15.7 %copy-start.61 = (f32[1,1024]{1,0:T(1,128)S(1)}, f32[1,1024]{1,0:T(1,128)}, u32[]{:S(2)}) copy-start(f32[1,1024]{1,0:T(1,128)} %copy-done.60) | copy-start | bytes 12292
  207.3 15.7 %copy-start.63 = (f32[1,1024]{1,0:T(1,128)S(1)}, f32[1,1024]{1,0:T(1,128)}, u32[]{:S(2)}) copy-start(f32[1,1024]{1,0:T(1,128)} %copy-done.62) | copy-start | bytes 12292
  207.4 15.7 %copy-start.65 = (f32[1,1024]{1,0:T(1,128)S(1)}, f32[1,1024]{1,0:T(1,128)}, u32[]{:S(2)}) copy-start(f32[1,1024]{1,0:T(1,128)} %copy-done.64) | copy-start | bytes 12292
  207.4 15.7 %copy-start.67 = (f32[1,1024]{1,0:T(1,128)S(1)}, f32[1,1024]{1,0:T(1,128)}, u32[]{:S(2)}) copy-start(f32[1,1024]{1,0:T(1,128)} %copy-done.66) | copy-start | bytes 12292
  207.4 15.7 %copy-start.69 = (f32[1,1024]{1,0:T(1,128)S(1)}, f32[1,1024]{1,0:T(1,128)}, u32[]{:S(2)}) copy-start(f32[1,1024]{1,0:T(1,128)} %copy-done.68) | copy-start | bytes 12292
  207.4 15.7 %copy-start.71 = (f32[1,1024]{1,0:T(1,128)S(1)}, f32[1,1024]{1,0:T(1,128)}, u32[]{:S(2)}) copy-start(f32[1,1024]{1,0:T(1,128)} %copy-done.70) | copy-start | bytes 12292
  207.4 15.7 %copy-start.73 = (f32[1,1024]{1,0:T(1,128)S(1)}, f32[1,1024]{1,0:T(1,128)}, u32[]{:S(2)}) copy-start(f32[1,1024]{1,0:T(1,128)} %copy-done.72) | copy-start | bytes 12292
  207.4 15.7 %copy-start.75 = (f32[1,1024]{1,0:T(1,128)S(1)}, f32[1,1024]{1,0:T(1,128)}, u32[]{:S(2)}) copy-start(f32[1,1024]{1,0:T(1,128)} %copy-done.74) | copy-start | bytes 12292
  223.1 9.0 %copy-start.8 = (bf16[1,256,2048]{2,1,0:T(8,128)(2,1)S(1)}, bf16[1,256,2048]{2,1,0:T(8,128)(2,1)}, u32[]{:S(2)}) copy-start(bf16[1,256,2048]{2,1,0:T(8,128)(2,1)} %param.20) | copy-start | bytes 3145732
  225.5 8.3 %copy-start.80 = (f32[1,256,16]{1,2,0:T(8,128)S(1)}, f32[1,256,16]{1,2,0:T(8,128)}, u32[]{:S(2)}) copy-start(f32[1,256,16]{1,2,0:T(8,128)} %param.21) | copy-start | bytes 49156
  225.5 23.4 %collective-permute-start.3 = (bf16[16,1024]{1,0:T(8,128)(2,1)S(1)}, bf16[16,1024]{1,0:T(8,128)(2,1)S(1)}, u32[]{:S(2)}, u32[]{:S(2)}) collective-permute-start(bf16[16,1024]{1,0:T(8,128)(2,1)S(1)} %get-tuple-element.77), channel_id=1, source_target_pairs={{1,0},{2,1},{3,2},{4,3},{5,4},{6,5},{7,6},{8,7},{9,8},{10,9},{11,1... | collective-permute-start | bytes 98312 | tf_op jit(solution)/shard_map/ppermute | solution.py:25
  226.9 22.6 %collective-permute-start.2 = (bf16[16,1024]{1,0:T(8,128)(2,1)S(1)}, bf16[16,1024]{1,0:T(8,128)(2,1)}, u32[]{:S(2)}, u32[]{:S(2)}) collective-permute-start(bf16[16,1024]{1,0:T(8,128)(2,1)S(1)} %get-tuple-element.76), channel_id=1, source_target_pairs={{0,1},{1,2},{2,3},{3,4},{4,5},{5,6},{6,7},{7,8},{8,9},{9,10},{10,1... | collective-permute-start | bytes 98312 | tf_op jit(solution)/shard_map/ppermute | solution.py:23
  233.9 8.8 %copy-start.11 = (f32[256,16]{1,0:T(8,128)}, f32[256,16]{1,0:T(8,128)S(1)}, u32[]{:S(2)}) copy-start(f32[256,16]{1,0:T(8,128)S(1)} %copy.50) | copy-start | bytes 49156
  (48 other events, 198.3 us)
Sparse Core Ops, SparseCore 0:
  10.2 37.1 all-gather.4
  71.3 44.9 reduce-scatter.4
  152.7 34.4 all-gather.2
  196.1 44.5 reduce-scatter.2
  263.9 123.0 all-reduce.1
where the time goes:
time: 396 us; the launch traced here: 395 us
  waiting for transfers between devices  198 us (50%)
  local copies, waits for them, and re-layouts  64.8 us (16%)
  other arithmetic  62 us (16%)
  starting transfers between devices  33.4 us (8%)
  matrix products  22 us (6%)
  between operations  15.1 us (4%)
    psum x1, waiting for transfers between devices, body(): conv_total = lax.psum(conv_terms, ('dp', 'expert'))  98.2 us
    all_gather x1, waiting for transfers between devices, body(): lax.all_gather(down_master.astype(jnp.bfloat16), 'dp', axis=1, tiled=True)  34.4 us
    reduce_scatter x1, waiting for transfers between devices, body(): lax.psum_scatter(down_part[None].astype(jnp.bfloat16), 'dp', scatter_dime...  29.6 us
    reduce_max x2, other arithmetic, adam_block(): square_top = jnp.max(square_new, axis=-1) + scale_eps  21.1 us
    unnamed x179, local copies, waits for them, and re-layouts  19.3 us
    convert_element_type x2, other arithmetic, adam_block(): (square_new / square_top[..., None]).reshape(full_shape)  14.9 us
    all_to_all x1, waiting for transfers between devices, body(): lax.all_to_all(grad_rows, 'expert', split_axis=0, concat_axis=0, tiled=True)  13 us
    all_to_all x1, waiting for transfers between devices, body(): lax.all_to_all(send_rows, 'expert', split_axis=0, concat_axis=0, tiled=True)  12 us
  transfers between devices with their start and end apart: 12, of which 7 were waited for; matrix products, arithmetic and copies ran while one was open for 23% of the time, Pallas kernels for 0%

commit v1 on v0

v1 whole, which is shorter than its diff:
```python
import functools

import jax
import jax.numpy as jnp
from jax import lax
from jax.experimental import pallas as pl
from jax.experimental.pallas import tpu as pltpu
from jax.sharding import PartitionSpec as P

beta_one = 0.9
beta_two = 0.95
bias_one = 1.0 - beta_one**10
bias_two = 1.0 - beta_two**10
learn_rate = 0.001
adam_eps = 1e-08
scale_eps = 1e-06

f32 = jnp.float32
bf16 = jnp.bfloat16
MIB = 1 << 20


def swish_parts(values):
    gate_value = 1.0 / (1.0 + jnp.exp(-values))
    return (values * gate_value, gate_value * (1.0 + values * (1.0 - gate_value)))


def across(lhs, rhs):
    return lax.dot_general(lhs, rhs, (((0,), (0,)), ((), ())), preferred_element_type=f32)


def along(lhs, rhs):
    return lax.dot_general(lhs, rhs, (((1,), (1,)), ((), ())), preferred_element_type=f32)


def staged(kernel, counts, spans, *refs):
    groups = []
    for count in counts:
        groups.append(refs[:count])
        refs = refs[count:]
    scalars, sources, targets, held, made, scratch = groups
    in_sems, out_sems = refs
    arriving = []
    for index, source in enumerate(sources):
        if spans[index] is not None:
            source = source.at[pl.ds(*spans[index]), :]
        copy = pltpu.make_async_copy(source, held[index], in_sems.at[index])
        copy.start()
        arriving.append(copy)
    leaving = {}

    def take(index):
        if arriving[index] is not None:
            arriving[index].wait()
            arriving[index] = None
        return held[index]

    def give(index):
        leaving[index] = pltpu.make_async_copy(made[index], targets[index], out_sems.at[index])
        leaving[index].start()

    kernel(scalars, take, made, give, scratch)
    for index in range(len(targets)):
        if index not in leaving:
            give(index)
    for index in range(len(sources)):
        take(index)
    for copy in leaving.values():
        copy.wait()


def call(kernel, name, scalars, inputs, outs, scratch=(), flops=0, moved=0, limit=40):
    hbm = pl.BlockSpec(memory_space=pltpu.HBM)
    smem = pl.BlockSpec(memory_space=pltpu.SMEM)
    pairs = [item if isinstance(item, tuple) else (item, None) for item in inputs]
    arrays = [array for array, _ in pairs]
    spans = [span for _, span in pairs]
    held = [
        pltpu.VMEM(array.shape if span is None else (span[1],) + array.shape[1:], array.dtype)
        for array, span in pairs
    ]
    made = [pltpu.VMEM(shape, kind) for shape, kind in outs]
    counts = (len(scalars), len(arrays), len(outs), len(held), len(made), len(scratch))
    return pl.pallas_call(
        functools.partial(staged, kernel, counts, spans),
        out_shape=[jax.ShapeDtypeStruct(shape, kind) for shape, kind in outs],
        in_specs=[smem] * len(scalars) + [hbm] * len(arrays),
        out_specs=[hbm] * len(outs),
        scratch_shapes=held
        + made
        + list(scratch)
        + [pltpu.SemaphoreType.DMA((len(arrays),)), pltpu.SemaphoreType.DMA((len(outs),))],
        compiler_params=pltpu.CompilerParams(vmem_limit_bytes=limit * MIB),
        cost_estimate=pl.CostEstimate(flops=flops, bytes_accessed=moved, transcendentals=0),
        name=name,
    )(*scalars, *arrays)


def dispatch_kernel(experts, capacity, scalars, take, made, give, scratch):
    place_ref, out_ref = made
    ids = take(0)[...]
    length = ids.shape[1]
    rows = lax.broadcasted_iota(jnp.int32, (experts, length), 0)
    one_hot = (rows == ids).astype(f32)
    earlier = lax.broadcasted_iota(jnp.int32, (length, length), 0)
    later = lax.broadcasted_iota(jnp.int32, (length, length), 1)
    ranks = jnp.dot(one_hot, (earlier < later).astype(f32), preferred_element_type=f32)
    slot = jnp.sum(ranks * one_hot, axis=0, keepdims=True).astype(jnp.int32)
    position = ids * capacity + slot
    slots = lax.broadcasted_iota(jnp.int32, (experts * capacity, length), 0)
    place = (slots == position).astype(f32).astype(bf16)
    place_ref[...] = place
    out_ref[...] = jnp.dot(place, take(1)[...], preferred_element_type=f32).astype(bf16)


def fill_padded(pad_ref, left_ref, middle_ref, right_ref):
    side, length = left_ref.shape[0], middle_ref.shape[0]
    pad_ref[0:side, :] = left_ref[...].astype(f32)
    pad_ref[side : side + length, :] = middle_ref[...].astype(f32)
    pad_ref[side + length : side + length + side, :] = right_ref[...].astype(f32)


def conv_kernel(scalars, take, made, give, scratch):
    slope_ref, out_ref = made
    pad_ref, feat_ref = scratch
    fill_padded(pad_ref, take(0), take(1), take(2))
    taps_ref = take(3)
    length, width = feat_ref.shape

    def lanes(step, carry):
        cols = pl.ds(pl.multiple_of(step * 128, 128), 128)
        total = jnp.zeros((length, 128), f32)
        for tap in range(taps_ref.shape[0]):
            total = total + taps_ref[tap : tap + 1, cols] * pad_ref[tap : tap + length, cols]
        active, slope = swish_parts(total)
        slope_ref[:, cols] = slope
        feat_ref[:, cols] = active.astype(bf16)
        return carry

    lax.fori_loop(0, width // 128, lanes, 0)
    out_ref[...] = jnp.dot(take(4)[...], feat_ref[...], preferred_element_type=f32).astype(bf16)


def forward_kernel(shards, scalars, take, made, give, scratch):
    (order_ref,) = scalars
    slope_ref, keep_ref, send_ref = made
    (hidden_ref,) = scratch
    rows_ref = take(0)
    up_refs = [take(2 + shard) for shard in range(shards)]
    slots, width = rows_ref.shape
    depth = width // shards
    chunk = 512

    for half in range(hidden_ref.shape[1] // width):

        def step(index, carry):
            start = pl.multiple_of(index * chunk, chunk)
            cols = pl.ds(start, chunk)
            pre = 0.0
            for shard, up_ref in enumerate(up_refs):
                at = pl.ds(pl.multiple_of(order_ref[shard] * depth, depth), depth)
                weight = up_ref[half * depth : (half + 1) * depth, cols]
                pre = pre + jnp.dot(rows_ref[:, at], weight, preferred_element_type=f32)
            active, slope = swish_parts(pre)
            spot = pl.ds(pl.multiple_of(half * width + start, chunk), chunk)
            hidden_ref[:, spot] = active.astype(bf16)
            slope_ref[:, spot] = slope
            return carry

        lax.fori_loop(0, width // chunk, step, 0)
    give(0)
    grads = take(1)[...]
    share = hidden_ref.shape[1] // shards
    for out_ref, side in ((send_ref, 1), (keep_ref, 0)):
        for index in range(shards // 2):
            place = order_ref[shards + 2 * index + side]
            at = pl.ds(pl.multiple_of(place * share, share), share)
            out_ref[index * share : (index + 1) * share, :] = across(
                hidden_ref[:, at], grads
            ).astype(bf16)
        give(1 if out_ref is keep_ref else 2)


def backward_kernel(shards, scalars, take, made, give, scratch):
    (order_ref,) = scalars
    pre_ref, out_ref = made
    grads_ref = take(0)
    slope_ref = take(1)
    slots, width = grads_ref.shape
    hidden = pre_ref.shape[1]
    share, depth = hidden // shards, width // shards
    for shard in range(shards):
        at = pl.ds(pl.multiple_of(order_ref[shard] * share, share), share)
        back = along(grads_ref[...], take(2 + shard)[...])
        pre_ref[:, at] = (back * slope_ref[:, at]).astype(bf16)
    give(0)
    for shard in range(shards):
        at = pl.ds(pl.multiple_of(order_ref[shard] * depth, depth), depth)
        up_ref = take(2 + shards + shard)
        back = 0.0
        for half in range(hidden // width):
            back = back + along(
                pre_ref[:, half * width : (half + 1) * width],
                up_ref[half * depth : (half + 1) * depth, :],
            )
        out_ref[:, at] = back.astype(bf16)


def up_grad_kernel(shards, scalars, take, made, give, scratch):
    (order_ref,) = scalars
    keep_ref, send_ref = made
    rows_ref, pre = take(0), take(1)[...]
    depth = rows_ref.shape[1] // shards
    for out_ref, side in ((send_ref, 1), (keep_ref, 0)):
        for index in range(shards // 2):
            place = order_ref[shards + 2 * index + side]
            at = pl.ds(pl.multiple_of(place * depth, depth), depth)
            out_ref[index * depth : (index + 1) * depth, :] = across(
                rows_ref[:, at], pre
            ).astype(bf16)
        give(0 if out_ref is keep_ref else 1)


def cast_kernel(scalars, take, made, give, scratch):
    up_ref, down_ref, both_ref = made
    up, down = take(0), take(1)
    depth, hidden = up.shape
    share, width = down.shape
    for half in range(hidden // width):
        values = up[:, half * width : (half + 1) * width].astype(bf16)
        up_ref[half * depth : (half + 1) * depth, :] = values
        both_ref[half * depth : (half + 1) * depth, :] = values
    give(0)
    values = down[...].astype(bf16)
    down_ref[...] = values
    both_ref[share : 2 * share, :] = values


def taps_kernel(scalars, take, made, give, scratch):
    grad_ref, head_ref, tail_ref, terms_ref = made
    (pad_ref,) = scratch
    fill_padded(pad_ref, take(2), take(3), take(4))
    length, width = grad_ref.shape
    side = head_ref.shape[0]
    features = across(take(0)[...], take(5)[...]).astype(bf16).astype(f32)
    grad = (features * take(1)[...]).astype(bf16)
    grad_ref[...] = grad
    head_ref[...] = grad[:side]
    tail_ref[...] = grad[length - side :]
    give(1)
    give(2)
    give(0)

    def lanes(step, carry):
        cols = pl.ds(pl.multiple_of(step * 128, 128), 128)
        local = grad_ref[:, cols].astype(f32)
        for tap in range(terms_ref.shape[0]):
            product = local * pad_ref[tap : tap + length, cols]
            terms_ref[tap : tap + 1, cols] = jnp.sum(product, axis=0, keepdims=True)
        return carry

    lax.fori_loop(0, width // 128, lanes, 0)


def frames_kernel(scalars, take, made, give, scratch):
    (out_ref,) = made
    (pad_ref,) = scratch
    length, width = out_ref.shape
    fill_padded(pad_ref, take(0), take(1), take(2))
    taps_ref, cot_ref = take(3), take(4)
    count = taps_ref.shape[0]

    def lanes(step, carry):
        cols = pl.ds(pl.multiple_of(step * 128, 128), 128)
        total = cot_ref[:, cols].astype(f32)
        for tap in range(count):
            start = count - tap
            total = total + taps_ref[tap : tap + 1, cols] * pad_ref[start : start + length, cols]
        out_ref[:, cols] = total.astype(bf16)
        return carry

    lax.fori_loop(0, width // 128, lanes, 0)


def adam_kernel(terms, master_ref, mean_ref, mean_scale_ref, square_ref, square_scale_ref, *refs):
    grad_refs, refs = refs[:terms], refs[terms:]
    next_ref, mean_next_ref, mean_top_ref, square_next_ref, square_top_ref = refs[:5]
    scales_ref, tops_ref = refs[5:]
    rows, width = master_ref.shape
    blocks = mean_scale_ref.shape[0]
    size = width // blocks
    step = pl.program_id(0)
    steps = pl.num_programs(0)

    @pl.when(step == 0)
    def _():
        scales_ref[0, :, :blocks] = mean_scale_ref[...].T
        scales_ref[1, :, :blocks] = square_scale_ref[...].T

    here = pl.ds(pl.multiple_of(step * rows, rows), rows)
    mean_scales = scales_ref[0, here, :]
    square_scales = scales_ref[1, here, :]
    for block in range(blocks):
        cols = slice(block * size, (block + 1) * size)
        grad = grad_refs[0][:, cols].astype(f32)
        for grad_ref in grad_refs[1:]:
            grad = grad + grad_ref[:, cols].astype(f32)
        mean = beta_one * (
            mean_ref[:, cols].astype(f32) * mean_scales[:, block : block + 1]
        ) + (1.0 - beta_one) * grad
        square = beta_two * (
            square_ref[:, cols].astype(f32) * square_scales[:, block : block + 1]
        ) + (1.0 - beta_two) * (grad * grad)
        root = jnp.sqrt(square * (1.0 / bias_two)) + adam_eps
        next_ref[:, cols] = master_ref[:, cols] - (learn_rate / bias_one) * (mean / root)
        mean_top = jnp.max(jnp.abs(mean), axis=1, keepdims=True) + scale_eps
        square_top = jnp.max(square, axis=1, keepdims=True) + scale_eps
        mean_next_ref[:, cols] = (mean * (1.0 / mean_top)).astype(bf16)
        square_next_ref[:, cols] = (square * (1.0 / square_top)).astype(bf16)
        tops_ref[0, here, block : block + 1] = mean_top
        tops_ref[1, here, block : block + 1] = square_top

    @pl.when(step == steps - 1)
    def _():
        mean_top_ref[...] = tops_ref[0, :, :blocks].T
        square_top_ref[...] = tops_ref[1, :, :blocks].T


def adam(name, master, grads, mean_code, mean_scale, square_code, square_scale):
    _, rows, width = master.shape
    blocks = mean_scale.shape[-1]
    part = 32
    tile = pl.BlockSpec((part, width), lambda i: (i, 0))
    whole = pl.BlockSpec((blocks, rows), lambda i: (0, 0))
    wide = jax.ShapeDtypeStruct((rows, width), f32)
    code = jax.ShapeDtypeStruct((rows, width), bf16)
    scale = jax.ShapeDtypeStruct((blocks, rows), f32)
    results = pl.pallas_call(
        functools.partial(adam_kernel, len(grads)),
        grid=(rows // part,),
        out_shape=[wide, code, scale, code, scale],
        in_specs=[tile, tile, whole, tile, whole] + [tile] * len(grads),
        out_specs=[tile, tile, whole, tile, whole],
        scratch_shapes=[pltpu.VMEM((2, rows, 128), f32), pltpu.VMEM((2, rows, 128), f32)],
        compiler_params=pltpu.CompilerParams(vmem_limit_bytes=32 * MIB),
        cost_estimate=pl.CostEstimate(
            flops=20 * rows * width,
            bytes_accessed=(16 + 2 * len(grads)) * rows * width,
            transcendentals=0,
        ),
        name=name,
    )(master[0], mean_code[0], mean_scale[0].T, square_code[0], square_scale[0].T, *grads)
    new_master, mean_next, mean_top, square_next, square_top = results
    return (new_master[None], mean_next[None], mean_top.T[None], square_next[None], square_top.T[None])


def by_expert(rows):
    experts = lax.axis_size("expert")
    slots, width = rows.shape
    cells = rows.reshape(experts, slots // experts, width)
    return lax.all_to_all(cells, "expert", 0, 0, tiled=True).reshape(slots, width)


def to_chip(values, shift):
    count = lax.axis_size("dp")
    chips = count // 2
    return lax.ppermute(
        values, "dp", [(i, (i // 2 + shift) % chips * 2 + i % 2) for i in range(count)]
    )


def to_core(values):
    count = lax.axis_size("dp")
    return lax.ppermute(values, "dp", [(i, i ^ 1) for i in range(count)])


def gather_shards(up_shard, down_shard, both):
    chips = lax.axis_size("dp") // 2
    share = up_shard.shape[0]
    upper, lower = (0, share), (share, share)
    near = to_core(both)
    ups, downs = [(both, upper), (near, upper)], [(both, lower), (near, lower)]
    far_ups = [to_chip(up_shard, shift) for shift in range(1, chips)]
    far_downs = [to_chip(down_shard, shift) for shift in range(1, chips)]
    for arrived in far_ups:
        ups = ups + [arrived, to_core(arrived)]
    for arrived in far_downs:
        downs = downs + [arrived, to_core(arrived)]
    return ups, downs


def sum_shares(keep, send):
    chips = lax.axis_size("dp") // 2
    theirs = to_core(send)
    share = keep.shape[0] // chips
    grads = [keep, theirs]
    for shift in range(1, chips):
        part = slice(shift * share, (shift + 1) * share)
        chip_sum = (keep[part].astype(f32) + theirs[part].astype(f32)).astype(bf16)
        grads.append(to_chip(chip_sum, shift))
    return grads


def halo(head, tail):
    axes = ("dp", "expert")
    count = lax.axis_size("dp") * lax.axis_size("expert")
    right = [(i, i + 1) for i in range(count - 1)]
    left = [(i + 1, i) for i in range(count - 1)]
    return lax.ppermute(tail, axes, right), lax.ppermute(head, axes, left)


def sum_everywhere(terms):
    axes = ("dp", "expert")
    count = lax.axis_size("dp") * lax.axis_size("expert")
    taps, width = terms.shape
    cells = terms.reshape(count, taps * width // count)
    parts = lax.all_to_all(cells[:, None], axes, 0, 0, tiled=True)
    mine = jnp.sum(parts, axis=0)
    spread = jnp.broadcast_to(mine[None], (count,) + mine.shape)
    return lax.all_to_all(spread, axes, 0, 0, tiled=True).reshape(taps, width)


def body(
    frames,
    cotangent,
    expert_ids,
    conv_weight,
    up_master,
    down_master,
    up_mean_code,
    up_mean_scale,
    up_square_code,
    up_square_scale,
    down_mean_code,
    down_mean_scale,
    down_square_code,
    down_square_scale,
):
    length, width = frames.shape
    taps = conv_weight.shape[0]
    side = taps // 2
    experts = lax.axis_size("expert")
    dp_size = lax.axis_size("dp")
    capacity = 2 * length // experts
    slots = experts * capacity
    hidden = up_master.shape[2]
    rank = lax.axis_index("dp").astype(jnp.int32)
    chip, core, chips = rank // 2, rank % 2, dp_size // 2
    came = [(chip + chips - shift) % chips * 2 for shift in range(chips)]
    goes = [(chip + shift) % chips * 2 for shift in range(chips)]
    order = [base + side_core for base in came for side_core in (core, 1 - core)]
    order = order + [base + side_core for base in goes for side_core in (core, 1 - core)]
    order = jnp.stack(order).astype(jnp.int32)
    product = 2 * slots * width * hidden
    row_shape = ((slots, width), bf16)
    share, depth = hidden // dp_size, width // dp_size

    left, right = halo(frames[:side], frames[length - side :])
    ups, downs = gather_shards(
        *call(
            cast_kernel,
            "cast",
            [],
            [up_master[0], down_master[0]],
            [((share, width), bf16), ((share, width), bf16), ((2 * share, width), bf16)],
            moved=16 * share * width,
        )
    )
    place, send_grads = call(
        functools.partial(dispatch_kernel, experts, capacity),
        "dispatch",
        [],
        [expert_ids.reshape(1, length), cotangent],
        [((slots, length), bf16), row_shape],
        flops=2 * slots * length * width,
        moved=4 * slots * width,
    )
    recv_grads = by_expert(send_grads)
    slope, send_rows = call(
        conv_kernel,
        "convolve",
        [],
        [left, frames, right, conv_weight, place],
        [((length, width), f32), row_shape],
        scratch=[pltpu.VMEM((length + 2 * side, width), f32), pltpu.VMEM((length, width), bf16)],
        flops=2 * slots * length * width,
        moved=8 * slots * width,
    )
    recv_rows = by_expert(send_rows)

    hidden_slope, *down_shares = call(
        functools.partial(forward_kernel, dp_size),
        "forward",
        [order],
        [recv_rows, recv_grads] + ups,
        [((slots, hidden), f32)] + [((chips * share, width), bf16)] * 2,
        scratch=[pltpu.VMEM((slots, hidden), bf16)],
        flops=2 * product,
        moved=4 * width * hidden,
    )
    down_grads = sum_shares(*down_shares)
    grad_pre, back_rows = call(
        functools.partial(backward_kernel, dp_size),
        "backward",
        [order],
        [recv_grads, hidden_slope] + downs + ups,
        [((slots, hidden), bf16), row_shape],
        flops=2 * product,
        moved=4 * width * hidden,
    )
    returned = by_expert(back_rows)
    up_shares = call(
        functools.partial(up_grad_kernel, dp_size),
        "up_grad",
        [order],
        [recv_rows, grad_pre],
        [((chips * depth, hidden), bf16)] * 2,
        flops=product,
        moved=2 * width * hidden,
    )
    up_grads = sum_shares(*up_shares)

    grad_conv, head, tail, conv_terms = call(
        taps_kernel,
        "taps",
        [],
        [place, slope, left, frames, right, returned],
        [((length, width), bf16), ((side, width), bf16), ((side, width), bf16), ((taps, width), f32)],
        scratch=[pltpu.VMEM((length + 2 * side, width), f32)],
        flops=2 * slots * length * width,
        moved=8 * slots * width,
    )
    grad_left, grad_right = halo(head, tail)
    conv_total = sum_everywhere(conv_terms)
    (grad_frames,) = call(
        frames_kernel,
        "frames",
        [],
        [grad_left, grad_conv, grad_right, conv_weight, cotangent],
        [((length, width), bf16)],
        scratch=[pltpu.VMEM((length + 2 * side, width), f32)],
        flops=2 * slots * length * width,
        moved=4 * slots * width,
    )
    down_next = adam(
        "adam_down", down_master, down_grads,
        down_mean_code, down_mean_scale, down_square_code, down_square_scale,
    )
    up_next = adam(
        "adam_up", up_master, up_grads,
        up_mean_code, up_mean_scale, up_square_code, up_square_scale,
    )
    return (grad_frames, conv_total) + up_next + down_next


def solution(mesh):
    frames = P(("dp", "expert"), None)
    shared = P()
    state = P("expert", "dp", None)
    return jax.shard_map(
        body,
        mesh=mesh,
        in_specs=(frames,) * 3 + (shared,) + (state,) * 10,
        out_specs=(frames, shared) + (state,) * 10,
        check_vma=False,
    )
```

time: 396 us -> 209 us (0.53)
  waiting for transfers between devices: 198 us -> 39.8 us
  Pallas kernels: 0 us -> 59.5 us
  other arithmetic: 62 us -> 6.93 us
  local copies, waits for them, and re-layouts: 64.8 us -> 17.7 us
  blocking collectives: 0 us -> 33.3 us
  matrix products: 22 us -> 0 us
  between operations: 15.1 us -> 0.98 us
  starting transfers between devices: 33.4 us -> 47.3 us
    psum x1 -> x0, waiting for transfers between devices: 98.2 us -> none  [body(): conv_total = lax.psum(conv_terms, ('dp', 'expert'))]
    pallas_call x0 -> x10, Pallas kernels: none -> 59.5 us  [the longest x8 31 us: call(): pl.pallas_call(functools.partial(staged, kernel, counts, spans), out_shap...]
    all_gather x2 -> x0, waiting for transfers between devices: 34.4 us -> none  [the longest x1 34.4 us: body(): lax.all_gather(down_master.astype(jnp.bfloat16), 'dp', axis=1, tiled=True)]
    all_to_all x0 -> x1, blocking collectives: none -> 33.3 us  [sum_everywhere(): parts = lax.all_to_all(cells[:, None], axes, 0, 0, tiled=True)]
    reduce_scatter x2 -> x0, waiting for transfers between devices: 29.6 us -> none  [the longest x1 29.6 us: body(): lax.psum_scatter(down_part[None].astype(jnp.bfloat16), 'dp', scatter_dime...]
    ppermute x4 -> x13, waiting for transfers between devices: 0.69 us -> 22.9 us  [the longest x4 16.6 us: to_chip(): lax.ppermute(values, 'dp', [(i, (i // 2 + shift) % chips * 2 + i % 2) for...]
    dot_general x5 -> x0, matrix products: 22 us -> none  [the longest x1 5.09 us: body(): jnp.einsum('rh,rd->hd', hidden, grads_in, preferred_element_type=jnp.floa...]
    reduce_max x2 -> x0, other arithmetic: 21.1 us -> none  [adam_block(): square_top = jnp.max(square_new, axis=-1) + scale_eps]
  transfers between devices with their start and end apart: 12 -> 17, of which waited for: 7 -> 7; matrix products, arithmetic and copies ran while one was open for 23% -> 5% of each run, Pallas kernels for 0% -> 22%
where the time goes in v1:
time: 209 us; the launch traced here: 205 us
  Pallas kernels  59.5 us (28%)
  starting transfers between devices  47.3 us (23%)
  waiting for transfers between devices  39.8 us (19%)
  blocking collectives  33.3 us (16%)
  local copies, waits for them, and re-layouts  17.7 us (8%)
  other arithmetic  6.93 us (3%)
    all_to_all x1, blocking collectives, sum_everywhere(): parts = lax.all_to_all(cells[:, None], axes, 0, 0, tiled=True)  33.3 us
    pallas_call x8, Pallas kernels, call(): pl.pallas_call(functools.partial(staged, kernel, counts, spans), out_shap...  31 us
    pallas_call x2, Pallas kernels, adam(): pl.pallas_call(functools.partial(adam_kernel, len(grads)), grid=(rows //...  28.5 us
    all_to_all x3, starting transfers between devices, by_expert(): lax.all_to_all(cells, 'expert', 0, 0, tiled=True).reshape(slots, width)  18.7 us
    all_to_all x3, waiting for transfers between devices, by_expert(): lax.all_to_all(cells, 'expert', 0, 0, tiled=True).reshape(slots, width)  16.9 us
    ppermute x4, waiting for transfers between devices, to_chip(): lax.ppermute(values, 'dp', [(i, (i // 2 + shift) % chips * 2 + i % 2) for...  16.6 us
    unnamed x63, local copies, waits for them, and re-layouts  16 us
    ppermute x4, starting transfers between devices, halo(): return (lax.ppermute(tail, axes, right), lax.ppermute(head, axes, left))  10.7 us
  transfers between devices with their start and end apart: 17, of which 7 were waited for; matrix products, arithmetic and copies ran while one was open for 5% of the time, Pallas kernels for 22%

profile of v1, /device:TPU:0, one launch (start us, length us, event | category | flops | bytes accessed | tf_op | source)
XLA Modules:
  0.0 205.5 jit_solution(14938167343625667828)
XLA Ops:
  0.7 1.6 copy-done
  2.2 1.6 copy-done.2
  3.8 1.8 cast.1
  5.6 3.0 %collective-permute-start.3 = (bf16[512,1024]{1,0:T(8,128)(2,1)}, bf16[512,1024]{1,0:T(8,128)(2,1)}, u32[]{:S(2)}, u32[]{:S(2)}) collective-permute-start(bf16[512,1024]{1,0:T(8,128)(2,1)} %get-tuple-element.45), channel_id=1, source_target_pairs={{0,16},{8,24},{16,0},{24,8},{1,17},{9,25},{17,1},{25,9},{2,18},{10... | collective-permute-start | bytes 3145736 | tf_op jit(solution)/shard_map/ppermute | solution.py:367
  8.8 0.6 dispatch.1
  9.5 0.8 copy-done.18
  10.3 6.2 %all-to-all-start = ((bf16[8,32,1024]{2,1,0:T(8,128)(2,1)}), bf16[8,32,1024]{2,1,0:T(8,128)(2,1)S(1)}, u32[]{:S(2)}, u32[]{:S(2)}) async-start(bf16[8,32,1024]{2,1,0:T(8,128)(2,1)} %bitcast.66), calls=%async_computation | async-start | bytes 1048576 | tf_op jit(solution)/shard_map/all_to_all | solution.py:361
  16.4 16.5 %collective-permute-done.3.refs_5_.refs_9_ = bf16[512,1024]{1,0:T(8,128)(2,1)} collective-permute-done((bf16[512,1024]{1,0:T(8,128)(2,1)}, bf16[512,1024]{1,0:T(8,128)(2,1)}, u32[]{:S(2)}, u32[]{:S(2)}) %collective-permute-start.3) | collective-permute-done | bytes 1048608 | tf_op jit(solution)/shard_map/ppermute | solution.py:367
  33.0 1.3 collective-permute-start.1
  34.3 4.6 %collective-permute-start = (bf16[16,1024]{1,0:T(8,128)(2,1)S(1)}, bf16[16,1024]{1,0:T(8,128)(2,1)S(1)}, u32[]{:S(2)}, u32[]{:S(2)}) collective-permute-start(bf16[16,1024]{1,0:T(8,128)(2,1)S(1)} %get-tuple-element.69), channel_id=1, source_target_pairs={{0,1},{1,2},{2,3},{3,4},{4,5},{5,6},{6,7},{7,8},{8,9},{9,10},{10,1... | collective-permute-start | bytes 98312 | tf_op jit(solution)/shard_map/ppermute | solution.py:409
  39.0 1.5 collective-permute-done.refs_0_.refs_2_
  40.4 3.8 %convolve.1 = (f32[128,1024]{1,0:T(8,128)S(1)}, bf16[256,1024]{1,0:T(8,128)(2,1)S(1)}) custom-call(bf16[16,1024]{1,0:T(8,128)(2,1)S(1)} %collective-permute-done.refs_0_.refs_2_, bf16[128,1024]{1,0:T(8,128)(2,1)S(1)} %copy-done.10, bf16[16,1024]{1,0:T(8,128)(2,1)S(1)} %collective-permute-done.1.refs_2_.refs_4_, f32[32,1024]{1,0:T(8,128)S(1)} %copy-done.19, ...), custom_call_target="tpu_custom_call" | custom-call | flops 67108864 | bytes 2097152 | tf_op jit(solution)/shard_map/convolve/pallas_call | solution.py:84
  44.2 0.8 copy-done.16
  45.0 0.8 copy-done.20
  45.8 8.7 %all-to-all-start.1 = ((bf16[8,32,1024]{2,1,0:T(8,128)(2,1)}), bf16[8,32,1024]{2,1,0:T(8,128)(2,1)}, u32[]{:S(2)}, u32[]{:S(2)}) async-start(bf16[8,32,1024]{2,1,0:T(8,128)(2,1)} %bitcast.64), calls=%async_computation.1 | async-start | bytes 1048576 | tf_op jit(solution)/shard_map/all_to_all | solution.py:361
  54.6 3.0 %collective-permute-start.6 = (bf16[512,1024]{1,0:T(8,128)(2,1)}, bf16[512,1024]{1,0:T(8,128)(2,1)}, u32[]{:S(2)}, u32[]{:S(2)}) collective-permute-start(bf16[512,1024]{1,0:T(8,128)(2,1)} %collective-permute-done.5.refs_5_), channel_id=1, source_target_pairs={{0,8},{8,0},{16,24},{24,16},{1,9},{9,1},{17,25},{25,17},{2,10},{10... | collective-permute-start | bytes 3145736 | tf_op jit(solution)/shard_map/ppermute | solution.py:374
  57.7 11.1 %all-to-all-done.1 = bf16[8,32,1024]{2,1,0:T(8,128)(2,1)} async-done(((bf16[8,32,1024]{2,1,0:T(8,128)(2,1)}), bf16[8,32,1024]{2,1,0:T(8,128)(2,1)}, u32[]{:S(2)}, u32[]{:S(2)}) %all-to-all-start.1) | async-done | bytes 524320 | tf_op jit(solution)/shard_map/all_to_all | solution.py:361
  68.8 7.3 %forward.1 = (f32[256,2048]{1,0:T(8,128)S(1)}, bf16[1024,1024]{1,0:T(8,128)(2,1)S(1)}, bf16[1024,1024]{1,0:T(8,128)(2,1)}) custom-call(s32[8]{0:T(128)S(1)} %stack.29.refs_0_, bf16[256,1024]{1,0:T(8,128)(2,1)} %bitcast.10.refs_1_, bf16[256,1024]{1,0:T(8,128)(2,1)S(1)} %bitcast.57, bf16[1024,1024]{1,0:T(8,128)(2,1)S(1)} %get-tuple-element.44.refs_3_.refs_7_, ...), custom_call_target="tpu_custom_call" | custom-call | flops 2147483648 | bytes 8388608 | tf_op jit(solution)/shard_map/forward/pallas_call | solution.py:84
  76.1 1.7 collective-permute-start.11
  77.8 6.6 %backward.1 = (bf16[256,2048]{1,0:T(8,128)(2,1)S(1)}, bf16[256,1024]{1,0:T(8,128)(2,1)S(1)}) custom-call(s32[8]{0:T(128)S(1)} %stack.29.refs_0_, bf16[256,1024]{1,0:T(8,128)(2,1)S(1)} %bitcast.58, f32[256,2048]{1,0:T(8,128)S(1)} %get-tuple-element.46.refs_2_, bf16[1024,1024]{1,0:T(8,128)(2,1)S(1)} %get-tuple-element.44.refs_3_.refs_7_, ...), custom_call_target="tpu_custom_call" | custom-call | flops 2147483648 | bytes 8388608 | tf_op jit(solution)/shard_map/backward/pallas_call | solution.py:84
  84.5 0.8 copy-done.17
  85.3 3.8 %up_grad.1 = (bf16[512,2048]{1,0:T(8,128)(2,1)S(1)}, bf16[512,2048]{1,0:T(8,128)(2,1)}) custom-call(s32[8]{0:T(128)S(1)} %stack.29.refs_0_, bf16[256,1024]{1,0:T(8,128)(2,1)} %bitcast.10.refs_1_, bf16[256,2048]{1,0:T(8,128)(2,1)S(1)} %get-tuple-element.53.refs_2_), custom_call_target="tpu_custom_call" | custom-call | flops 1073741824 | bytes 4194304 | tf_op jit(solution)/shard_map/up_grad/pallas_call | solution.py:84
  89.1 1.3 copy-done.7
  90.4 3.8 %all-to-all-start.2 = ((bf16[8,32,1024]{2,1,0:T(8,128)(2,1)}), bf16[8,32,1024]{2,1,0:T(8,128)(2,1)S(1)}, u32[]{:S(2)}, u32[]{:S(2)}) async-start(bf16[8,32,1024]{2,1,0:T(8,128)(2,1)} %bitcast.65), calls=%async_computation.2 | async-start | bytes 1048576 | tf_op jit(solution)/shard_map/all_to_all | solution.py:361
  94.2 2.7 %add_convert_fusion = bf16[512,1024]{1,0:T(8,128)(2,1)} fusion(bf16[1024,1024]{1,0:T(8,128)(2,1)} %collective-permute-done.11.refs_1_, bf16[1024,1024]{1,0:T(8,128)(2,1)S(1)} %copy-done.5), kind=kLoop, calls=%fused_computation | loop fusion | flops 2097152 | bytes 3145728 | tf_op jit(solution)/shard_map/convert_element_type | solution.py:399
  97.0 3.9 %collective-permute-start.12 = (bf16[512,1024]{1,0:T(8,128)(2,1)}, bf16[512,1024]{1,0:T(8,128)(2,1)}, u32[]{:S(2)}, u32[]{:S(2)}) collective-permute-start(bf16[512,1024]{1,0:T(8,128)(2,1)} %add_convert_fusion), channel_id=1, source_target_pairs={{0,16},{8,24},{16,0},{24,8},{1,17},{9,25},{17,1},{25,9},{2,18},{10... | collective-permute-start | bytes 3145736 | tf_op jit(solution)/shard_map/ppermute | solution.py:367
  100.9 2.6 %add_convert_fusion.1 = bf16[256,2048]{1,0:T(8,128)(2,1)} fusion(bf16[512,2048]{1,0:T(8,128)(2,1)} %collective-permute-done.9.refs_1_, bf16[512,2048]{1,0:T(8,128)(2,1)S(1)} %copy-done.8), kind=kLoop, calls=%fused_computation.1 | loop fusion | flops 2097152 | bytes 3145728 | tf_op jit(solution)/shard_map/convert_element_type | solution.py:399
  103.5 5.8 %all-to-all-done.2 = bf16[8,32,1024]{2,1,0:T(8,128)(2,1)S(1)} async-done(((bf16[8,32,1024]{2,1,0:T(8,128)(2,1)}), bf16[8,32,1024]{2,1,0:T(8,128)(2,1)S(1)}, u32[]{:S(2)}, u32[]{:S(2)}) %all-to-all-start.2) | async-done | bytes 524320 | tf_op jit(solution)/shard_map/all_to_all | solution.py:361
  109.3 1.0 copy-done.21
  110.3 3.3 %taps.1 = (bf16[128,1024]{1,0:T(8,128)(2,1)S(1)}, bf16[16,1024]{1,0:T(8,128)(2,1)S(1)}, bf16[16,1024]{1,0:T(8,128)(2,1)S(1)}, f32[32,1024]{1,0:T(8,128)S(1)}) custom-call(bf16[256,128]{1,0:T(8,128)(2,1)S(1)} %get-tuple-element.40.refs_4_.refs_0_, f32[128,1024]{1,0:T(8,128)S(1)} %copy-done.21, bf16[16,1024]{1,0:T(8,128)(2,1)S(1)} %collective-permute-done.refs_0_.refs_2_, ...), custom_call_target="tpu_custom_call" | custom-call | flops 67108864 | bytes 2097152 | tf_op jit(solution)/shard_map/taps/pallas_call | solution.py:84
  113.7 0.7 copy-done.22
  114.5 0.5 copy-done.29
  115.0 33.3 %all_to_all.25 = f32[32,1,1024]{2,1,0:T(1,128)} all-to-all(f32[32,1,1024]{2,1,0:T(1,128)S(1)} %copy.26), channel_id=1, replica_groups=mesh['dp'=4,'expert'=8] {'dp','expert'}, dimensions={0} | all-to-all | bytes 262144 | tf_op jit(solution)/shard_map/all_to_all | solution.py:417
  148.3 1.6 reduce_sum.9
  149.9 1.4 broadcast_in_dim.40
  151.3 6.0 %all-to-all-start.4 = ((f32[32,1,1024]{2,1,0:T(1,128)}), f32[32,1,1024]{2,1,0:T(1,128)}, u32[]{:S(2)}, u32[]{:S(2)}) async-start(f32[32,1,1024]{2,1,0:T(1,128)} %broadcast_in_dim.40), calls=%async_computation.4 | async-start | bytes 262144 | tf_op jit(solution)/shard_map/all_to_all | solution.py:420
  157.4 3.6 %collective-permute-start.7 = (bf16[16,1024]{1,0:T(8,128)(2,1)}, bf16[16,1024]{1,0:T(8,128)(2,1)S(1)}, u32[]{:S(2)}, u32[]{:S(2)}) collective-permute-start(bf16[16,1024]{1,0:T(8,128)(2,1)} %copy-done.30), channel_id=1, source_target_pairs={{0,1},{1,2},{2,3},{3,4},{4,5},{5,6},{6,7},{7,8},{8,9},{9,10},{10,1... | collective-permute-start | bytes 98312 | tf_op jit(solution)/shard_map/ppermute | solution.py:409
  161.0 1.3 collective-permute-start.8
  162.3 0.6 collective-permute-done.7.refs_0_
  162.9 4.1 %collective-permute-done.8.refs_2_ = bf16[16,1024]{1,0:T(8,128)(2,1)S(1)} collective-permute-done((bf16[16,1024]{1,0:T(8,128)(2,1)}, bf16[16,1024]{1,0:T(8,128)(2,1)S(1)}, u32[]{:S(2)}, u32[]{:S(2)}) %collective-permute-start.8) | collective-permute-done | bytes 32800 | tf_op jit(solution)/shard_map/ppermute | solution.py:409
  167.0 0.9 copy-done.23
  168.0 3.8 %frames.1 = bf16[128,1024]{1,0:T(8,128)(2,1)} custom-call(bf16[16,1024]{1,0:T(8,128)(2,1)S(1)} %collective-permute-done.7.refs_0_, bf16[128,1024]{1,0:T(8,128)(2,1)S(1)} %copy-done.23, bf16[16,1024]{1,0:T(8,128)(2,1)S(1)} %collective-permute-done.8.refs_2_, f32[32,1024]{1,0:T(8,128)S(1)} %copy-done.19, bf16[128,1024]{1,0:T(8,128)(2,1)S(1)} %copy-done.15), custom_call_target="tpu_custom_call" | custom-call | flops 67108864 | bytes 1048576 | tf_op jit(solution)/shard_map/frames/pallas_call | solution.py:84
  171.7 1.6 copy.29
  173.4 1.6 copy-done.6
  174.9 1.2 copy-done.12
  176.2 0.7 copy-done.25
  176.9 15.1 %adam_down.1 = (f32[512,1024]{1,0:T(8,128)}, bf16[512,1024]{1,0:T(8,128)(2,1)}, f32[8,512]{1,0:T(8,128)}, bf16[512,1024]{1,0:T(8,128)(2,1)}, f32[8,512]{1,0:T(8,128)}) custom-call(f32[512,1024]{1,0:T(8,128)S(1)} %bitcast.54, bf16[512,1024]{1,0:T(8,128)(2,1)S(1)} %bitcast.60, f32[8,512]{1,0:T(8,128)S(1)} %bitcast.68, bf16[512,1024]{1,0:T(8,128)(2,1)S(1)} %bitcast.61, ...), custom_call_target="tpu_custom_call" | custom-call | flops 10485760 | bytes 11534336 | tf_op jit(solution)/shard_map/adam_down/pallas_call | solution.py:338
  192.1 13.4 %adam_up.1 = (f32[256,2048]{1,0:T(8,128)}, bf16[256,2048]{1,0:T(8,128)(2,1)}, f32[16,256]{1,0:T(8,128)}, bf16[256,2048]{1,0:T(8,128)(2,1)}, f32[16,256]{1,0:T(8,128)}) custom-call(f32[256,2048]{1,0:T(8,128)S(1)} %bitcast.56, bf16[256,2048]{1,0:T(8,128)(2,1)S(1)} %bitcast.62, f32[16,256]{1,0:T(8,128)S(1)} %bitcast.70, bf16[256,2048]{1,0:T(8,128)(2,1)S(1)} %bitcast.63, ...), custom_call_target="tpu_custom_call" | custom-call | flops 10485760 | bytes 11534336 | tf_op jit(solution)/shard_map/adam_up/pallas_call | solution.py:338
  (67 shorter events, 0.7 us)
Async XLA Ops:
  0.6 1.6 copy-start
  2.2 1.6 copy-start.2
  3.8 5.0 %copy-start.15 = (bf16[128,1024]{1,0:T(8,128)(2,1)S(1)}, bf16[128,1024]{1,0:T(8,128)(2,1)}, u32[]{:S(2)}) copy-start(bf16[128,1024]{1,0:T(8,128)(2,1)} %refs_4_.1) | copy-start | bytes 786436
  3.8 5.0 %copy-start.28 = (s32[128,1]{0,1:T(1,128)S(1)}, s32[128,1]{0,1:T(1,128)}, u32[]{:S(2)}) copy-start(s32[128,1]{0,1:T(1,128)} %param.16) | copy-start | bytes 1540
  3.8 29.1 %copy-start.10 = (bf16[128,1024]{1,0:T(8,128)(2,1)S(1)}, bf16[128,1024]{1,0:T(8,128)(2,1)}, u32[]{:S(2)}) copy-start(bf16[128,1024]{1,0:T(8,128)(2,1)} %refs_3_.4) | copy-start | bytes 786436
  3.8 36.6 %copy-start.19 = (f32[32,1024]{1,0:T(8,128)S(1)}, f32[32,1024]{1,0:T(8,128)}, u32[]{:S(2)}) copy-start(f32[32,1024]{1,0:T(8,128)} %refs_3_.5) | copy-start | bytes 393220
  5.6 27.3 %collective-permute-start.3 = (bf16[512,1024]{1,0:T(8,128)(2,1)}, bf16[512,1024]{1,0:T(8,128)(2,1)}, u32[]{:S(2)}, u32[]{:S(2)}) collective-permute-start(bf16[512,1024]{1,0:T(8,128)(2,1)} %get-tuple-element.45), channel_id=1, source_target_pairs={{0,16},{8,24},{16,0},{24,8},{1,17},{9,25},{17,1},{25,9},{2,18},{10... | collective-permute-start | bytes 3145736 | tf_op jit(solution)/shard_map/ppermute | solution.py:367
  8.7 60.2 %collective-permute-start.2 = (bf16[1024,1024]{1,0:T(8,128)(2,1)S(1)}, bf16[1024,1024]{1,0:T(8,128)(2,1)}, u32[]{:S(2)}, u32[]{:S(2)}) collective-permute-start(bf16[1024,1024]{1,0:T(8,128)(2,1)S(1)} %get-tuple-element.44.refs_3_.refs_7_), channel_id=1, source_target_pairs={{0,8},{8,0},{16,24},{24,16},{1,9},{9,1},{17,25},{25,17},{2,10},{10... | collective-permute-start | bytes 6291464 | tf_op jit(solution)/shard_map/ppermute | solution.py:374
  8.7 45.9 %collective-permute-start.5 = (bf16[512,1024]{1,0:T(8,128)(2,1)}, bf16[512,1024]{1,0:T(8,128)(2,1)}, u32[]{:S(2)}, u32[]{:S(2)}) collective-permute-start(bf16[512,1024]{1,0:T(8,128)(2,1)} %get-tuple-element.47), channel_id=1, source_target_pairs={{0,16},{8,24},{16,0},{24,8},{1,17},{9,25},{17,1},{25,9},{2,18},{10... | collective-permute-start | bytes 3145736 | tf_op jit(solution)/shard_map/ppermute | solution.py:367
  9.5 0.8 copy-start.18
  10.3 35.5 %all-to-all-start = ((bf16[8,32,1024]{2,1,0:T(8,128)(2,1)}), bf16[8,32,1024]{2,1,0:T(8,128)(2,1)S(1)}, u32[]{:S(2)}, u32[]{:S(2)}) async-start(bf16[8,32,1024]{2,1,0:T(8,128)(2,1)} %bitcast.66), calls=%async_computation | async-start | bytes 1048576 | tf_op jit(solution)/shard_map/all_to_all | solution.py:361
  33.0 35.9 %collective-permute-start.4 = (bf16[512,1024]{1,0:T(8,128)(2,1)}, bf16[512,1024]{1,0:T(8,128)(2,1)}, u32[]{:S(2)}, u32[]{:S(2)}) collective-permute-start(bf16[512,1024]{1,0:T(8,128)(2,1)} %collective-permute-done.3.refs_5_.refs_9_), channel_id=1, source_target_pairs={{0,8},{8,0},{16,24},{24,16},{1,9},{9,1},{17,25},{25,17},{2,10},{10... | collective-permute-start | bytes 3145736 | tf_op jit(solution)/shard_map/ppermute | solution.py:374
  33.0 6.0 %collective-permute-start.1 = (bf16[16,1024]{1,0:T(8,128)(2,1)S(1)}, bf16[16,1024]{1,0:T(8,128)(2,1)S(1)}, u32[]{:S(2)}, u32[]{:S(2)}) collective-permute-start(bf16[16,1024]{1,0:T(8,128)(2,1)S(1)} %get-tuple-element.68), channel_id=1, source_target_pairs={{1,0},{2,1},{3,2},{4,3},{5,4},{6,5},{7,6},{8,7},{9,8},{10,9},{11,1... | collective-permute-start | bytes 98312 | tf_op jit(solution)/shard_map/ppermute | solution.py:409
  34.3 6.1 %collective-permute-start = (bf16[16,1024]{1,0:T(8,128)(2,1)S(1)}, bf16[16,1024]{1,0:T(8,128)(2,1)S(1)}, u32[]{:S(2)}, u32[]{:S(2)}) collective-permute-start(bf16[16,1024]{1,0:T(8,128)(2,1)S(1)} %get-tuple-element.69), channel_id=1, source_target_pairs={{0,1},{1,2},{2,3},{3,4},{4,5},{5,6},{6,7},{7,8},{8,9},{9,10},{10,1... | collective-permute-start | bytes 98312 | tf_op jit(solution)/shard_map/ppermute | solution.py:409
  44.2 0.8 copy-start.16
  45.0 0.8 copy-start.20
  45.8 23.0 %all-to-all-start.1 = ((bf16[8,32,1024]{2,1,0:T(8,128)(2,1)}), bf16[8,32,1024]{2,1,0:T(8,128)(2,1)}, u32[]{:S(2)}, u32[]{:S(2)}) async-start(bf16[8,32,1024]{2,1,0:T(8,128)(2,1)} %bitcast.64), calls=%async_computation.1 | async-start | bytes 1048576 | tf_op jit(solution)/shard_map/all_to_all | solution.py:361
  54.6 23.2 %collective-permute-start.6 = (bf16[512,1024]{1,0:T(8,128)(2,1)}, bf16[512,1024]{1,0:T(8,128)(2,1)}, u32[]{:S(2)}, u32[]{:S(2)}) collective-permute-start(bf16[512,1024]{1,0:T(8,128)(2,1)} %collective-permute-done.5.refs_5_), channel_id=1, source_target_pairs={{0,8},{8,0},{16,24},{24,16},{1,9},{9,1},{17,25},{25,17},{2,10},{10... | collective-permute-start | bytes 3145736 | tf_op jit(solution)/shard_map/ppermute | solution.py:374
  76.1 8.3 %copy-start.4 = (bf16[1024,1024]{1,0:T(8,128)(2,1)}, bf16[1024,1024]{1,0:T(8,128)(2,1)S(1)}, u32[]{:S(2)}) copy-start(bf16[1024,1024]{1,0:T(8,128)(2,1)S(1)} %get-tuple-element.61.refs_0_) | copy-start | bytes 6291460
  76.1 18.1 %collective-permute-start.11 = (bf16[1024,1024]{1,0:T(8,128)(2,1)}, bf16[1024,1024]{1,0:T(8,128)(2,1)}, u32[]{:S(2)}, u32[]{:S(2)}) collective-permute-start(bf16[1024,1024]{1,0:T(8,128)(2,1)} %get-tuple-element.62), channel_id=1, source_target_pairs={{0,8},{8,0},{16,24},{24,16},{1,9},{9,1},{17,25},{25,17},{2,10},{10... | collective-permute-start | bytes 6291464 | tf_op jit(solution)/shard_map/ppermute | solution.py:374
  84.5 0.8 copy-start.17
  85.3 9.0 %copy-start.5 = (bf16[1024,1024]{1,0:T(8,128)(2,1)S(1)}, bf16[1024,1024]{1,0:T(8,128)(2,1)}, u32[]{:S(2)}) copy-start(bf16[1024,1024]{1,0:T(8,128)(2,1)} %copy-done.4) | copy-start | bytes 6291460
  89.1 1.3 copy-start.7
  90.4 10.5 %collective-permute-start.9 = (bf16[512,2048]{1,0:T(8,128)(2,1)}, bf16[512,2048]{1,0:T(8,128)(2,1)}, u32[]{:S(2)}, u32[]{:S(2)}) collective-permute-start(bf16[512,2048]{1,0:T(8,128)(2,1)} %get-tuple-element.55), channel_id=1, source_target_pairs={{0,8},{8,0},{16,24},{24,16},{1,9},{9,1},{17,25},{25,17},{2,10},{10... | collective-permute-start | bytes 6291464 | tf_op jit(solution)/shard_map/ppermute | solution.py:374
  90.4 18.8 %all-to-all-start.2 = ((bf16[8,32,1024]{2,1,0:T(8,128)(2,1)}), bf16[8,32,1024]{2,1,0:T(8,128)(2,1)S(1)}, u32[]{:S(2)}, u32[]{:S(2)}) async-start(bf16[8,32,1024]{2,1,0:T(8,128)(2,1)} %bitcast.65), calls=%async_computation.2 | async-start | bytes 1048576 | tf_op jit(solution)/shard_map/all_to_all | solution.py:361
  94.2 6.7 %copy-start.8 = (bf16[512,2048]{1,0:T(8,128)(2,1)S(1)}, bf16[512,2048]{1,0:T(8,128)(2,1)}, u32[]{:S(2)}) copy-start(bf16[512,2048]{1,0:T(8,128)(2,1)} %copy-done.7) | copy-start | bytes 6291460
  97.0 76.4 %collective-permute-start.12 = (bf16[512,1024]{1,0:T(8,128)(2,1)}, bf16[512,1024]{1,0:T(8,128)(2,1)}, u32[]{:S(2)}, u32[]{:S(2)}) collective-permute-start(bf16[512,1024]{1,0:T(8,128)(2,1)} %add_convert_fusion), channel_id=1, source_target_pairs={{0,16},{8,24},{16,0},{24,8},{1,17},{9,25},{17,1},{25,9},{2,18},{10... | collective-permute-start | bytes 3145736 | tf_op jit(solution)/shard_map/ppermute | solution.py:367
  100.9 72.4 %copy-start.24 = (f32[1,512,8]{1,2,0:T(8,128)S(1)}, f32[1,512,8]{1,2,0:T(8,128)}, u32[]{:S(2)}) copy-start(f32[1,512,8]{1,2,0:T(8,128)} %param.25) | copy-start | bytes 49156
  103.5 69.8 %copy-start.1 = (f32[1,512,1024]{2,1,0:T(8,128)S(1)}, f32[1,512,1024]{2,1,0:T(8,128)}, u32[]{:S(2)}) copy-start(f32[1,512,1024]{2,1,0:T(8,128)} %param.19) | copy-start | bytes 6291460
  103.5 88.5 %collective-permute-start.10 = (bf16[256,2048]{1,0:T(8,128)(2,1)}, bf16[256,2048]{1,0:T(8,128)(2,1)}, u32[]{:S(2)}, u32[]{:S(2)}) collective-permute-start(bf16[256,2048]{1,0:T(8,128)(2,1)} %add_convert_fusion.1), channel_id=1, source_target_pairs={{0,16},{8,24},{16,0},{24,8},{1,17},{9,25},{17,1},{25,9},{2,18},{10... | collective-permute-start | bytes 3145736 | tf_op jit(solution)/shard_map/ppermute | solution.py:367
  109.3 1.0 copy-start.21
  113.7 0.7 copy-start.22
  114.4 0.6 copy-start.29
  114.4 0.6 copy-start.30
  114.4 59.0 %copy-start.11 = (bf16[1,512,1024]{2,1,0:T(8,128)(2,1)S(1)}, bf16[1,512,1024]{2,1,0:T(8,128)(2,1)}, u32[]{:S(2)}) copy-start(bf16[1,512,1024]{2,1,0:T(8,128)(2,1)} %param.24) | copy-start | bytes 3145732
  151.3 20.4 %all-to-all-start.4 = ((f32[32,1,1024]{2,1,0:T(1,128)}), f32[32,1,1024]{2,1,0:T(1,128)}, u32[]{:S(2)}, u32[]{:S(2)}) async-start(f32[32,1,1024]{2,1,0:T(1,128)} %broadcast_in_dim.40), calls=%async_computation.4 | async-start | bytes 262144 | tf_op jit(solution)/shard_map/all_to_all | solution.py:420
  157.4 5.5 %collective-permute-start.7 = (bf16[16,1024]{1,0:T(8,128)(2,1)}, bf16[16,1024]{1,0:T(8,128)(2,1)S(1)}, u32[]{:S(2)}, u32[]{:S(2)}) collective-permute-start(bf16[16,1024]{1,0:T(8,128)(2,1)} %copy-done.30), channel_id=1, source_target_pairs={{0,1},{1,2},{2,3},{3,4},{4,5},{5,6},{6,7},{7,8},{8,9},{9,10},{10,1... | collective-permute-start | bytes 98312 | tf_op jit(solution)/shard_map/ppermute | solution.py:409
  161.0 6.0 %collective-permute-start.8 = (bf16[16,1024]{1,0:T(8,128)(2,1)}, bf16[16,1024]{1,0:T(8,128)(2,1)S(1)}, u32[]{:S(2)}, u32[]{:S(2)}) collective-permute-start(bf16[16,1024]{1,0:T(8,128)(2,1)} %copy-done.29), channel_id=1, source_target_pairs={{1,0},{2,1},{3,2},{4,3},{5,4},{6,5},{7,6},{8,7},{9,8},{10,9},{11,1... | collective-permute-start | bytes 98312 | tf_op jit(solution)/shard_map/ppermute | solution.py:409
  167.0 1.0 copy-start.23
  173.3 1.6 copy-start.6
  174.9 1.2 copy-start.12
  176.2 0.7 copy-start.25
  176.9 15.1 %copy-start.3 = (f32[1,256,2048]{2,1,0:T(8,128)S(1)}, f32[1,256,2048]{2,1,0:T(8,128)}, u32[]{:S(2)}) copy-start(f32[1,256,2048]{2,1,0:T(8,128)} %param.18) | copy-start | bytes 6291460
  176.9 15.1 %copy-start.9 = (bf16[512,2048]{1,0:T(8,128)(2,1)S(1)}, bf16[512,2048]{1,0:T(8,128)(2,1)}, u32[]{:S(2)}) copy-start(bf16[512,2048]{1,0:T(8,128)(2,1)} %copy-done.7) | copy-start | bytes 6291460
  176.9 15.1 %copy-start.13 = (bf16[1,256,2048]{2,1,0:T(8,128)(2,1)S(1)}, bf16[1,256,2048]{2,1,0:T(8,128)(2,1)}, u32[]{:S(2)}) copy-start(bf16[1,256,2048]{2,1,0:T(8,128)(2,1)} %param.20) | copy-start | bytes 3145732
  176.9 15.1 %copy-start.14 = (bf16[1,256,2048]{2,1,0:T(8,128)(2,1)S(1)}, bf16[1,256,2048]{2,1,0:T(8,128)(2,1)}, u32[]{:S(2)}) copy-start(bf16[1,256,2048]{2,1,0:T(8,128)(2,1)} %param.22) | copy-start | bytes 3145732
  176.9 15.1 %copy-start.26 = (f32[1,256,16]{1,2,0:T(8,128)S(1)}, f32[1,256,16]{1,2,0:T(8,128)}, u32[]{:S(2)}) copy-start(f32[1,256,16]{1,2,0:T(8,128)} %param.21) | copy-start | bytes 49156
  176.9 15.1 %copy-start.27 = (f32[1,256,16]{1,2,0:T(8,128)S(1)}, f32[1,256,16]{1,2,0:T(8,128)}, u32[]{:S(2)}) copy-start(f32[1,256,16]{1,2,0:T(8,128)} %param.23) | copy-start | bytes 49156

commit v2 on v1

v2 whole, which is shorter than its diff:
```python
import functools

import jax
import jax.numpy as jnp
from jax import lax
from jax.experimental import pallas as pl
from jax.experimental.pallas import tpu as pltpu
from jax.sharding import PartitionSpec as P

beta_one = 0.9
beta_two = 0.95
bias_one = 1.0 - beta_one**10
bias_two = 1.0 - beta_two**10
learn_rate = 0.001
adam_eps = 1e-08
scale_eps = 1e-06

f32 = jnp.float32
bf16 = jnp.bfloat16
MIB = 1 << 20


def swish_parts(values):
    gate_value = jax.nn.sigmoid(values)
    return (values * gate_value, gate_value * (1.0 + values * (1.0 - gate_value)))


def across(lhs, rhs):
    return lax.dot_general(lhs, rhs, (((0,), (0,)), ((), ())), preferred_element_type=f32)


def along(lhs, rhs):
    return lax.dot_general(lhs, rhs, (((1,), (1,)), ((), ())), preferred_element_type=f32)


class Place:
    def __init__(self, dp_size, experts, index_ref):
        index = index_ref[0]
        rank = index // experts
        chips = dp_size // 2
        self.chip, self.core = rank // 2, rank % 2
        self.first = (index > 0).astype(f32)
        self.last = (index < dp_size * experts - 1).astype(f32)
        self.came = [(self.chip + chips - shift) % chips for shift in range(chips)]
        self.goes = [(self.chip + shift) % chips for shift in range(chips)]
        self.shards = [2 * chip + core for chip in self.came for core in (self.core, 1 - self.core)]


def at(block, size):
    return pl.ds(pl.multiple_of(block * size, size), size)


def staged(kernel, counts, spans, *refs):
    groups = []
    for count in counts:
        groups.append(refs[:count])
        refs = refs[count:]
    scalars, sources, _, targets, held, made, scratch = groups
    in_sems, out_sems = refs
    arriving = []
    for index, source in enumerate(sources):
        if spans[index] is not None:
            source = source.at[pl.ds(*spans[index]), :]
        copy = pltpu.make_async_copy(source, held[index], in_sems.at[index])
        copy.start()
        arriving.append(copy)
    leaving = {}

    def take(index):
        if arriving[index] is not None:
            arriving[index].wait()
            arriving[index] = None
        return held[index]

    def give(index):
        leaving[index] = pltpu.make_async_copy(made[index], targets[index], out_sems.at[index])
        leaving[index].start()

    kernel(scalars, take, made, give, scratch)
    for index in range(len(targets)):
        if index not in leaving:
            give(index)
    for index in range(len(sources)):
        take(index)
    for copy in leaving.values():
        copy.wait()


def call(kernel, name, scalars, inputs, outs, scratch=(), after=(), flops=0, moved=0, limit=60):
    hbm = pl.BlockSpec(memory_space=pltpu.HBM)
    smem = pl.BlockSpec(memory_space=pltpu.SMEM)
    pairs = [item if isinstance(item, tuple) else (item, None) for item in inputs]
    arrays = [array for array, _ in pairs]
    spans = [span for _, span in pairs]
    held = [
        pltpu.VMEM(array.shape if span is None else (span[1],) + array.shape[1:], array.dtype)
        for array, span in pairs
    ]
    made = [pltpu.VMEM(shape, kind) for shape, kind in outs]
    counts = (len(scalars), len(arrays), len(after), len(outs), len(held), len(made), len(scratch))
    return pl.pallas_call(
        functools.partial(staged, kernel, counts, spans),
        out_shape=[jax.ShapeDtypeStruct(shape, kind) for shape, kind in outs],
        in_specs=[smem] * len(scalars) + [hbm] * (len(arrays) + len(after)),
        out_specs=[hbm] * len(outs),
        scratch_shapes=held
        + made
        + list(scratch)
        + [pltpu.SemaphoreType.DMA((len(arrays),)), pltpu.SemaphoreType.DMA((len(outs),))],
        compiler_params=pltpu.CompilerParams(vmem_limit_bytes=limit * MIB),
        cost_estimate=pl.CostEstimate(flops=flops, bytes_accessed=moved, transcendentals=0),
        name=name,
    )(*scalars, *arrays, *after)


def dispatch_kernel(experts, capacity, scalars, take, made, give, scratch):
    place_ref, out_ref = made
    ids = take(0)[...]
    length = ids.shape[1]
    rows = lax.broadcasted_iota(jnp.int32, (experts, length), 0)
    one_hot = (rows == ids).astype(f32)
    earlier = lax.broadcasted_iota(jnp.int32, (length, length), 0)
    later = lax.broadcasted_iota(jnp.int32, (length, length), 1)
    ranks = jnp.dot(one_hot, (earlier < later).astype(f32), preferred_element_type=f32)
    slot = jnp.sum(ranks * one_hot, axis=0, keepdims=True).astype(jnp.int32)
    position = ids * capacity + slot
    slots = lax.broadcasted_iota(jnp.int32, (experts * capacity, length), 0)
    place = (slots == position).astype(f32).astype(bf16)
    place_ref[...] = place
    out_ref[...] = jnp.dot(place, take(1)[...], preferred_element_type=f32).astype(bf16)


def fill_padded(pad_ref, place, left, middle, right, cols):
    side, length = left.shape[0], middle.shape[0]
    pad_ref[0:side, :] = left[:, cols].astype(f32) * place.first
    pad_ref[side : side + length, :] = middle[:, cols].astype(f32)
    pad_ref[side + length : side + length + side, :] = right[:, cols].astype(f32) * place.last
    pad_ref[side + length + side :, :] = jnp.zeros((8, pad_ref.shape[1]), f32)


def slide(pad_ref, shift_ref, weights, length):
    total = None
    for rest in range(8):
        part = None
        for tile in range(0, len(weights) - rest, 8):
            if weights[tile + rest] is not None:
                term = weights[tile + rest] * pad_ref[tile : tile + length + 8, :]
                part = term if part is None else part + term
        if rest == 0:
            total = part[:length]
        else:
            shift_ref[: length + 8, :] = part
            total = total + shift_ref[rest : rest + length, :]
    return total


def conv_kernel(here, scalars, take, made, give, scratch):
    slope_ref, out_ref = made
    pad_ref, shift_ref, feat_ref = scratch
    place = here(scalars[0])
    left, frames, right, taps_ref = take(0), take(1), take(2), take(3)
    length, width = feat_ref.shape

    def lanes(step, carry):
        cols = at(step, 128)
        fill_padded(pad_ref, place, left, frames, right, cols)
        weights = [taps_ref[tap : tap + 1, cols] for tap in range(taps_ref.shape[0])]
        active, slope = swish_parts(slide(pad_ref, shift_ref, weights, length))
        slope_ref[:, cols] = slope
        feat_ref[:, cols] = active.astype(bf16)
        return carry

    lax.fori_loop(0, width // 128, lanes, 0)
    give(0)
    out_ref[...] = jnp.dot(take(4)[...], feat_ref[...], preferred_element_type=f32).astype(bf16)


def group_kernel(here, scalars, take, made, give, scratch):
    hidden_ref, pre_ref, part_ref = made
    (slope_ref,) = scratch
    place = here(scalars[0])
    rows_ref = take(0)
    up_refs = [take(1 + shard) for shard in range(len(place.shards))]
    depth = up_refs[0].shape[0]
    units = hidden_ref.shape[1]
    chunk = 256

    def step(index, carry):
        cols = at(index, chunk)
        pre = 0.0
        for shard, up_ref in zip(place.shards, up_refs):
            pre = pre + jnp.dot(
                rows_ref[:, at(shard, depth)], up_ref[:, cols], preferred_element_type=f32
            )
        active, slope = swish_parts(pre)
        hidden_ref[:, cols] = active.astype(bf16)
        slope_ref[:, cols] = slope
        return carry

    lax.fori_loop(0, units // chunk, step, 0, unroll=True)
    give(0)
    grads = take(1 + len(up_refs))[...]
    share = units // 2
    for side, core in enumerate((place.core, 1 - place.core)):
        cols = at(core, share)
        back = along(grads, take(2 + len(up_refs) + side)[...])
        pre_ref[:, cols] = (back * slope_ref[:, cols]).astype(bf16)
    give(1)
    pre = pre_ref[...]
    for shard, up_ref in zip(place.shards, up_refs):
        part_ref[:, at(shard, depth)] = along(pre, up_ref[...]).astype(part_ref.dtype)


def up_grad_kernel(here, groups, scalars, take, made, give, scratch):
    keep_ref, send_ref = made
    place = here(scalars[0])
    row_refs = [take(group) for group in range(groups)]
    pres = [take(groups + group)[...] for group in range(groups)]
    depth = keep_ref.shape[0] // groups
    for out_ref, core in ((send_ref, 1 - place.core), (keep_ref, place.core)):
        for index, chip in enumerate(place.goes):
            total = 0.0
            for row_ref, pre in zip(row_refs, pres):
                total = total + across(row_ref[:, at(2 * chip + core, depth)], pre)
            out_ref[index * depth : (index + 1) * depth, :] = total.astype(bf16)
        give(0 if out_ref is keep_ref else 1)


def down_grad_kernel(here, groups, scalars, take, made, give, scratch):
    keep_ref, send_ref = made
    place = here(scalars[0])
    share = keep_ref.shape[0]
    hidden_refs = [take(group) for group in range(groups)]
    grads = [take(groups + group)[...] for group in range(groups)]
    for out_ref, core in ((send_ref, 1 - place.core), (keep_ref, place.core)):
        total = 0.0
        for hidden_ref, grad in zip(hidden_refs, grads):
            total = total + across(hidden_ref[:, at(core, share)], grad)
        out_ref[...] = total.astype(bf16)
        give(0 if out_ref is keep_ref else 1)


def cast_far_kernel(here, scalars, take, made, give, scratch):
    place = here(scalars[0])
    units = made[0].shape[1]
    for index, up_ref in enumerate(made):
        up_ref[...] = take(0)[:, at(place.goes[index + 1], units)].astype(bf16)
        give(index)


def cast_near_kernel(here, scalars, take, made, give, scratch):
    place = here(scalars[0])
    up_ref, down_ref = made
    up_ref[...] = take(0)[:, at(place.chip, up_ref.shape[1])].astype(bf16)
    give(0)
    down_ref[...] = take(1)[...].astype(bf16)


def taps_kernel(here, scalars, take, made, give, scratch):
    grad_ref, head_ref, tail_ref, terms_ref = made
    pad_ref, shift_ref = scratch
    place = here(scalars[0])
    length, width = grad_ref.shape
    side = head_ref.shape[0]
    features = across(take(0)[...], take(5)[...]).astype(bf16).astype(f32)
    grad = (features * take(1)[...]).astype(bf16)
    grad_ref[...] = grad
    head_ref[...] = grad[:side]
    tail_ref[...] = grad[length - side :]
    give(1)
    give(2)
    give(0)
    left, frames, right = take(2), take(3), take(4)
    shift_ref[0:8, :] = jnp.zeros((8, 128), f32)
    shift_ref[8 + length :, :] = jnp.zeros((8, 128), f32)
    for step in range(width // 128):
        cols = slice(step * 128, (step + 1) * 128)
        fill_padded(pad_ref, place, left, frames, right, cols)
        shift_ref[8 : 8 + length, :] = grad_ref[:, cols].astype(f32)
        for rest in range(8):
            moved = shift_ref[8 - rest : 8 - rest + length + 8, :]
            for tap in range(rest, terms_ref.shape[0], 8):
                product = moved * pad_ref[tap - rest : tap - rest + length + 8, :]
                terms_ref[tap, step : step + 1, :] = jnp.sum(product, axis=0, keepdims=True)


def frames_kernel(here, scalars, take, made, give, scratch):
    (out_ref,) = made
    pad_ref, shift_ref = scratch
    place = here(scalars[0])
    length, width = out_ref.shape
    left, grad, right, taps_ref, cot_ref = take(0), take(1), take(2), take(3), take(4)
    count = taps_ref.shape[0]

    def lanes(step, carry):
        cols = at(step, 128)
        fill_padded(pad_ref, place, left, grad, right, cols)
        weights = [None] + [taps_ref[tap : tap + 1, cols] for tap in range(count - 1, -1, -1)]
        total = slide(pad_ref, shift_ref, weights, length)
        out_ref[:, cols] = (cot_ref[:, cols].astype(f32) + total).astype(bf16)
        return carry

    lax.fori_loop(0, width // 128, lanes, 0)


def adam_kernel(
    here, sums, index_ref, master_ref, mean_ref, mean_scale_ref, square_ref, square_scale_ref, *refs
):
    keep_ref, theirs_ref, far_refs, refs = refs[0], refs[1], refs[2 : 2 + sums], refs[2 + sums :]
    next_ref, mean_next_ref, mean_top_ref, square_next_ref, square_top_ref = refs[:5]
    scales_ref, tops_ref, grad_ref = refs[5:]
    rows, width = master_ref.shape
    blocks = mean_scale_ref.shape[0]
    size = width // blocks
    units = keep_ref.shape[1]
    step = pl.program_id(0)
    steps = pl.num_programs(0)

    @pl.when(step == 0)
    def _():
        scales_ref[0, :, :blocks] = mean_scale_ref[...].T
        scales_ref[1, :, :blocks] = square_scale_ref[...].T

    place = here(index_ref)
    near = slice(0, width) if units == width else at(place.chip, units)
    grad_ref[:, near] = keep_ref[...].astype(f32) + theirs_ref[...].astype(f32)
    for index, far_ref in enumerate(far_refs):
        grad_ref[:, at(place.came[index + 1], units)] = far_ref[...].astype(f32)

    part = at(step, rows)
    mean_scales = scales_ref[0, part, :]
    square_scales = scales_ref[1, part, :]
    for block in range(blocks):
        cols = slice(block * size, (block + 1) * size)
        grad = grad_ref[:, cols]
        mean = beta_one * (
            mean_ref[:, cols].astype(f32) * mean_scales[:, block : block + 1]
        ) + (1.0 - beta_one) * grad
        square = beta_two * (
            square_ref[:, cols].astype(f32) * square_scales[:, block : block + 1]
        ) + (1.0 - beta_two) * (grad * grad)
        root = jnp.sqrt(square * (1.0 / bias_two)) + adam_eps
        next_ref[:, cols] = master_ref[:, cols] - (learn_rate / bias_one) * (mean / root)
        mean_top = jnp.max(jnp.abs(mean), axis=1, keepdims=True) + scale_eps
        square_top = jnp.max(square, axis=1, keepdims=True) + scale_eps
        mean_next_ref[:, cols] = (mean * (1.0 / mean_top)).astype(bf16)
        square_next_ref[:, cols] = (square * (1.0 / square_top)).astype(bf16)
        tops_ref[0, part, block : block + 1] = mean_top
        tops_ref[1, part, block : block + 1] = square_top

    @pl.when(step == steps - 1)
    def _():
        mean_top_ref[...] = tops_ref[0, :, :blocks].T
        square_top_ref[...] = tops_ref[1, :, :blocks].T


def adam(name, here, index, master, grads, mean_code, mean_scale, square_code, square_scale):
    _, rows, width = master.shape
    blocks = mean_scale.shape[-1]
    part = min(rows, (1 << 18) // width)
    tile = pl.BlockSpec((part, width), lambda i: (i, 0))
    whole = pl.BlockSpec((blocks, rows), lambda i: (0, 0))
    pieces = [pl.BlockSpec((part, grad.shape[1]), lambda i: (i, 0)) for grad in grads]
    wide = jax.ShapeDtypeStruct((rows, width), f32)
    code = jax.ShapeDtypeStruct((rows, width), bf16)
    scale = jax.ShapeDtypeStruct((blocks, rows), f32)
    results = pl.pallas_call(
        functools.partial(adam_kernel, here, len(grads) - 2),
        grid=(rows // part,),
        out_shape=[wide, code, scale, code, scale],
        in_specs=[pl.BlockSpec(memory_space=pltpu.SMEM), tile, tile, whole, tile, whole] + pieces,
        out_specs=[tile, tile, whole, tile, whole],
        scratch_shapes=[
            pltpu.VMEM((2, rows, 128), f32),
            pltpu.VMEM((2, rows, 128), f32),
            pltpu.VMEM((part, width), f32),
        ],
        compiler_params=pltpu.CompilerParams(vmem_limit_bytes=60 * MIB),
        cost_estimate=pl.CostEstimate(
            flops=20 * rows * width,
            bytes_accessed=(16 + 2 * len(grads)) * rows * width,
            transcendentals=0,
        ),
        name=name,
    )(index, master[0], mean_code[0], mean_scale[0].T, square_code[0], square_scale[0].T, *grads)
    new_master, mean_next, mean_top, square_next, square_top = results
    return (new_master[None], mean_next[None], mean_top.T[None], square_next[None], square_top.T[None])


def by_expert(rows):
    experts = lax.axis_size("expert")
    slots, width = rows.shape
    cells = rows.reshape(experts, slots // experts, width)
    return lax.all_to_all(cells, "expert", 0, 0, tiled=True).reshape(slots, width)


def to_chip(values, shift):
    count = lax.axis_size("dp")
    chips = count // 2
    return lax.ppermute(
        values, "dp", [(i, (i // 2 + shift) % chips * 2 + i % 2) for i in range(count)]
    )


def to_core(values):
    count = lax.axis_size("dp")
    return lax.ppermute(values, "dp", [(i, i ^ 1) for i in range(count)])


def halo(head, tail):
    axes = ("dp", "expert")
    count = lax.axis_size("dp") * lax.axis_size("expert")
    right = [(i, (i + 1) % count) for i in range(count)]
    left = [((i + 1) % count, i) for i in range(count)]
    return lax.ppermute(tail, axes, right), lax.ppermute(head, axes, left)


def sum_everywhere(terms):
    axes = ("dp", "expert")
    count = lax.axis_size("dp") * lax.axis_size("expert")
    taps, strips, lanes = terms.shape
    cells = terms.reshape(count, taps * strips // count, lanes)
    mine = jnp.sum(lax.all_to_all(cells, axes, 0, 0, tiled=True), axis=0)
    spread = jnp.broadcast_to(mine[None], cells.shape)
    return lax.all_to_all(spread, axes, 0, 0, tiled=True).reshape(taps, strips * lanes)


def body(
    frames,
    cotangent,
    expert_ids,
    conv_weight,
    up_master,
    down_master,
    up_mean_code,
    up_mean_scale,
    up_square_code,
    up_square_scale,
    down_mean_code,
    down_mean_scale,
    down_square_code,
    down_square_scale,
):
    length, width = frames.shape
    taps = conv_weight.shape[0]
    side = taps // 2
    experts = lax.axis_size("expert")
    dp_size = lax.axis_size("dp")
    capacity = 2 * length // experts
    slots = experts * capacity
    hidden = up_master.shape[2]
    chips = dp_size // 2
    index = lax.axis_index("dp") * experts + lax.axis_index("expert")
    index = index.astype(jnp.int32).reshape(1)
    here = functools.partial(Place, dp_size, experts)
    product = 2 * slots * width * hidden // chips
    row_shape = ((slots, width), bf16)
    strips = [pltpu.VMEM((length + 2 * side + 8, 128), f32), pltpu.VMEM((length + 16, 128), f32)]
    share, depth, units = hidden // dp_size, width // dp_size, hidden // chips

    left, right = halo(frames[:side], frames[length - side :])
    up_parts = call(
        functools.partial(cast_far_kernel, here),
        "cast_far",
        [index],
        [up_master[0]],
        [((depth, units), bf16)] * (chips - 1),
        moved=12 * share * width,
    )
    far_ups = [to_chip(part, shift + 1) for shift, part in enumerate(up_parts)]
    up_own, down_own = call(
        functools.partial(cast_near_kernel, here),
        "cast_near",
        [index],
        [up_master[0], down_master[0]],
        [((depth, units), bf16), ((share, width), bf16)],
        after=up_parts[:1],
        moved=12 * share * width,
    )
    ups = [up_own, to_core(up_own)]
    downs = [down_own, to_core(down_own)]
    for arrived in far_ups:
        ups = ups + [arrived, to_core(arrived)]
    place, send_grads = call(
        functools.partial(dispatch_kernel, experts, capacity),
        "dispatch",
        [],
        [expert_ids.reshape(1, length), cotangent],
        [((slots, length), bf16), row_shape],
        after=up_parts[:1],
        flops=2 * slots * length * width,
        moved=4 * slots * width,
    )
    grads_in = by_expert(send_grads)
    slope, send_rows = call(
        functools.partial(conv_kernel, here),
        "convolve",
        [index],
        [left, frames, right, conv_weight, place],
        [((length, width), f32), row_shape],
        after=far_ups,
        scratch=strips + [pltpu.VMEM((length, width), bf16)],
        flops=2 * slots * length * width,
        moved=8 * slots * width,
    )
    rows_in = by_expert(send_rows)

    group_rows = [rows_in] + [to_chip(rows_in, shift) for shift in range(1, chips)]
    group_grads = [grads_in] + [to_chip(grads_in, shift) for shift in range(1, chips)]
    hiddens, pres, parts = [], [], []
    for group in range(chips):
        results = call(
            functools.partial(group_kernel, here),
            "own_group" if group == 0 else "far_group",
            [index],
            [group_rows[group]] + ups + [group_grads[group]] + downs,
            [
                ((slots, units), bf16),
                ((slots, units), bf16),
                ((slots, width), f32 if group == 0 else bf16),
            ],
            scratch=[pltpu.VMEM((slots, units), f32)],
            after=parts[:1],
            flops=3 * product,
            moved=8 * width * units,
        )
        for kind, result in zip((hiddens, pres, parts), results):
            kind.append(result)
    back_total = parts[0]
    for shift in range(1, chips):
        back_total = back_total + to_chip(parts[shift], -shift).astype(f32)
    returned = by_expert(back_total.astype(bf16))
    up_keep, up_send = call(
        functools.partial(up_grad_kernel, here, chips),
        "up_grad",
        [index],
        group_rows + pres,
        [((chips * depth, units), bf16)] * 2,
        flops=chips * product,
        moved=8 * width * units,
    )
    up_theirs = to_core(up_send)
    up_grads = [up_keep, up_theirs]
    for shift in range(1, chips):
        part = slice(shift * depth, (shift + 1) * depth)
        chip_sum = (up_keep[part].astype(f32) + up_theirs[part].astype(f32)).astype(bf16)
        up_grads.append(to_chip(chip_sum, shift))
    down_keep, down_send = call(
        functools.partial(down_grad_kernel, here, chips),
        "down_grad",
        [index],
        hiddens + group_grads,
        [((share, width), bf16)] * 2,
        flops=chips * product,
        moved=8 * width * units,
    )
    down_grads = [down_keep, to_core(down_send)]

    down_next = adam(
        "adam_down", here, index, down_master, down_grads,
        down_mean_code, down_mean_scale, down_square_code, down_square_scale,
    )
    grad_conv, head, tail, conv_terms = call(
        functools.partial(taps_kernel, here),
        "taps",
        [index],
        [place, slope, left, frames, right, returned],
        [((length, width), bf16), ((side, width), bf16), ((side, width), bf16), ((taps, width // 128, 128), f32)],
        after=[down_next[0]],
        scratch=strips,
        flops=2 * slots * length * width,
        moved=8 * slots * width,
    )
    grad_left, grad_right = halo(head, tail)
    conv_total = sum_everywhere(conv_terms)
    (grad_frames,) = call(
        functools.partial(frames_kernel, here),
        "frames",
        [index],
        [grad_left, grad_conv, grad_right, conv_weight, cotangent],
        [((length, width), bf16)],
        scratch=strips,
        flops=2 * slots * length * width,
        moved=4 * slots * width,
    )
    up_next = adam(
        "adam_up", here, index, up_master, up_grads,
        up_mean_code, up_mean_scale, up_square_code, up_square_scale,
    )
    return (grad_frames, conv_total) + up_next + down_next


def solution(mesh):
    frames = P(("dp", "expert"), None)
    shared = P()
    state = P("expert", "dp", None)
    return jax.shard_map(
        body,
        mesh=mesh,
        in_specs=(frames,) * 3 + (shared,) + (state,) * 10,
        out_specs=(frames, shared) + (state,) * 10,
        check_vma=False,
    )
```

time: 209 us -> 149 us (0.71); the launches traced: 205 us -> 148 us
  blocking collectives: 33.3 us -> 11.5 us
  local copies, waits for them, and re-layouts: 17.7 us -> 7.74 us
  waiting for transfers between devices: 39.8 us -> 32.2 us
  Pallas kernels: 59.5 us -> 52.4 us
  starting transfers between devices: 47.3 us -> 41.1 us
  other arithmetic: 6.93 us -> 2.12 us
    all_to_all x1, blocking collectives: 33.3 us -> 11.5 us  [sum_everywhere(): mine = jnp.sum(lax.all_to_all(cells, axes, 0, 0, tiled=True), axis=0)]
    pallas_call x2, Pallas kernels: 28.5 us -> 15.4 us  [adam(): pl.pallas_call(functools.partial(adam_kernel, here, len(grads) - 2), grid...]
    unnamed x63 -> x33, local copies, waits for them, and re-layouts: 16 us -> 6.3 us
    pallas_call x8 -> x10, Pallas kernels: 31 us -> 37 us  [call(): pl.pallas_call(functools.partial(staged, kernel, counts, spans), out_shap...]
    all_to_all x3, waiting for transfers between devices: 16.9 us -> 11.1 us  [by_expert(): lax.all_to_all(cells, 'expert', 0, 0, tiled=True).reshape(slots, width)]
    ppermute x4 -> x5, waiting for transfers between devices: 16.6 us -> 11.5 us  [to_chip(): lax.ppermute(values, 'dp', [(i, (i // 2 + shift) % chips * 2 + i % 2) for...]
    ppermute x5, starting transfers between devices: 4.7 us -> 1.2 us  [to_core(): return lax.ppermute(values, 'dp', [(i, i ^ 1) for i in range(count)])]
    all_to_all x1, starting transfers between devices: 6.04 us -> 2.58 us  [sum_everywhere(): lax.all_to_all(spread, axes, 0, 0, tiled=True).reshape(taps, strips * lanes)]
  transfers between devices with their start and end apart: 17 -> 18, of which waited for: 7 -> 7; matrix products, arithmetic and copies ran while one was open for 5% -> 2% of each run, Pallas kernels for 22% -> 29%
where the time goes in v2:
time: 149 us; the launch traced here: 148 us
  Pallas kernels  52.4 us (35%)
  starting transfers between devices  41.1 us (28%)
  waiting for transfers between devices  32.2 us (22%)
  blocking collectives  11.5 us (8%)
  local copies, waits for them, and re-layouts  7.74 us (5%)
  other arithmetic  2.12 us (1%)
    pallas_call x10, Pallas kernels, call(): pl.pallas_call(functools.partial(staged, kernel, counts, spans), out_shap...  37 us
    all_to_all x3, starting transfers between devices, by_expert(): lax.all_to_all(cells, 'expert', 0, 0, tiled=True).reshape(slots, width)  19 us
    pallas_call x2, Pallas kernels, adam(): pl.pallas_call(functools.partial(adam_kernel, here, len(grads) - 2), grid...  15.4 us
    all_to_all x1, blocking collectives, sum_everywhere(): mine = jnp.sum(lax.all_to_all(cells, axes, 0, 0, tiled=True), axis=0)  11.5 us
    ppermute x5, waiting for transfers between devices, to_chip(): lax.ppermute(values, 'dp', [(i, (i // 2 + shift) % chips * 2 + i % 2) for...  11.5 us
    all_to_all x3, waiting for transfers between devices, by_expert(): lax.all_to_all(cells, 'expert', 0, 0, tiled=True).reshape(slots, width)  11.1 us
    ppermute x4, starting transfers between devices, halo(): return (lax.ppermute(tail, axes, right), lax.ppermute(head, axes, left))  10.7 us
    ppermute x4, waiting for transfers between devices, halo(): return (lax.ppermute(tail, axes, right), lax.ppermute(head, axes, left))  9.62 us
  transfers between devices with their start and end apart: 18, of which 7 were waited for; matrix products, arithmetic and copies ran while one was open for 2% of the time, Pallas kernels for 29%

profile of v2, /device:TPU:0, one launch (start us, length us, event | category | flops | bytes accessed | tf_op | source)
XLA Modules:
  0.0 148.0 jit_solution(18156603027999328185)
XLA Ops:
  0.6 2.5 %cast_far.1.refs_2_.refs_3_ = bf16[256,1024]{1,0:T(8,128)(2,1)} custom-call(s32[1]{0:T(128)} %bitcast.refs_0_.index_ref, f32[256,2048]{1,0:T(8,128)} %bitcast.48), custom_call_target="tpu_custom_call" | custom-call | bytes 6291456 | tf_op jit(solution)/shard_map/cast_far/pallas_call | solution.py:101
  3.1 2.1 %dispatch.1 = (bf16[256,128]{1,0:T(8,128)(2,1)}, bf16[256,1024]{1,0:T(8,128)(2,1)}) custom-call(s32[1,128]{1,0:T(1,128)} %bitcast.71, bf16[128,1024]{1,0:T(8,128)(2,1)} %refs_5_.1, bf16[256,1024]{1,0:T(8,128)(2,1)} %cast_far.1.refs_2_.refs_3_), custom_call_target="tpu_custom_call" | custom-call | flops 67108864 | bytes 1048576 | tf_op jit(solution)/shard_map/dispatch/pallas_call | solution.py:101
  5.2 7.3 %all-to-all-start.1 = ((bf16[8,32,1024]{2,1,0:T(8,128)(2,1)}), bf16[8,32,1024]{2,1,0:T(8,128)(2,1)S(1)}, u32[]{:S(2)}, u32[]{:S(2)}) async-start(bf16[8,32,1024]{2,1,0:T(8,128)(2,1)} %bitcast.63), calls=%async_computation.1 | async-start | bytes 1048576 | tf_op jit(solution)/shard_map/all_to_all | solution.py:394
  12.5 1.5 %collective-permute-start.2 = (bf16[256,1024]{1,0:T(8,128)(2,1)}, bf16[256,1024]{1,0:T(8,128)(2,1)S(1)}, u32[]{:S(2)}, u32[]{:S(2)}) collective-permute-start(bf16[256,1024]{1,0:T(8,128)(2,1)} %cast_far.1.refs_2_.refs_3_), channel_id=1, source_target_pairs={{0,16},{8,24},{16,0},{24,8},{1,17},{9,25},{17,1},{25,9},{2,18},{10... | collective-permute-start | bytes 1572872 | tf_op jit(solution)/shard_map/ppermute | solution.py:400
  14.0 0.8 fusion
  14.8 2.0 %collective-permute-start = (bf16[16,1024]{1,0:T(8,128)(2,1)S(1)}, bf16[16,1024]{1,0:T(8,128)(2,1)S(1)}, u32[]{:S(2)}, u32[]{:S(2)}) collective-permute-start(bf16[16,1024]{1,0:T(8,128)(2,1)S(1)} %get-tuple-element.73), channel_id=1, source_target_pairs={{0,1},{1,2},{2,3},{3,4},{4,5},{5,6},{6,7},{7,8},{8,9},{9,10},{10,1... | collective-permute-start | bytes 98312 | tf_op jit(solution)/shard_map/ppermute | solution.py:415
  16.8 3.3 %collective-permute-start.1 = (bf16[16,1024]{1,0:T(8,128)(2,1)S(1)}, bf16[16,1024]{1,0:T(8,128)(2,1)S(1)}, u32[]{:S(2)}, u32[]{:S(2)}) collective-permute-start(bf16[16,1024]{1,0:T(8,128)(2,1)S(1)} %get-tuple-element.72), channel_id=1, source_target_pairs={{1,0},{2,1},{3,2},{4,3},{5,4},{6,5},{7,6},{8,7},{9,8},{10,9},{11,1... | collective-permute-start | bytes 98312 | tf_op jit(solution)/shard_map/ppermute | solution.py:415
  20.1 6.1 %collective-permute-done.refs_1_.refs_3_ = bf16[16,1024]{1,0:T(8,128)(2,1)S(1)} collective-permute-done((bf16[16,1024]{1,0:T(8,128)(2,1)S(1)}, bf16[16,1024]{1,0:T(8,128)(2,1)S(1)}, u32[]{:S(2)}, u32[]{:S(2)}) %collective-permute-start) | collective-permute-done | bytes 32800 | tf_op jit(solution)/shard_map/ppermute | solution.py:415
  26.2 0.2 collective-permute-done.2.refs_6_.refs_4_
  26.4 0.4 copy-done.12
  26.9 0.4 copy-done.3
  27.2 3.8 %convolve.1 = (f32[128,1024]{1,0:T(8,128)}, bf16[256,1024]{1,0:T(8,128)(2,1)}) custom-call(s32[1]{0:T(128)} %bitcast.refs_0_.index_ref, bf16[16,1024]{1,0:T(8,128)(2,1)} %copy-done.12, bf16[128,1024]{1,0:T(8,128)(2,1)} %refs_4_.4, bf16[16,1024]{1,0:T(8,128)(2,1)} %copy-done.13, f32[32,1024]{1,0:T(8,128)} %refs_4_.5, ...), custom_call_target="tpu_custom_call" | custom-call | flops 67108864 | bytes 2097152 | tf_op jit(solution)/shard_map/convolve/pallas_call | solution.py:101
  31.1 5.7 %all-to-all-start = ((bf16[8,32,1024]{2,1,0:T(8,128)(2,1)}), bf16[8,32,1024]{2,1,0:T(8,128)(2,1)}, u32[]{:S(2)}, u32[]{:S(2)}) async-start(bf16[8,32,1024]{2,1,0:T(8,128)(2,1)} %bitcast.64), calls=%async_computation | async-start | bytes 1048576 | tf_op jit(solution)/shard_map/all_to_all | solution.py:394
  36.8 3.4 %cast_near.1 = (bf16[256,1024]{1,0:T(8,128)(2,1)}, bf16[512,1024]{1,0:T(8,128)(2,1)}) custom-call(s32[1]{0:T(128)} %bitcast.refs_0_.index_ref, f32[256,2048]{1,0:T(8,128)} %bitcast.49, f32[512,1024]{1,0:T(8,128)} %bitcast.51, bf16[256,1024]{1,0:T(8,128)(2,1)} %cast_far.1.refs_2_.refs_3_), custom_call_target="tpu_custom_call" | custom-call | bytes 6291456 | tf_op jit(solution)/shard_map/cast_near/pallas_call | solution.py:101
  40.3 0.5 collective-permute-start.3
  40.8 1.5 %collective-permute-start.7 = (bf16[256,1024]{1,0:T(8,128)(2,1)S(1)}, bf16[256,1024]{1,0:T(8,128)(2,1)S(1)}, u32[]{:S(2)}, u32[]{:S(2)}) collective-permute-start(bf16[256,1024]{1,0:T(8,128)(2,1)S(1)} %bitcast.60), channel_id=1, source_target_pairs={{0,16},{8,24},{16,0},{24,8},{1,17},{9,25},{17,1},{25,9},{2,18},{10... | collective-permute-start | bytes 1572872 | tf_op jit(solution)/shard_map/ppermute | solution.py:400
  42.4 8.0 %all-to-all-done = bf16[8,32,1024]{2,1,0:T(8,128)(2,1)} async-done(((bf16[8,32,1024]{2,1,0:T(8,128)(2,1)}), bf16[8,32,1024]{2,1,0:T(8,128)(2,1)}, u32[]{:S(2)}, u32[]{:S(2)}) %all-to-all-start) | async-done | bytes 524320 | tf_op jit(solution)/shard_map/all_to_all | solution.py:394
  50.3 1.5 %collective-permute-start.6 = (bf16[256,1024]{1,0:T(8,128)(2,1)}, bf16[256,1024]{1,0:T(8,128)(2,1)S(1)}, u32[]{:S(2)}, u32[]{:S(2)}) collective-permute-start(bf16[256,1024]{1,0:T(8,128)(2,1)} %bitcast.4.refs_1_), channel_id=1, source_target_pairs={{0,16},{8,24},{16,0},{24,8},{1,17},{9,25},{17,1},{25,9},{2,18},{10... | collective-permute-start | bytes 1572872 | tf_op jit(solution)/shard_map/ppermute | solution.py:400
  51.9 0.8 copy-done.8
  52.6 1.0 copy-done.6
  53.6 5.2 %own_group.1 = (bf16[256,1024]{1,0:T(8,128)(2,1)}, bf16[256,1024]{1,0:T(8,128)(2,1)}, f32[256,1024]{1,0:T(8,128)}) custom-call(s32[1]{0:T(128)} %bitcast.refs_0_.index_ref, bf16[256,1024]{1,0:T(8,128)(2,1)} %bitcast.4.refs_1_, bf16[256,1024]{1,0:T(8,128)(2,1)} %get-tuple-element.45.refs_2_, bf16[256,1024]{1,0:T(8,128)(2,1)} %copy-done.8, ...), custom_call_target="tpu_custom_call" | custom-call | flops 1610612736 | bytes 8388608 | tf_op jit(solution)/shard_map/own_group/pallas_call | solution.py:101
  58.9 7.5 %collective-permute-done.6.refs_1_.refs_2_ = bf16[256,1024]{1,0:T(8,128)(2,1)S(1)} collective-permute-done((bf16[256,1024]{1,0:T(8,128)(2,1)}, bf16[256,1024]{1,0:T(8,128)(2,1)S(1)}, u32[]{:S(2)}, u32[]{:S(2)}) %collective-permute-start.6) | collective-permute-done | bytes 524320 | tf_op jit(solution)/shard_map/ppermute | solution.py:400
  66.4 0.8 copy-done.9
  67.2 5.1 %far_group.1 = (bf16[256,1024]{1,0:T(8,128)(2,1)}, bf16[256,1024]{1,0:T(8,128)(2,1)}, bf16[256,1024]{1,0:T(8,128)(2,1)}) custom-call(s32[1]{0:T(128)} %bitcast.refs_0_.index_ref, bf16[256,1024]{1,0:T(8,128)(2,1)} %copy-done.9, bf16[256,1024]{1,0:T(8,128)(2,1)} %get-tuple-element.45.refs_2_, bf16[256,1024]{1,0:T(8,128)(2,1)} %copy-done.8, ...), custom_call_target="tpu_custom_call" | custom-call | flops 1610612736 | bytes 8388608 | tf_op jit(solution)/shard_map/far_group/pallas_call | solution.py:101
  72.3 1.6 %collective-permute-start.8 = (bf16[256,1024]{1,0:T(8,128)(2,1)}, bf16[256,1024]{1,0:T(8,128)(2,1)S(1)}, u32[]{:S(2)}, u32[]{:S(2)}) collective-permute-start(bf16[256,1024]{1,0:T(8,128)(2,1)} %get-tuple-element.49), channel_id=1, source_target_pairs={{0,16},{8,24},{16,0},{24,8},{1,17},{9,25},{17,1},{25,9},{2,18},{10... | collective-permute-start | bytes 1572872 | tf_op jit(solution)/shard_map/ppermute | solution.py:400
  73.8 3.9 %up_grad.1 = (bf16[512,1024]{1,0:T(8,128)(2,1)}, bf16[512,1024]{1,0:T(8,128)(2,1)}) custom-call(s32[1]{0:T(128)} %bitcast.refs_0_.index_ref, bf16[256,1024]{1,0:T(8,128)(2,1)} %bitcast.4.refs_1_, bf16[256,1024]{1,0:T(8,128)(2,1)} %copy-done.9, bf16[256,1024]{1,0:T(8,128)(2,1)} %get-tuple-element.59.refs_3_, bf16[256,1024]{1,0:T(8,128)(2,1)} %get-tuple-element.60.refs_4_), custom_call_target="tpu_custom_call" | custom-call | flops 1073741824 | bytes 8388608 | tf_op jit(solution)/shard_map/up_grad/pallas_call | solution.py:101
  77.8 3.9 %down_grad.1 = (bf16[512,1024]{1,0:T(8,128)(2,1)}, bf16[512,1024]{1,0:T(8,128)(2,1)}) custom-call(s32[1]{0:T(128)} %bitcast.refs_0_.index_ref, bf16[256,1024]{1,0:T(8,128)(2,1)} %get-tuple-element.50.refs_1_, bf16[256,1024]{1,0:T(8,128)(2,1)} %get-tuple-element.51.refs_2_, bf16[256,1024]{1,0:T(8,128)(2,1)} %bitcast.62, bf16[256,1024]{1,0:T(8,128)(2,1)} %copy-done.7), custom_call_target="tpu_custom_call" | custom-call | flops 1073741824 | bytes 8388608 | tf_op jit(solution)/shard_map/down_grad/pallas_call | solution.py:101
  81.7 0.5 collective-permute-start.9
  82.2 3.8 %collective-permute-done.8 = bf16[256,1024]{1,0:T(8,128)(2,1)S(1)} collective-permute-done((bf16[256,1024]{1,0:T(8,128)(2,1)}, bf16[256,1024]{1,0:T(8,128)(2,1)S(1)}, u32[]{:S(2)}, u32[]{:S(2)}) %collective-permute-start.8) | collective-permute-done | bytes 524320 | tf_op jit(solution)/shard_map/ppermute | solution.py:400
  86.0 1.0 add_convert_fusion.1
  87.0 6.0 %all-to-all-start.2 = ((bf16[8,32,1024]{2,1,0:T(8,128)(2,1)}), bf16[8,32,1024]{2,1,0:T(8,128)(2,1)S(1)}, u32[]{:S(2)}, u32[]{:S(2)}) async-start(bf16[8,32,1024]{2,1,0:T(8,128)(2,1)} %bitcast.8), calls=%async_computation.2 | async-start | bytes 1048576 | tf_op jit(solution)/shard_map/all_to_all | solution.py:394
  93.0 1.1 add_convert_fusion
  94.1 1.5 %collective-permute-start.13 = (bf16[256,1024]{1,0:T(8,128)(2,1)}, bf16[256,1024]{1,0:T(8,128)(2,1)S(1)}, u32[]{:S(2)}, u32[]{:S(2)}) collective-permute-start(bf16[256,1024]{1,0:T(8,128)(2,1)} %add_convert_fusion), channel_id=1, source_target_pairs={{0,16},{8,24},{16,0},{24,8},{1,17},{9,25},{17,1},{25,9},{2,18},{10... | collective-permute-start | bytes 1572872 | tf_op jit(solution)/shard_map/ppermute | solution.py:400
  95.7 7.6 %adam_down.1 = (f32[512,1024]{1,0:T(8,128)}, bf16[512,1024]{1,0:T(8,128)(2,1)}, f32[8,512]{1,0:T(8,128)}, bf16[512,1024]{1,0:T(8,128)(2,1)}, f32[8,512]{1,0:T(8,128)}) custom-call(s32[1]{0:T(128)} %bitcast.refs_0_.index_ref, f32[512,1024]{1,0:T(8,128)} %bitcast.52, bf16[512,1024]{1,0:T(8,128)(2,1)} %bitcast.56, f32[8,512]{1,0:T(8,128)} %bitcast.67, ...), custom_call_target="tpu_custom_call" | custom-call | flops 10485760 | bytes 10485760 | tf_op jit(solution)/shard_map/adam_down/pallas_call | solution.py:367
  103.3 3.1 %all-to-all-done.2 = bf16[8,32,1024]{2,1,0:T(8,128)(2,1)S(1)} async-done(((bf16[8,32,1024]{2,1,0:T(8,128)(2,1)}), bf16[8,32,1024]{2,1,0:T(8,128)(2,1)S(1)}, u32[]{:S(2)}, u32[]{:S(2)}) %all-to-all-start.2) | async-done | bytes 524320 | tf_op jit(solution)/shard_map/all_to_all | solution.py:394
  106.4 0.8 copy-done.5
  107.2 3.8 %taps.1 = (bf16[128,1024]{1,0:T(8,128)(2,1)}, bf16[16,1024]{1,0:T(8,128)(2,1)}, bf16[16,1024]{1,0:T(8,128)(2,1)}, f32[32,8,128]{2,1,0:T(8,128)}) custom-call(s32[1]{0:T(128)} %bitcast.refs_0_.index_ref, bf16[256,128]{1,0:T(8,128)(2,1)} %get-tuple-element.42.refs_5_.refs_1_, f32[128,1024]{1,0:T(8,128)} %get-tuple-element.43.refs_2_, ...), custom_call_target="tpu_custom_call" | custom-call | flops 67108864 | bytes 2097152 | tf_op jit(solution)/shard_map/taps/pallas_call | solution.py:101
  111.0 11.5 %all_to_all.25 = f32[32,8,128]{2,1,0:T(8,128)S(1)} all-to-all(f32[32,8,128]{2,1,0:T(8,128)} %get-tuple-element.58), channel_id=1, replica_groups=mesh['dp'=4,'expert'=8] {'dp','expert'}, dimensions={0} | all-to-all | bytes 262144 | tf_op jit(solution)/shard_map/all_to_all | solution.py:423
  122.5 0.7 broadcast_in_dim.37
  123.2 2.6 %all-to-all-start.4 = ((f32[32,8,128]{2,1,0:T(8,128)}), f32[32,8,128]{2,1,0:T(8,128)S(1)}, u32[]{:S(2)}, u32[]{:S(2)}) async-start(f32[32,8,128]{2,1,0:T(8,128)} %broadcast_in_dim.37), calls=%async_computation.4 | async-start | bytes 262144 | tf_op jit(solution)/shard_map/all_to_all | solution.py:425
  125.7 1.7 %collective-permute-start.10 = (bf16[16,1024]{1,0:T(8,128)(2,1)}, bf16[16,1024]{1,0:T(8,128)(2,1)S(1)}, u32[]{:S(2)}, u32[]{:S(2)}) collective-permute-start(bf16[16,1024]{1,0:T(8,128)(2,1)} %get-tuple-element.55), channel_id=1, source_target_pairs={{0,1},{1,2},{2,3},{3,4},{4,5},{5,6},{6,7},{7,8},{8,9},{9,10},{10,1... | collective-permute-start | bytes 98312 | tf_op jit(solution)/shard_map/ppermute | solution.py:415
  127.4 3.7 %collective-permute-start.11 = (bf16[16,1024]{1,0:T(8,128)(2,1)}, bf16[16,1024]{1,0:T(8,128)(2,1)S(1)}, u32[]{:S(2)}, u32[]{:S(2)}) collective-permute-start(bf16[16,1024]{1,0:T(8,128)(2,1)} %get-tuple-element.57), channel_id=1, source_target_pairs={{1,0},{2,1},{3,2},{4,3},{5,4},{6,5},{7,6},{8,7},{9,8},{10,9},{11,1... | collective-permute-start | bytes 98312 | tf_op jit(solution)/shard_map/ppermute | solution.py:415
  131.1 3.5 %collective-permute-done.10.refs_1_ = bf16[16,1024]{1,0:T(8,128)(2,1)S(1)} collective-permute-done((bf16[16,1024]{1,0:T(8,128)(2,1)}, bf16[16,1024]{1,0:T(8,128)(2,1)S(1)}, u32[]{:S(2)}, u32[]{:S(2)}) %collective-permute-start.10) | collective-permute-done | bytes 32800 | tf_op jit(solution)/shard_map/ppermute | solution.py:415
  134.6 0.6 copy-done.14
  135.3 3.4 %frames.1 = bf16[128,1024]{1,0:T(8,128)(2,1)} custom-call(s32[1]{0:T(128)} %bitcast.refs_0_.index_ref, bf16[16,1024]{1,0:T(8,128)(2,1)} %copy-done.14, bf16[128,1024]{1,0:T(8,128)(2,1)} %get-tuple-element.56.refs_2_, bf16[16,1024]{1,0:T(8,128)(2,1)} %copy-done.15, f32[32,1024]{1,0:T(8,128)} %refs_4_.5, bf16[128,1024]{1,0:T(8,128)(2,1)} %refs_5_.1), custom_call_target="tpu_custom_call" | custom-call | flops 67108864 | bytes 1048576 | tf_op jit(solution)/shard_map/frames/pallas_call | solution.py:101
  138.7 0.8 copy-done.11
  139.5 7.8 %adam_up.1 = (f32[256,2048]{1,0:T(8,128)}, bf16[256,2048]{1,0:T(8,128)(2,1)}, f32[16,256]{1,0:T(8,128)}, bf16[256,2048]{1,0:T(8,128)(2,1)}, f32[16,256]{1,0:T(8,128)}) custom-call(s32[1]{0:T(128)} %bitcast.refs_0_.index_ref, f32[256,2048]{1,0:T(8,128)} %bitcast.50, bf16[256,2048]{1,0:T(8,128)(2,1)} %bitcast.58, f32[16,256]{1,0:T(8,128)} %bitcast.69, ...), custom_call_target="tpu_custom_call" | custom-call | flops 10485760 | bytes 11534336 | tf_op jit(solution)/shard_map/adam_up/pallas_call | solution.py:367
  147.3 0.7 copy.28
  (39 shorter events, 0.4 us)
Async XLA Ops:
  5.2 25.8 %all-to-all-start.1 = ((bf16[8,32,1024]{2,1,0:T(8,128)(2,1)}), bf16[8,32,1024]{2,1,0:T(8,128)(2,1)S(1)}, u32[]{:S(2)}, u32[]{:S(2)}) async-start(bf16[8,32,1024]{2,1,0:T(8,128)(2,1)} %bitcast.63), calls=%async_computation.1 | async-start | bytes 1048576 | tf_op jit(solution)/shard_map/all_to_all | solution.py:394
  12.5 13.9 %collective-permute-start.2 = (bf16[256,1024]{1,0:T(8,128)(2,1)}, bf16[256,1024]{1,0:T(8,128)(2,1)S(1)}, u32[]{:S(2)}, u32[]{:S(2)}) collective-permute-start(bf16[256,1024]{1,0:T(8,128)(2,1)} %cast_far.1.refs_2_.refs_3_), channel_id=1, source_target_pairs={{0,16},{8,24},{16,0},{24,8},{1,17},{9,25},{17,1},{25,9},{2,18},{10... | collective-permute-start | bytes 1572872 | tf_op jit(solution)/shard_map/ppermute | solution.py:400
  14.8 11.5 %collective-permute-start = (bf16[16,1024]{1,0:T(8,128)(2,1)S(1)}, bf16[16,1024]{1,0:T(8,128)(2,1)S(1)}, u32[]{:S(2)}, u32[]{:S(2)}) collective-permute-start(bf16[16,1024]{1,0:T(8,128)(2,1)S(1)} %get-tuple-element.73), channel_id=1, source_target_pairs={{0,1},{1,2},{2,3},{3,4},{4,5},{5,6},{6,7},{7,8},{8,9},{9,10},{10,1... | collective-permute-start | bytes 98312 | tf_op jit(solution)/shard_map/ppermute | solution.py:415
  16.8 9.4 %collective-permute-start.1 = (bf16[16,1024]{1,0:T(8,128)(2,1)S(1)}, bf16[16,1024]{1,0:T(8,128)(2,1)S(1)}, u32[]{:S(2)}, u32[]{:S(2)}) collective-permute-start(bf16[16,1024]{1,0:T(8,128)(2,1)S(1)} %get-tuple-element.72), channel_id=1, source_target_pairs={{1,0},{2,1},{3,2},{4,3},{5,4},{6,5},{7,6},{8,7},{9,8},{10,9},{11,1... | collective-permute-start | bytes 98312 | tf_op jit(solution)/shard_map/ppermute | solution.py:415
  26.2 0.6 copy-start.12
  26.2 0.6 copy-start.13
  26.4 0.8 copy-start.3
  31.0 9.8 %copy-start.10 = (bf16[8,32,1024]{2,1,0:T(8,128)(2,1)}, bf16[8,32,1024]{2,1,0:T(8,128)(2,1)S(1)}, u32[]{:S(2)}) copy-start(bf16[8,32,1024]{2,1,0:T(8,128)(2,1)S(1)} %all-to-all-done.1) | copy-start | bytes 1572868
  31.1 19.3 %all-to-all-start = ((bf16[8,32,1024]{2,1,0:T(8,128)(2,1)}), bf16[8,32,1024]{2,1,0:T(8,128)(2,1)}, u32[]{:S(2)}, u32[]{:S(2)}) async-start(bf16[8,32,1024]{2,1,0:T(8,128)(2,1)} %bitcast.64), calls=%async_computation | async-start | bytes 1048576 | tf_op jit(solution)/shard_map/all_to_all | solution.py:394
  36.8 4.0 %copy-start.4 = (bf16[256,1024]{1,0:T(8,128)(2,1)S(1)}, bf16[256,1024]{1,0:T(8,128)(2,1)}, u32[]{:S(2)}) copy-start(bf16[256,1024]{1,0:T(8,128)(2,1)} %copy-done.3) | copy-start | bytes 1572868
  40.2 11.7 %collective-permute-start.5 = (bf16[512,1024]{1,0:T(8,128)(2,1)}, bf16[512,1024]{1,0:T(8,128)(2,1)S(1)}, u32[]{:S(2)}, u32[]{:S(2)}) collective-permute-start(bf16[512,1024]{1,0:T(8,128)(2,1)} %get-tuple-element.47.refs_7_), channel_id=1, source_target_pairs={{0,8},{8,0},{16,24},{24,16},{1,9},{9,1},{17,25},{25,17},{2,10},{10... | collective-permute-start | bytes 3145736 | tf_op jit(solution)/shard_map/ppermute | solution.py:407
  40.3 11.6 %collective-permute-start.3 = (bf16[256,1024]{1,0:T(8,128)(2,1)}, bf16[256,1024]{1,0:T(8,128)(2,1)S(1)}, u32[]{:S(2)}, u32[]{:S(2)}) collective-permute-start(bf16[256,1024]{1,0:T(8,128)(2,1)} %get-tuple-element.45.refs_2_), channel_id=1, source_target_pairs={{0,8},{8,0},{16,24},{24,16},{1,9},{9,1},{17,25},{25,17},{2,10},{10... | collective-permute-start | bytes 1572872 | tf_op jit(solution)/shard_map/ppermute | solution.py:407
  40.8 11.1 %collective-permute-start.4 = (bf16[256,1024]{1,0:T(8,128)(2,1)S(1)}, bf16[256,1024]{1,0:T(8,128)(2,1)}, u32[]{:S(2)}, u32[]{:S(2)}) collective-permute-start(bf16[256,1024]{1,0:T(8,128)(2,1)S(1)} %copy-done.4), channel_id=1, source_target_pairs={{0,8},{8,0},{16,24},{24,16},{1,9},{9,1},{17,25},{25,17},{2,10},{10... | collective-permute-start | bytes 1572872 | tf_op jit(solution)/shard_map/ppermute | solution.py:407
  40.8 18.0 %collective-permute-start.7 = (bf16[256,1024]{1,0:T(8,128)(2,1)S(1)}, bf16[256,1024]{1,0:T(8,128)(2,1)S(1)}, u32[]{:S(2)}, u32[]{:S(2)}) collective-permute-start(bf16[256,1024]{1,0:T(8,128)(2,1)S(1)} %bitcast.60), channel_id=1, source_target_pairs={{0,16},{8,24},{16,0},{24,8},{1,17},{9,25},{17,1},{25,9},{2,18},{10... | collective-permute-start | bytes 1572872 | tf_op jit(solution)/shard_map/ppermute | solution.py:400
  50.3 16.0 %collective-permute-start.6 = (bf16[256,1024]{1,0:T(8,128)(2,1)}, bf16[256,1024]{1,0:T(8,128)(2,1)S(1)}, u32[]{:S(2)}, u32[]{:S(2)}) collective-permute-start(bf16[256,1024]{1,0:T(8,128)(2,1)} %bitcast.4.refs_1_), channel_id=1, source_target_pairs={{0,16},{8,24},{16,0},{24,8},{1,17},{9,25},{17,1},{25,9},{2,18},{10... | collective-permute-start | bytes 1572872 | tf_op jit(solution)/shard_map/ppermute | solution.py:400
  51.8 0.8 copy-start.8
  52.6 1.0 copy-start.6
  58.9 7.5 %copy-start.7 = (bf16[256,1024]{1,0:T(8,128)(2,1)}, bf16[256,1024]{1,0:T(8,128)(2,1)S(1)}, u32[]{:S(2)}) copy-start(bf16[256,1024]{1,0:T(8,128)(2,1)S(1)} %collective-permute-done.7.refs_6_.refs_4_) | copy-start | bytes 1572868
  66.4 0.8 copy-start.9
  72.3 13.8 %collective-permute-start.8 = (bf16[256,1024]{1,0:T(8,128)(2,1)}, bf16[256,1024]{1,0:T(8,128)(2,1)S(1)}, u32[]{:S(2)}, u32[]{:S(2)}) collective-permute-start(bf16[256,1024]{1,0:T(8,128)(2,1)} %get-tuple-element.49), channel_id=1, source_target_pairs={{0,16},{8,24},{16,0},{24,8},{1,17},{9,25},{17,1},{25,9},{2,18},{10... | collective-permute-start | bytes 1572872 | tf_op jit(solution)/shard_map/ppermute | solution.py:400
  77.7 8.3 %copy-start = (f32[256,1024]{1,0:T(8,128)S(1)}, f32[256,1024]{1,0:T(8,128)}, u32[]{:S(2)}) copy-start(f32[256,1024]{1,0:T(8,128)} %get-tuple-element.48.refs_9_) | copy-start | bytes 3145732
  77.7 15.2 %collective-permute-start.12 = (bf16[512,1024]{1,0:T(8,128)(2,1)}, bf16[512,1024]{1,0:T(8,128)(2,1)S(1)}, u32[]{:S(2)}, u32[]{:S(2)}) collective-permute-start(bf16[512,1024]{1,0:T(8,128)(2,1)} %get-tuple-element.62), channel_id=1, source_target_pairs={{0,8},{8,0},{16,24},{24,16},{1,9},{9,1},{17,25},{25,17},{2,10},{10... | collective-permute-start | bytes 3145736 | tf_op jit(solution)/shard_map/ppermute | solution.py:407
  81.7 11.3 %copy-start.1 = (bf16[512,1024]{1,0:T(8,128)(2,1)S(1)}, bf16[512,1024]{1,0:T(8,128)(2,1)}, u32[]{:S(2)}) copy-start(bf16[512,1024]{1,0:T(8,128)(2,1)} %get-tuple-element.61.refs_0_) | copy-start | bytes 3145732
  81.7 13.9 %collective-permute-start.9 = (bf16[512,1024]{1,0:T(8,128)(2,1)}, bf16[512,1024]{1,0:T(8,128)(2,1)}, u32[]{:S(2)}, u32[]{:S(2)}) collective-permute-start(bf16[512,1024]{1,0:T(8,128)(2,1)} %get-tuple-element.53), channel_id=1, source_target_pairs={{0,8},{8,0},{16,24},{24,16},{1,9},{9,1},{17,25},{25,17},{2,10},{10... | collective-permute-start | bytes 3145736 | tf_op jit(solution)/shard_map/ppermute | solution.py:407
  87.0 19.4 %all-to-all-start.2 = ((bf16[8,32,1024]{2,1,0:T(8,128)(2,1)}), bf16[8,32,1024]{2,1,0:T(8,128)(2,1)S(1)}, u32[]{:S(2)}, u32[]{:S(2)}) async-start(bf16[8,32,1024]{2,1,0:T(8,128)(2,1)} %bitcast.8), calls=%async_computation.2 | async-start | bytes 1048576 | tf_op jit(solution)/shard_map/all_to_all | solution.py:394
  93.0 10.3 %copy-start.2 = (bf16[512,1024]{1,0:T(8,128)(2,1)}, bf16[512,1024]{1,0:T(8,128)(2,1)S(1)}, u32[]{:S(2)}) copy-start(bf16[512,1024]{1,0:T(8,128)(2,1)S(1)} %collective-permute-done.12.refs_1_) | copy-start | bytes 3145732
  94.1 44.6 %collective-permute-start.13 = (bf16[256,1024]{1,0:T(8,128)(2,1)}, bf16[256,1024]{1,0:T(8,128)(2,1)S(1)}, u32[]{:S(2)}, u32[]{:S(2)}) collective-permute-start(bf16[256,1024]{1,0:T(8,128)(2,1)} %add_convert_fusion), channel_id=1, source_target_pairs={{0,16},{8,24},{16,0},{24,8},{1,17},{9,25},{17,1},{25,9},{2,18},{10... | collective-permute-start | bytes 1572872 | tf_op jit(solution)/shard_map/ppermute | solution.py:400
  106.4 0.8 copy-start.5
  123.2 24.1 %all-to-all-start.4 = ((f32[32,8,128]{2,1,0:T(8,128)}), f32[32,8,128]{2,1,0:T(8,128)S(1)}, u32[]{:S(2)}, u32[]{:S(2)}) async-start(f32[32,8,128]{2,1,0:T(8,128)} %broadcast_in_dim.37), calls=%async_computation.4 | async-start | bytes 262144 | tf_op jit(solution)/shard_map/all_to_all | solution.py:425
  125.7 8.9 %collective-permute-start.10 = (bf16[16,1024]{1,0:T(8,128)(2,1)}, bf16[16,1024]{1,0:T(8,128)(2,1)S(1)}, u32[]{:S(2)}, u32[]{:S(2)}) collective-permute-start(bf16[16,1024]{1,0:T(8,128)(2,1)} %get-tuple-element.55), channel_id=1, source_target_pairs={{0,1},{1,2},{2,3},{3,4},{4,5},{5,6},{6,7},{7,8},{8,9},{9,10},{10,1... | collective-permute-start | bytes 98312 | tf_op jit(solution)/shard_map/ppermute | solution.py:415
  127.4 7.2 %collective-permute-start.11 = (bf16[16,1024]{1,0:T(8,128)(2,1)}, bf16[16,1024]{1,0:T(8,128)(2,1)S(1)}, u32[]{:S(2)}, u32[]{:S(2)}) collective-permute-start(bf16[16,1024]{1,0:T(8,128)(2,1)} %get-tuple-element.57), channel_id=1, source_target_pairs={{1,0},{2,1},{3,2},{4,3},{5,4},{6,5},{7,6},{8,7},{9,8},{10,9},{11,1... | collective-permute-start | bytes 98312 | tf_op jit(solution)/shard_map/ppermute | solution.py:415
  134.6 0.6 copy-start.14
  134.6 0.6 copy-start.15
  138.7 0.8 copy-start.11

commit v3 on v2

--- a/solution.py
+++ b/solution.py
@@ -1,4 +1,5 @@
 import functools
+import math
 
 import jax
 import jax.numpy as jnp
@@ -55,7 +56,7 @@
     for count in counts:
         groups.append(refs[:count])
         refs = refs[count:]
-    scalars, sources, _, targets, held, made, scratch = groups
+    scalars, resident, sources, _, targets, held, made, scratch = groups
     in_sems, out_sems = refs
     arriving = []
     for index, source in enumerate(sources):
@@ -76,7 +77,7 @@
         leaving[index] = pltpu.make_async_copy(made[index], targets[index], out_sems.at[index])
         leaving[index].start()
 
-    kernel(scalars, take, made, give, scratch)
+    kernel(scalars + resident, take, made, give, scratch)
     for index in range(len(targets)):
         if index not in leaving:
             give(index)
@@ -86,8 +87,9 @@
         copy.wait()
 
 
-def call(kernel, name, scalars, inputs, outs, scratch=(), after=(), flops=0, moved=0, limit=60):
-    hbm = pl.BlockSpec(memory_space=pltpu.HBM)
+def call(kernel, name, scalars, inputs, outs, scratch=(), after=(), resident=(), flops=0, moved=0, limit=60):
+    hbm = pl.BlockSpec(memory_space=pl.ANY)
+    vmem = pl.BlockSpec(memory_space=pltpu.VMEM)
     smem = pl.BlockSpec(memory_space=pltpu.SMEM)
     pairs = [item if isinstance(item, tuple) else (item, None) for item in inputs]
     arrays = [array for array, _ in pairs]
@@ -97,11 +99,15 @@
         for array, span in pairs
     ]
     made = [pltpu.VMEM(shape, kind) for shape, kind in outs]
-    counts = (len(scalars), len(arrays), len(after), len(outs), len(held), len(made), len(scratch))
+    counts = (
+        len(scalars), len(resident), len(arrays), len(after), len(outs), len(held), len(made), len(scratch)
+    )
     return pl.pallas_call(
         functools.partial(staged, kernel, counts, spans),
         out_shape=[jax.ShapeDtypeStruct(shape, kind) for shape, kind in outs],
-        in_specs=[smem] * len(scalars) + [hbm] * (len(arrays) + len(after)),
+        in_specs=[smem] * len(scalars)
+        + [vmem] * len(resident)
+        + [hbm] * (len(arrays) + len(after)),
         out_specs=[hbm] * len(outs),
         scratch_shapes=held
         + made
@@ -110,13 +116,19 @@
         compiler_params=pltpu.CompilerParams(vmem_limit_bytes=limit * MIB),
         cost_estimate=pl.CostEstimate(flops=flops, bytes_accessed=moved, transcendentals=0),
         name=name,
-    )(*scalars, *arrays, *after)
-
-
-def dispatch_kernel(experts, capacity, scalars, take, made, give, scratch):
-    place_ref, out_ref = made
+    )(*scalars, *resident, *arrays, *after)
+
+
+def prepare_kernel(here, experts, capacity, scalars, take, made, give, scratch):
+    head_ref, tail_ref, place_ref, out_ref, *up_refs = made
+    place = here(scalars[0])
+    side, length = head_ref.shape[0], place_ref.shape[1]
+    frames_ref = take(2)
+    head_ref[...] = frames_ref[:side, :]
+    give(0)
+    tail_ref[...] = frames_ref[length - side :, :]
+    give(1)
     ids = take(0)[...]
-    length = ids.shape[1]
     rows = lax.broadcasted_iota(jnp.int32, (experts, length), 0)
     one_hot = (rows == ids).astype(f32)
     earlier = lax.broadcasted_iota(jnp.int32, (length, length), 0)
@@ -125,9 +137,15 @@
     slot = jnp.sum(ranks * one_hot, axis=0, keepdims=True).astype(jnp.int32)
     position = ids * capacity + slot
     slots = lax.broadcasted_iota(jnp.int32, (experts * capacity, length), 0)
-    place = (slots == position).astype(f32).astype(bf16)
-    place_ref[...] = place
-    out_ref[...] = jnp.dot(place, take(1)[...], preferred_element_type=f32).astype(bf16)
+    spots = (slots == position).astype(f32).astype(bf16)
+    place_ref[...] = spots
+    give(2)
+    out_ref[...] = jnp.dot(spots, take(1)[...], preferred_element_type=f32).astype(bf16)
+    give(3)
+    units = up_refs[0].shape[1] if up_refs else 0
+    for index, up_ref in enumerate(up_refs):
+        up_ref[...] = take(3)[:, at(place.goes[index + 1], units)].astype(bf16)
+        give(4 + index)
 
 
 def fill_padded(pad_ref, place, left, middle, right, cols):
@@ -175,7 +193,7 @@
     out_ref[...] = jnp.dot(take(4)[...], feat_ref[...], preferred_element_type=f32).astype(bf16)
 
 
-def group_kernel(here, scalars, take, made, give, scratch):
+def group_kernel(here, others, scalars, take, made, give, scratch):
     hidden_ref, pre_ref, part_ref = made
     (slope_ref,) = scratch
     place = here(scalars[0])
@@ -207,8 +225,14 @@
         pre_ref[:, cols] = (back * slope_ref[:, cols]).astype(bf16)
     give(1)
     pre = pre_ref[...]
+    spot = slice(None)
+    if others:
+        slots = rows_ref.shape[0]
+        spot = at(place.came[others], slots)
+        for turn in range(others):
+            part_ref[at(place.came[turn], slots), :] = take(4 + len(up_refs) + turn)[...]
     for shard, up_ref in zip(place.shards, up_refs):
-        part_ref[:, at(shard, depth)] = along(pre, up_ref[...]).astype(part_ref.dtype)
+        part_ref[spot, at(shard, depth)] = along(pre, up_ref[...]).astype(bf16)
 
 
 def up_grad_kernel(here, groups, scalars, take, made, give, scratch):
@@ -216,7 +240,7 @@
     place = here(scalars[0])
     row_refs = [take(group) for group in range(groups)]
     pres = [take(groups + group)[...] for group in range(groups)]
-    depth = keep_ref.shape[0] // groups
+    depth = keep_ref.shape[0] // len(place.goes)
     for out_ref, core in ((send_ref, 1 - place.core), (keep_ref, place.core)):
         for index, chip in enumerate(place.goes):
             total = 0.0
@@ -240,14 +264,6 @@
         give(0 if out_ref is keep_ref else 1)
 
 
-def cast_far_kernel(here, scalars, take, made, give, scratch):
-    place = here(scalars[0])
-    units = made[0].shape[1]
-    for index, up_ref in enumerate(made):
-        up_ref[...] = take(0)[:, at(place.goes[index + 1], units)].astype(bf16)
-        give(index)
-
-
 def cast_near_kernel(here, scalars, take, made, give, scratch):
     place = here(scalars[0])
     up_ref, down_ref = made
@@ -262,7 +278,12 @@
     place = here(scalars[0])
     length, width = grad_ref.shape
     side = head_ref.shape[0]
-    features = across(take(0)[...], take(5)[...]).astype(bf16).astype(f32)
+    spots, back_ref = take(0)[...], take(5)
+    slots = spots.shape[0]
+    features = 0.0
+    for chip in range(back_ref.shape[0] // slots):
+        features = features + across(spots, back_ref[chip * slots : (chip + 1) * slots, :])
+    features = features.astype(bf16).astype(f32)
     grad = (features * take(1)[...]).astype(bf16)
     grad_ref[...] = grad
     head_ref[...] = grad[:side]
@@ -301,6 +322,11 @@
         return carry
 
     lax.fori_loop(0, width // 128, lanes, 0)
+
+
+def spread_kernel(scalars, take, made, give, scratch):
+    total = jnp.sum(take(0)[...], axis=0, keepdims=True)
+    made[0][...] = jnp.broadcast_to(total, made[0].shape)
 
 
 def adam_kernel(
@@ -394,34 +420,37 @@
     return lax.all_to_all(cells, "expert", 0, 0, tiled=True).reshape(slots, width)
 
 
+def to_senders(rows):
+    axes = ("chip", "expert")
+    count = lax.axis_size("chip") * lax.axis_size("expert")
+    cells = rows.reshape(count, rows.shape[0] // count, rows.shape[1])
+    return lax.all_to_all(cells, axes, 0, 0, tiled=True).reshape(rows.shape)
+
+
 def to_chip(values, shift):
-    count = lax.axis_size("dp")
-    chips = count // 2
-    return lax.ppermute(
-        values, "dp", [(i, (i // 2 + shift) % chips * 2 + i % 2) for i in range(count)]
-    )
+    chips = lax.axis_size("chip")
+    return lax.ppermute(values, "chip", [(i, (i + shift) % chips) for i in range(chips)])
 
 
 def to_core(values):
-    count = lax.axis_size("dp")
-    return lax.ppermute(values, "dp", [(i, i ^ 1) for i in range(count)])
+    return lax.ppermute(values, "core", [(0, 1), (1, 0)])
 
 
 def halo(head, tail):
-    axes = ("dp", "expert")
-    count = lax.axis_size("dp") * lax.axis_size("expert")
+    axes = ("chip", "core", "expert")
+    count = math.prod(lax.axis_size(axis) for axis in axes)
     right = [(i, (i + 1) % count) for i in range(count)]
     left = [((i + 1) % count, i) for i in range(count)]
     return lax.ppermute(tail, axes, right), lax.ppermute(head, axes, left)
 
 
-def sum_everywhere(terms):
-    axes = ("dp", "expert")
-    count = lax.axis_size("dp") * lax.axis_size("expert")
+def sum_everywhere(terms, after):
+    axes = ("chip", "core", "expert")
+    count = math.prod(lax.axis_size(axis) for axis in axes)
     taps, strips, lanes = terms.shape
     cells = terms.reshape(count, taps * strips // count, lanes)
-    mine = jnp.sum(lax.all_to_all(cells, axes, 0, 0, tiled=True), axis=0)
-    spread = jnp.broadcast_to(mine[None], cells.shape)
+    parts = lax.all_to_all(cells, axes, 0, 0, tiled=True)
+    (spread,) = call(spread_kernel, "spread", [], [parts], [(cells.shape, f32)], after=after)
     return lax.all_to_all(spread, axes, 0, 0, tiled=True).reshape(taps, strips * lanes)
 
 
@@ -445,12 +474,12 @@
     taps = conv_weight.shape[0]
     side = taps // 2
     experts = lax.axis_size("expert")
-    dp_size = lax.axis_size("dp")
+    chips = lax.axis_size("chip")
+    dp_size = 2 * chips
     capacity = 2 * length // experts
     slots = experts * capacity
     hidden = up_master.shape[2]
-    chips = dp_size // 2
-    index = lax.axis_index("dp") * experts + lax.axis_index("expert")
+    index = lax.axis_index(("chip", "core", "expert"))
     index = index.astype(jnp.int32).reshape(1)
     here = functools.partial(Place, dp_size, experts)
     product = 2 * slots * width * hidden // chips
@@ -458,15 +487,18 @@
     strips = [pltpu.VMEM((length + 2 * side + 8, 128), f32), pltpu.VMEM((length + 16, 128), f32)]
     share, depth, units = hidden // dp_size, width // dp_size, hidden // chips
 
-    left, right = halo(frames[:side], frames[length - side :])
-    up_parts = call(
-        functools.partial(cast_far_kernel, here),
-        "cast_far",
+    head, tail, place, send_grads, *up_parts = call(
+        functools.partial(prepare_kernel, here, experts, capacity),
+        "prepare",
         [index],
-        [up_master[0]],
-        [((depth, units), bf16)] * (chips - 1),
-        moved=12 * share * width,
-    )
+        [expert_ids.reshape(1, length), cotangent, frames, up_master[0]],
+        [((side, width), bf16)] * 2
+        + [((slots, length), bf16), row_shape]
+        + [((depth, units), bf16)] * (chips - 1),
+        flops=2 * slots * length * width,
+        moved=4 * slots * width,
+    )
+    left, right = halo(head, tail)
     far_ups = [to_chip(part, shift + 1) for shift, part in enumerate(up_parts)]
     up_own, down_own = call(
         functools.partial(cast_near_kernel, here),
@@ -474,23 +506,13 @@
         [index],
         [up_master[0], down_master[0]],
         [((depth, units), bf16), ((share, width), bf16)],
-        after=up_parts[:1],
+        after=[place],
         moved=12 * share * width,
     )
     ups = [up_own, to_core(up_own)]
     downs = [down_own, to_core(down_own)]
     for arrived in far_ups:
         ups = ups + [arrived, to_core(arrived)]
-    place, send_grads = call(
-        functools.partial(dispatch_kernel, experts, capacity),
-        "dispatch",
-        [],
-        [expert_ids.reshape(1, length), cotangent],
-        [((slots, length), bf16), row_shape],
-        after=up_parts[:1],
-        flops=2 * slots * length * width,
-        moved=4 * slots * width,
-    )
     grads_in = by_expert(send_grads)
     slope, send_rows = call(
         functools.partial(conv_kernel, here),
@@ -498,40 +520,41 @@
         [index],
         [left, frames, right, conv_weight, place],
         [((length, width), f32), row_shape],
-        after=far_ups,
+        after=far_ups + [down_own],
         scratch=strips + [pltpu.VMEM((length, width), bf16)],
         flops=2 * slots * length * width,
         moved=8 * slots * width,
     )
     rows_in = by_expert(send_rows)
 
-    group_rows = [rows_in] + [to_chip(rows_in, shift) for shift in range(1, chips)]
-    group_grads = [grads_in] + [to_chip(grads_in, shift) for shift in range(1, chips)]
+    spans = [(rows_in, grads_in)]
+    for shift in range(1, chips):
+        spans.append((to_chip(rows_in, shift), to_chip(grads_in, shift)))
     hiddens, pres, parts = [], [], []
-    for group in range(chips):
+    for turn, (rows, grads) in enumerate(spans):
+        last = turn == chips - 1
         results = call(
-            functools.partial(group_kernel, here),
-            "own_group" if group == 0 else "far_group",
+            functools.partial(group_kernel, here, turn if last else 0),
+            "far_group" if turn else "own_group",
             [index],
-            [group_rows[group]] + ups + [group_grads[group]] + downs,
+            [rows] + ups + [grads] + downs + (parts if last else []),
             [
                 ((slots, units), bf16),
                 ((slots, units), bf16),
-                ((slots, width), f32 if group == 0 else bf16),
+                ((chips * slots if last else slots, width), bf16),
             ],
             scratch=[pltpu.VMEM((slots, units), f32)],
-            after=parts[:1],
+            after=parts[-1:],
             flops=3 * product,
             moved=8 * width * units,
         )
         for kind, result in zip((hiddens, pres, parts), results):
             kind.append(result)
-    back_total = parts[0]
-    for shift in range(1, chips):
-        back_total = back_total + to_chip(parts[shift], -shift).astype(f32)
-    returned = by_expert(back_total.astype(bf16))
+    returned = to_senders(parts[-1])
+    group_rows = [rows for rows, _ in spans]
+    group_grads = [grads for _, grads in spans]
     up_keep, up_send = call(
-        functools.partial(up_grad_kernel, here, chips),
+        functools.partial(up_grad_kernel, here, len(spans)),
         "up_grad",
         [index],
         group_rows + pres,
@@ -546,7 +569,7 @@
         chip_sum = (up_keep[part].astype(f32) + up_theirs[part].astype(f32)).astype(bf16)
         up_grads.append(to_chip(chip_sum, shift))
     down_keep, down_send = call(
-        functools.partial(down_grad_kernel, here, chips),
+        functools.partial(down_grad_kernel, here, len(spans)),
         "down_grad",
         [index],
         hiddens + group_grads,
@@ -572,7 +595,6 @@
         moved=8 * slots * width,
     )
     grad_left, grad_right = halo(head, tail)
-    conv_total = sum_everywhere(conv_terms)
     (grad_frames,) = call(
         functools.partial(frames_kernel, here),
         "frames",
@@ -587,16 +609,20 @@
         "adam_up", here, index, up_master, up_grads,
         up_mean_code, up_mean_scale, up_square_code, up_square_scale,
     )
+    conv_total = sum_everywhere(conv_terms, [grad_frames])
     return (grad_frames, conv_total) + up_next + down_next
 
 
 def solution(mesh):
-    frames = P(("dp", "expert"), None)
+    dp_size, experts = mesh.shape["dp"], mesh.shape["expert"]
+    devices = mesh.devices.reshape(dp_size // 2, 2, experts)
+    finer = jax.sharding.Mesh(devices, ("chip", "core", "expert"))
+    frames = P(("chip", "core", "expert"), None)
     shared = P()
-    state = P("expert", "dp", None)
+    state = P("expert", ("chip", "core"), None)
     return jax.shard_map(
         body,
-        mesh=mesh,
+        mesh=finer,
         in_specs=(frames,) * 3 + (shared,) + (state,) * 10,
         out_specs=(frames, shared) + (state,) * 10,
         check_vma=False,

time: 149 us -> 138 us (0.926)
  blocking collectives: 11.5 us -> 0 us
  starting transfers between devices: 41.1 us -> 45.5 us
  waiting for transfers between devices: 32.2 us -> 30.4 us
    all_to_all x1 -> x0, blocking collectives: 11.5 us -> none  [sum_everywhere(): mine = jnp.sum(lax.all_to_all(cells, axes, 0, 0, tiled=True), axis=0)]
    all_to_all x0 -> x2, starting transfers between devices: none -> 9.77 us  [the longest x1 7 us: to_senders(): return lax.all_to_all(cells, axes, 0, 0, tiled=True).reshape(rows.shape)]
    all_to_all x0 -> x2, waiting for transfers between devices: none -> 6.64 us  [the longest x1 6.63 us: to_senders(): return lax.all_to_all(cells, axes, 0, 0, tiled=True).reshape(rows.shape)]
    ppermute x10 -> x9, waiting for transfers between devices: 11.5 us -> 5.43 us  [the longest x4 5.42 us: to_chip(): lax.ppermute(values, 'chip', [(i, (i + shift) % chips) for i in range(chi...]
    all_to_all x3 -> x2, starting transfers between devices: 19 us -> 13 us  [by_expert(): lax.all_to_all(cells, 'expert', 0, 0, tiled=True).reshape(slots, width)]
    ppermute x4, waiting for transfers between devices: 9.62 us -> 7.03 us  [halo(): return (lax.ppermute(tail, axes, right), lax.ppermute(head, axes, left))]
    all_to_all x1, starting transfers between devices: 2.58 us -> 4.32 us  [sum_everywhere(): lax.all_to_all(spread, axes, 0, 0, tiled=True).reshape(taps, strips * lanes)]
    ppermute x10 -> x9, starting transfers between devices: 8.84 us -> 7.67 us  [the longest x4 6.47 us: to_chip(): lax.ppermute(values, 'chip', [(i, (i + shift) % chips) for i in range(chi...]
  transfers between devices with their start and end apart: 18 -> 18, of which waited for: 7 -> 6; matrix products, arithmetic and copies ran while one was open for 2% -> 1% of each run, Pallas kernels for 29% -> 33%
where the time goes in v3:
time: 138 us; the launch traced here: 137 us
  Pallas kernels  52.6 us (38%)
  starting transfers between devices  45.5 us (33%)
  waiting for transfers between devices  30.4 us (22%)
  local copies, waits for them, and re-layouts  6.3 us (5%)
    pallas_call x10, Pallas kernels, call(): pl.pallas_call(functools.partial(staged, kernel, counts, spans), out_shap...  37.2 us
    pallas_call x2, Pallas kernels, adam(): pl.pallas_call(functools.partial(adam_kernel, here, len(grads) - 2), grid...  15.4 us
    all_to_all x2, starting transfers between devices, by_expert(): lax.all_to_all(cells, 'expert', 0, 0, tiled=True).reshape(slots, width)  13 us
    all_to_all x2, waiting for transfers between devices, by_expert(): lax.all_to_all(cells, 'expert', 0, 0, tiled=True).reshape(slots, width)  11.3 us
    ppermute x4, starting transfers between devices, halo(): return (lax.ppermute(tail, axes, right), lax.ppermute(head, axes, left))  10.7 us
    ppermute x4, waiting for transfers between devices, halo(): return (lax.ppermute(tail, axes, right), lax.ppermute(head, axes, left))  7.03 us
    all_to_all x1, starting transfers between devices, to_senders(): return lax.all_to_all(cells, axes, 0, 0, tiled=True).reshape(rows.shape)  7 us
    all_to_all x1, waiting for transfers between devices, to_senders(): return lax.all_to_all(cells, axes, 0, 0, tiled=True).reshape(rows.shape)  6.63 us
  transfers between devices with their start and end apart: 18, of which 6 were waited for; matrix products, arithmetic and copies ran while one was open for 1% of the time, Pallas kernels for 33%

profile of v3, /device:TPU:0, one launch (start us, length us, event | category | flops | bytes accessed | tf_op | source)
XLA Modules:
  0.0 136.9 jit_solution(5660713983876311085)
XLA Ops:
  0.7 2.7 %prepare.1 = (bf16[16,1024]{1,0:T(8,128)(2,1)}, bf16[16,1024]{1,0:T(8,128)(2,1)}, bf16[256,128]{1,0:T(8,128)(2,1)}, bf16[256,1024]{1,0:T(8,128)(2,1)}, bf16[256,1024]{1,0:T(8,128)(2,1)}) custom-call(s32[1]{0:T(128)} %bitcast.refs_0_.index_ref, s32[1,128]{1,0:T(1,128)} %bitcast.72, bf16[128,1024]{1,0:T(8,128)(2,1)} %refs_5_.1, bf16[128,1024]{1,0:T(8,128)(2,1)} %refs_4_.4, ...), custom_call_target="tpu_custom_call" | custom-call | flops 67108864 | bytes 1048576 | tf_op jit(solution)/shard_map/prepare/pallas_call | solution.py:105
  3.4 7.3 %all-to-all-start.1 = ((bf16[8,32,1024]{2,1,0:T(8,128)(2,1)}), bf16[8,32,1024]{2,1,0:T(8,128)(2,1)S(1)}, u32[]{:S(2)}, u32[]{:S(2)}) async-start(bf16[8,32,1024]{2,1,0:T(8,128)(2,1)} %bitcast.64), calls=%async_computation.1 | async-start | bytes 1048576 | tf_op jit(solution)/shard_map/all_to_all | solution.py:420
  10.6 1.5 %collective-permute-start.2 = (bf16[256,1024]{1,0:T(8,128)(2,1)}, bf16[256,1024]{1,0:T(8,128)(2,1)S(1)}, u32[]{:S(2)}, u32[]{:S(2)}) collective-permute-start(bf16[256,1024]{1,0:T(8,128)(2,1)} %get-tuple-element.48), channel_id=1, source_target_pairs={{0,16},{16,0},{1,17},{17,1},{2,18},{18,2},{3,19},{19,3},{4,20},{20... | collective-permute-start | bytes 1572872 | tf_op jit(solution)/shard_map/ppermute | solution.py:432
  12.2 2.0 %collective-permute-start = (bf16[16,1024]{1,0:T(8,128)(2,1)}, bf16[16,1024]{1,0:T(8,128)(2,1)S(1)}, u32[]{:S(2)}, u32[]{:S(2)}) collective-permute-start(bf16[16,1024]{1,0:T(8,128)(2,1)} %get-tuple-element.46), channel_id=1, source_target_pairs={{0,1},{1,2},{2,3},{3,4},{4,5},{5,6},{6,7},{7,8},{8,9},{9,10},{10,1... | collective-permute-start | bytes 98312 | tf_op jit(solution)/shard_map/ppermute | solution.py:444
  14.2 3.3 %collective-permute-start.1 = (bf16[16,1024]{1,0:T(8,128)(2,1)}, bf16[16,1024]{1,0:T(8,128)(2,1)S(1)}, u32[]{:S(2)}, u32[]{:S(2)}) collective-permute-start(bf16[16,1024]{1,0:T(8,128)(2,1)} %get-tuple-element.47), channel_id=1, source_target_pairs={{1,0},{2,1},{3,2},{4,3},{5,4},{6,5},{7,6},{8,7},{9,8},{10,9},{11,1... | collective-permute-start | bytes 98312 | tf_op jit(solution)/shard_map/ppermute | solution.py:444
  17.5 3.3 %cast_near.1 = (bf16[256,1024]{1,0:T(8,128)(2,1)}, bf16[512,1024]{1,0:T(8,128)(2,1)}) custom-call(s32[1]{0:T(128)} %bitcast.refs_0_.index_ref, f32[256,2048]{1,0:T(8,128)} %bitcast.49, f32[512,1024]{1,0:T(8,128)} %bitcast.51, bf16[256,128]{1,0:T(8,128)(2,1)} %get-tuple-element.45.refs_3_.refs_5_.refs_1_), custom_call_target="tpu_custom_call" | custom-call | bytes 6291456 | tf_op jit(solution)/shard_map/cast_near/pallas_call | solution.py:105
  20.9 3.5 %collective-permute-done.refs_1_.refs_3_ = bf16[16,1024]{1,0:T(8,128)(2,1)S(1)} collective-permute-done((bf16[16,1024]{1,0:T(8,128)(2,1)}, bf16[16,1024]{1,0:T(8,128)(2,1)S(1)}, u32[]{:S(2)}, u32[]{:S(2)}) %collective-permute-start) | collective-permute-done | bytes 32800 | tf_op jit(solution)/shard_map/ppermute | solution.py:444
  24.4 0.2 collective-permute-done.2.refs_6_.refs_4_
  24.6 0.4 copy-done.12
  25.0 0.0 copy-done.13
  25.0 0.4 copy-done.4
  25.4 3.8 %convolve.1 = (f32[128,1024]{1,0:T(8,128)}, bf16[256,1024]{1,0:T(8,128)(2,1)}) custom-call(s32[1]{0:T(128)} %bitcast.refs_0_.index_ref, bf16[16,1024]{1,0:T(8,128)(2,1)} %copy-done.12, bf16[128,1024]{1,0:T(8,128)(2,1)} %refs_4_.4, bf16[16,1024]{1,0:T(8,128)(2,1)} %copy-done.13, f32[32,1024]{1,0:T(8,128)} %refs_4_.5, ...), custom_call_target="tpu_custom_call" | custom-call | flops 67108864 | bytes 2097152 | tf_op jit(solution)/shard_map/convolve/pallas_call | solution.py:105
  29.2 5.7 %all-to-all-start = ((bf16[8,32,1024]{2,1,0:T(8,128)(2,1)}), bf16[8,32,1024]{2,1,0:T(8,128)(2,1)}, u32[]{:S(2)}, u32[]{:S(2)}) async-start(bf16[8,32,1024]{2,1,0:T(8,128)(2,1)} %bitcast.65), calls=%async_computation | async-start | bytes 1048576 | tf_op jit(solution)/shard_map/all_to_all | solution.py:420
  34.9 0.1 collective-permute-start.7
  35.0 0.5 collective-permute-start.4
  35.5 0.1 collective-permute-start.5
  35.6 1.5 %collective-permute-start.6 = (bf16[256,1024]{1,0:T(8,128)(2,1)}, bf16[256,1024]{1,0:T(8,128)(2,1)S(1)}, u32[]{:S(2)}, u32[]{:S(2)}) collective-permute-start(bf16[256,1024]{1,0:T(8,128)(2,1)} %bitcast.61), channel_id=1, source_target_pairs={{0,16},{16,0},{1,17},{17,1},{2,18},{18,2},{3,19},{19,3},{4,20},{20... | collective-permute-start | bytes 1572872 | tf_op jit(solution)/shard_map/ppermute | solution.py:432
  37.1 11.3 %all-to-all-done = bf16[8,32,1024]{2,1,0:T(8,128)(2,1)} async-done(((bf16[8,32,1024]{2,1,0:T(8,128)(2,1)}), bf16[8,32,1024]{2,1,0:T(8,128)(2,1)}, u32[]{:S(2)}, u32[]{:S(2)}) %all-to-all-start) | async-done | bytes 524320 | tf_op jit(solution)/shard_map/all_to_all | solution.py:420
  48.5 1.5 %collective-permute-start.3 = (bf16[256,1024]{1,0:T(8,128)(2,1)}, bf16[256,1024]{1,0:T(8,128)(2,1)S(1)}, u32[]{:S(2)}, u32[]{:S(2)}) collective-permute-start(bf16[256,1024]{1,0:T(8,128)(2,1)} %bitcast.5.refs_1_), channel_id=1, source_target_pairs={{0,16},{16,0},{1,17},{17,1},{2,18},{18,2},{3,19},{19,3},{4,20},{20... | collective-permute-start | bytes 1572872 | tf_op jit(solution)/shard_map/ppermute | solution.py:432
  50.0 1.0 copy-done.5
  51.0 5.1 %own_group.1 = (bf16[256,1024]{1,0:T(8,128)(2,1)}, bf16[256,1024]{1,0:T(8,128)(2,1)}, bf16[256,1024]{1,0:T(8,128)(2,1)}) custom-call(s32[1]{0:T(128)} %bitcast.refs_0_.index_ref, bf16[256,1024]{1,0:T(8,128)(2,1)} %bitcast.5.refs_1_, bf16[256,1024]{1,0:T(8,128)(2,1)} %get-tuple-element.52.refs_2_, bf16[256,1024]{1,0:T(8,128)(2,1)} %collective-permute-done.4.refs_3_, ...), custom_call_target="tpu_custom_call" | custom-call | flops 1610612736 | bytes 8388608 | tf_op jit(solution)/shard_map/own_group/pallas_call | solution.py:105
  56.1 5.2 %collective-permute-done.3.refs_1_.refs_2_ = bf16[256,1024]{1,0:T(8,128)(2,1)S(1)} collective-permute-done((bf16[256,1024]{1,0:T(8,128)(2,1)}, bf16[256,1024]{1,0:T(8,128)(2,1)S(1)}, u32[]{:S(2)}, u32[]{:S(2)}) %collective-permute-start.3) | collective-permute-done | bytes 524320 | tf_op jit(solution)/shard_map/ppermute | solution.py:432
  61.3 0.8 copy-done.8
  62.1 5.4 %far_group.1 = (bf16[256,1024]{1,0:T(8,128)(2,1)}, bf16[256,1024]{1,0:T(8,128)(2,1)}, bf16[512,1024]{1,0:T(8,128)(2,1)}) custom-call(s32[1]{0:T(128)} %bitcast.refs_0_.index_ref, bf16[256,1024]{1,0:T(8,128)(2,1)} %copy-done.8, bf16[256,1024]{1,0:T(8,128)(2,1)} %get-tuple-element.52.refs_2_, bf16[256,1024]{1,0:T(8,128)(2,1)} %collective-permute-done.4.refs_3_, ...), custom_call_target="tpu_custom_call" | custom-call | flops 1610612736 | bytes 8388608 | tf_op jit(solution)/shard_map/far_group/pallas_call | solution.py:105
  67.5 7.0 %all-to-all-start.2 = ((bf16[16,32,1024]{2,1,0:T(8,128)(2,1)}), bf16[16,32,1024]{2,1,0:T(8,128)(2,1)S(1)}, u32[]{:S(2)}, u32[]{:S(2)}) async-start(bf16[16,32,1024]{2,1,0:T(8,128)(2,1)} %bitcast.58), calls=%async_computation.2 | async-start | bytes 2097152 | tf_op jit(solution)/shard_map/all_to_all | solution.py:427
  74.6 3.9 %up_grad.1 = (bf16[512,1024]{1,0:T(8,128)(2,1)}, bf16[512,1024]{1,0:T(8,128)(2,1)}) custom-call(s32[1]{0:T(128)} %bitcast.refs_0_.index_ref, bf16[256,1024]{1,0:T(8,128)(2,1)} %bitcast.5.refs_1_, bf16[256,1024]{1,0:T(8,128)(2,1)} %copy-done.8, bf16[256,1024]{1,0:T(8,128)(2,1)} %get-tuple-element.65.refs_3_, bf16[256,1024]{1,0:T(8,128)(2,1)} %get-tuple-element.66.refs_4_), custom_call_target="tpu_custom_call" | custom-call | flops 1073741824 | bytes 8388608 | tf_op jit(solution)/shard_map/up_grad/pallas_call | solution.py:105
  78.4 0.1 collective-permute-start.11
  78.5 3.9 %down_grad.1 = (bf16[512,1024]{1,0:T(8,128)(2,1)}, bf16[512,1024]{1,0:T(8,128)(2,1)}) custom-call(s32[1]{0:T(128)} %bitcast.refs_0_.index_ref, bf16[256,1024]{1,0:T(8,128)(2,1)} %get-tuple-element.56.refs_1_, bf16[256,1024]{1,0:T(8,128)(2,1)} %get-tuple-element.57.refs_2_, bf16[256,1024]{1,0:T(8,128)(2,1)} %bitcast.63, bf16[256,1024]{1,0:T(8,128)(2,1)} %copy-done.7), custom_call_target="tpu_custom_call" | custom-call | flops 1073741824 | bytes 8388608 | tf_op jit(solution)/shard_map/down_grad/pallas_call | solution.py:105
  82.4 0.5 collective-permute-start.8
  82.9 1.1 add_convert_fusion
  84.1 1.9 %collective-permute-start.12 = (bf16[256,1024]{1,0:T(8,128)(2,1)}, bf16[256,1024]{1,0:T(8,128)(2,1)S(1)}, u32[]{:S(2)}, u32[]{:S(2)}) collective-permute-start(bf16[256,1024]{1,0:T(8,128)(2,1)} %add_convert_fusion), channel_id=1, source_target_pairs={{0,16},{16,0},{1,17},{17,1},{2,18},{18,2},{3,19},{19,3},{4,20},{20... | collective-permute-start | bytes 1572872 | tf_op jit(solution)/shard_map/ppermute | solution.py:432
  86.0 7.6 %adam_down.1 = (f32[512,1024]{1,0:T(8,128)}, bf16[512,1024]{1,0:T(8,128)(2,1)}, f32[8,512]{1,0:T(8,128)}, bf16[512,1024]{1,0:T(8,128)(2,1)}, f32[8,512]{1,0:T(8,128)}) custom-call(s32[1]{0:T(128)} %bitcast.refs_0_.index_ref, f32[512,1024]{1,0:T(8,128)} %bitcast.52, bf16[512,1024]{1,0:T(8,128)(2,1)} %bitcast.56, f32[8,512]{1,0:T(8,128)} %bitcast.68, ...), custom_call_target="tpu_custom_call" | custom-call | flops 10485760 | bytes 10485760 | tf_op jit(solution)/shard_map/adam_down/pallas_call | solution.py:393
  93.6 6.6 %all-to-all-done.2 = bf16[16,32,1024]{2,1,0:T(8,128)(2,1)S(1)} async-done(((bf16[16,32,1024]{2,1,0:T(8,128)(2,1)}), bf16[16,32,1024]{2,1,0:T(8,128)(2,1)S(1)}, u32[]{:S(2)}, u32[]{:S(2)}) %all-to-all-start.2) | async-done | bytes 1048608 | tf_op jit(solution)/shard_map/all_to_all | solution.py:427
  100.3 1.0 copy-done.1
  101.2 4.0 %taps.1 = (bf16[128,1024]{1,0:T(8,128)(2,1)}, bf16[16,1024]{1,0:T(8,128)(2,1)}, bf16[16,1024]{1,0:T(8,128)(2,1)}, f32[32,8,128]{2,1,0:T(8,128)}) custom-call(s32[1]{0:T(128)} %bitcast.refs_0_.index_ref, bf16[256,128]{1,0:T(8,128)(2,1)} %get-tuple-element.45.refs_3_.refs_5_.refs_1_, f32[128,1024]{1,0:T(8,128)} %get-tuple-element.50.refs_2_, ...), custom_call_target="tpu_custom_call" | custom-call | flops 67108864 | bytes 2097152 | tf_op jit(solution)/shard_map/taps/pallas_call | solution.py:105
  105.3 2.8 %all-to-all-start.3 = ((f32[32,8,128]{2,1,0:T(8,128)}), f32[32,8,128]{2,1,0:T(8,128)S(1)}, u32[]{:S(2)}, u32[]{:S(2)}) async-start(f32[32,8,128]{2,1,0:T(8,128)} %get-tuple-element.64), calls=%async_computation.3 | async-start | bytes 262144 | tf_op jit(solution)/shard_map/all_to_all | solution.py:452
  108.0 1.8 %collective-permute-start.9 = (bf16[16,1024]{1,0:T(8,128)(2,1)}, bf16[16,1024]{1,0:T(8,128)(2,1)S(1)}, u32[]{:S(2)}, u32[]{:S(2)}) collective-permute-start(bf16[16,1024]{1,0:T(8,128)(2,1)} %get-tuple-element.61), channel_id=1, source_target_pairs={{0,1},{1,2},{2,3},{3,4},{4,5},{5,6},{6,7},{7,8},{8,9},{9,10},{10,1... | collective-permute-start | bytes 98312 | tf_op jit(solution)/shard_map/ppermute | solution.py:444
  109.9 3.6 %collective-permute-start.10 = (bf16[16,1024]{1,0:T(8,128)(2,1)}, bf16[16,1024]{1,0:T(8,128)(2,1)S(1)}, u32[]{:S(2)}, u32[]{:S(2)}) collective-permute-start(bf16[16,1024]{1,0:T(8,128)(2,1)} %get-tuple-element.63), channel_id=1, source_target_pairs={{1,0},{2,1},{3,2},{4,3},{5,4},{6,5},{7,6},{8,7},{9,8},{10,9},{11,1... | collective-permute-start | bytes 98312 | tf_op jit(solution)/shard_map/ppermute | solution.py:444
  113.4 3.5 %collective-permute-done.9.refs_1_ = bf16[16,1024]{1,0:T(8,128)(2,1)S(1)} collective-permute-done((bf16[16,1024]{1,0:T(8,128)(2,1)}, bf16[16,1024]{1,0:T(8,128)(2,1)S(1)}, u32[]{:S(2)}, u32[]{:S(2)}) %collective-permute-start.9) | collective-permute-done | bytes 32800 | tf_op jit(solution)/shard_map/ppermute | solution.py:444
  116.9 0.6 copy-done.14
  117.5 0.0 copy-done.15
  117.6 3.4 %frames.1.refs_1_ = bf16[128,1024]{1,0:T(8,128)(2,1)} custom-call(s32[1]{0:T(128)} %bitcast.refs_0_.index_ref, bf16[16,1024]{1,0:T(8,128)(2,1)} %copy-done.14, bf16[128,1024]{1,0:T(8,128)(2,1)} %get-tuple-element.62.refs_2_, bf16[16,1024]{1,0:T(8,128)(2,1)} %copy-done.15, f32[32,1024]{1,0:T(8,128)} %refs_4_.5, bf16[128,1024]{1,0:T(8,128)(2,1)} %refs_5_.1), custom_call_target="tpu_custom_call" | custom-call | flops 67108864 | bytes 1048576 | tf_op jit(solution)/shard_map/frames/pallas_call | solution.py:105
  121.0 0.6 copy-done.10
  121.7 1.6 %spread.1 = f32[32,8,128]{2,1,0:T(8,128)} custom-call(f32[32,8,128]{2,1,0:T(8,128)} %copy-done.10, bf16[128,1024]{1,0:T(8,128)(2,1)} %frames.1.refs_1_), custom_call_target="tpu_custom_call" | custom-call | tf_op jit(solution)/shard_map/spread/pallas_call | solution.py:105
  123.3 4.3 %all-to-all-start.4 = ((f32[32,8,128]{2,1,0:T(8,128)}), f32[32,8,128]{2,1,0:T(8,128)S(1)}, u32[]{:S(2)}, u32[]{:S(2)}) async-start(f32[32,8,128]{2,1,0:T(8,128)} %spread.1), calls=%async_computation.4 | async-start | bytes 262144 | tf_op jit(solution)/shard_map/all_to_all | solution.py:454
  127.6 0.8 copy-done.11
  128.4 7.8 %adam_up.1 = (f32[256,2048]{1,0:T(8,128)}, bf16[256,2048]{1,0:T(8,128)(2,1)}, f32[16,256]{1,0:T(8,128)}, bf16[256,2048]{1,0:T(8,128)(2,1)}, f32[16,256]{1,0:T(8,128)}) custom-call(s32[1]{0:T(128)} %bitcast.refs_0_.index_ref, f32[256,2048]{1,0:T(8,128)} %bitcast.50, bf16[256,2048]{1,0:T(8,128)(2,1)} %bitcast.59, f32[16,256]{1,0:T(8,128)} %bitcast.70, ...), custom_call_target="tpu_custom_call" | custom-call | flops 10485760 | bytes 11534336 | tf_op jit(solution)/shard_map/adam_up/pallas_call | solution.py:393
  136.2 0.7 copy.28
  (34 shorter events, 0.1 us)
Async XLA Ops:
  3.4 25.8 %all-to-all-start.1 = ((bf16[8,32,1024]{2,1,0:T(8,128)(2,1)}), bf16[8,32,1024]{2,1,0:T(8,128)(2,1)S(1)}, u32[]{:S(2)}, u32[]{:S(2)}) async-start(bf16[8,32,1024]{2,1,0:T(8,128)(2,1)} %bitcast.64), calls=%async_computation.1 | async-start | bytes 1048576 | tf_op jit(solution)/shard_map/all_to_all | solution.py:420
  10.6 13.9 %collective-permute-start.2 = (bf16[256,1024]{1,0:T(8,128)(2,1)}, bf16[256,1024]{1,0:T(8,128)(2,1)S(1)}, u32[]{:S(2)}, u32[]{:S(2)}) collective-permute-start(bf16[256,1024]{1,0:T(8,128)(2,1)} %get-tuple-element.48), channel_id=1, source_target_pairs={{0,16},{16,0},{1,17},{17,1},{2,18},{18,2},{3,19},{19,3},{4,20},{20... | collective-permute-start | bytes 1572872 | tf_op jit(solution)/shard_map/ppermute | solution.py:432
  12.2 12.2 %collective-permute-start = (bf16[16,1024]{1,0:T(8,128)(2,1)}, bf16[16,1024]{1,0:T(8,128)(2,1)S(1)}, u32[]{:S(2)}, u32[]{:S(2)}) collective-permute-start(bf16[16,1024]{1,0:T(8,128)(2,1)} %get-tuple-element.46), channel_id=1, source_target_pairs={{0,1},{1,2},{2,3},{3,4},{4,5},{5,6},{6,7},{7,8},{8,9},{9,10},{10,1... | collective-permute-start | bytes 98312 | tf_op jit(solution)/shard_map/ppermute | solution.py:444
  14.2 10.2 %collective-permute-start.1 = (bf16[16,1024]{1,0:T(8,128)(2,1)}, bf16[16,1024]{1,0:T(8,128)(2,1)S(1)}, u32[]{:S(2)}, u32[]{:S(2)}) collective-permute-start(bf16[16,1024]{1,0:T(8,128)(2,1)} %get-tuple-element.47), channel_id=1, source_target_pairs={{1,0},{2,1},{3,2},{4,3},{5,4},{6,5},{7,6},{8,7},{9,8},{10,9},{11,1... | collective-permute-start | bytes 98312 | tf_op jit(solution)/shard_map/ppermute | solution.py:444
  20.8 14.1 %copy-start = (bf16[512,1024]{1,0:T(8,128)(2,1)S(1)}, bf16[512,1024]{1,0:T(8,128)(2,1)}, u32[]{:S(2)}) copy-start(bf16[512,1024]{1,0:T(8,128)(2,1)} %get-tuple-element.49.refs_7_) | copy-start | bytes 3145732
  20.8 14.2 %copy-start.6 = (bf16[256,1024]{1,0:T(8,128)(2,1)S(1)}, bf16[256,1024]{1,0:T(8,128)(2,1)}, u32[]{:S(2)}) copy-start(bf16[256,1024]{1,0:T(8,128)(2,1)} %get-tuple-element.52.refs_2_) | copy-start | bytes 1572868
  24.4 0.6 copy-start.12
  24.4 0.6 copy-start.13
  24.6 0.8 copy-start.4
  29.2 6.4 %copy-start.9 = (bf16[8,32,1024]{2,1,0:T(8,128)(2,1)}, bf16[8,32,1024]{2,1,0:T(8,128)(2,1)S(1)}, u32[]{:S(2)}) copy-start(bf16[8,32,1024]{2,1,0:T(8,128)(2,1)S(1)} %all-to-all-done.1) | copy-start | bytes 1572868
  29.2 19.2 %all-to-all-start = ((bf16[8,32,1024]{2,1,0:T(8,128)(2,1)}), bf16[8,32,1024]{2,1,0:T(8,128)(2,1)}, u32[]{:S(2)}, u32[]{:S(2)}) async-start(bf16[8,32,1024]{2,1,0:T(8,128)(2,1)} %bitcast.65), calls=%async_computation | async-start | bytes 1048576 | tf_op jit(solution)/shard_map/all_to_all | solution.py:420
  34.9 15.0 %collective-permute-start.7 = (bf16[512,1024]{1,0:T(8,128)(2,1)S(1)}, bf16[512,1024]{1,0:T(8,128)(2,1)S(1)}, u32[]{:S(2)}, u32[]{:S(2)}) collective-permute-start(bf16[512,1024]{1,0:T(8,128)(2,1)S(1)} %copy-done), channel_id=1, source_target_pairs={{0,8},{8,0},{1,9},{9,1},{2,10},{10,2},{3,11},{11,3},{4,12},{12,4},... | collective-permute-start | bytes 3145736 | tf_op jit(solution)/shard_map/ppermute | solution.py:436
  35.0 15.0 %collective-permute-start.4 = (bf16[256,1024]{1,0:T(8,128)(2,1)S(1)}, bf16[256,1024]{1,0:T(8,128)(2,1)}, u32[]{:S(2)}, u32[]{:S(2)}) collective-permute-start(bf16[256,1024]{1,0:T(8,128)(2,1)S(1)} %copy-done.6), channel_id=1, source_target_pairs={{0,8},{8,0},{1,9},{9,1},{2,10},{10,2},{3,11},{11,3},{4,12},{12,4},... | collective-permute-start | bytes 1572872 | tf_op jit(solution)/shard_map/ppermute | solution.py:436
  35.5 14.5 %collective-permute-start.5 = (bf16[256,1024]{1,0:T(8,128)(2,1)}, bf16[256,1024]{1,0:T(8,128)(2,1)}, u32[]{:S(2)}, u32[]{:S(2)}) collective-permute-start(bf16[256,1024]{1,0:T(8,128)(2,1)} %copy-done.4), channel_id=1, source_target_pairs={{0,8},{8,0},{1,9},{9,1},{2,10},{10,2},{3,11},{11,3},{4,12},{12,4},... | collective-permute-start | bytes 1572872 | tf_op jit(solution)/shard_map/ppermute | solution.py:436
  35.6 20.5 %collective-permute-start.6 = (bf16[256,1024]{1,0:T(8,128)(2,1)}, bf16[256,1024]{1,0:T(8,128)(2,1)S(1)}, u32[]{:S(2)}, u32[]{:S(2)}) collective-permute-start(bf16[256,1024]{1,0:T(8,128)(2,1)} %bitcast.61), channel_id=1, source_target_pairs={{0,16},{16,0},{1,17},{17,1},{2,18},{18,2},{3,19},{19,3},{4,20},{20... | collective-permute-start | bytes 1572872 | tf_op jit(solution)/shard_map/ppermute | solution.py:432
  48.5 12.9 %collective-permute-start.3 = (bf16[256,1024]{1,0:T(8,128)(2,1)}, bf16[256,1024]{1,0:T(8,128)(2,1)S(1)}, u32[]{:S(2)}, u32[]{:S(2)}) collective-permute-start(bf16[256,1024]{1,0:T(8,128)(2,1)} %bitcast.5.refs_1_), channel_id=1, source_target_pairs={{0,16},{16,0},{1,17},{17,1},{2,18},{18,2},{3,19},{19,3},{4,20},{20... | collective-permute-start | bytes 1572872 | tf_op jit(solution)/shard_map/ppermute | solution.py:432
  50.0 1.0 copy-start.5
  56.1 5.2 %copy-start.7 = (bf16[256,1024]{1,0:T(8,128)(2,1)}, bf16[256,1024]{1,0:T(8,128)(2,1)S(1)}, u32[]{:S(2)}) copy-start(bf16[256,1024]{1,0:T(8,128)(2,1)S(1)} %collective-permute-done.6.refs_6_.refs_4_) | copy-start | bytes 1572868
  61.3 0.8 copy-start.8
  67.5 32.7 %all-to-all-start.2 = ((bf16[16,32,1024]{2,1,0:T(8,128)(2,1)}), bf16[16,32,1024]{2,1,0:T(8,128)(2,1)S(1)}, u32[]{:S(2)}, u32[]{:S(2)}) async-start(bf16[16,32,1024]{2,1,0:T(8,128)(2,1)} %bitcast.58), calls=%async_computation.2 | async-start | bytes 2097152 | tf_op jit(solution)/shard_map/all_to_all | solution.py:427
  78.4 4.5 %copy-start.2 = (bf16[512,1024]{1,0:T(8,128)(2,1)S(1)}, bf16[512,1024]{1,0:T(8,128)(2,1)}, u32[]{:S(2)}) copy-start(bf16[512,1024]{1,0:T(8,128)(2,1)} %get-tuple-element.67.refs_0_) | copy-start | bytes 3145732
  78.4 4.5 %collective-permute-start.11 = (bf16[512,1024]{1,0:T(8,128)(2,1)}, bf16[512,1024]{1,0:T(8,128)(2,1)S(1)}, u32[]{:S(2)}, u32[]{:S(2)}) collective-permute-start(bf16[512,1024]{1,0:T(8,128)(2,1)} %get-tuple-element.68), channel_id=1, source_target_pairs={{0,8},{8,0},{1,9},{9,1},{2,10},{10,2},{3,11},{11,3},{4,12},{12,4},... | collective-permute-start | bytes 3145736 | tf_op jit(solution)/shard_map/ppermute | solution.py:436
  82.4 3.6 %collective-permute-start.8 = (bf16[512,1024]{1,0:T(8,128)(2,1)}, bf16[512,1024]{1,0:T(8,128)(2,1)}, u32[]{:S(2)}, u32[]{:S(2)}) collective-permute-start(bf16[512,1024]{1,0:T(8,128)(2,1)} %get-tuple-element.59), channel_id=1, source_target_pairs={{0,8},{8,0},{1,9},{9,1},{2,10},{10,2},{3,11},{11,3},{4,12},{12,4},... | collective-permute-start | bytes 3145736 | tf_op jit(solution)/shard_map/ppermute | solution.py:436
  82.9 10.7 %copy-start.3 = (bf16[512,1024]{1,0:T(8,128)(2,1)}, bf16[512,1024]{1,0:T(8,128)(2,1)S(1)}, u32[]{:S(2)}) copy-start(bf16[512,1024]{1,0:T(8,128)(2,1)S(1)} %collective-permute-done.11.refs_1_) | copy-start | bytes 3145732
  84.1 43.5 %collective-permute-start.12 = (bf16[256,1024]{1,0:T(8,128)(2,1)}, bf16[256,1024]{1,0:T(8,128)(2,1)S(1)}, u32[]{:S(2)}, u32[]{:S(2)}) collective-permute-start(bf16[256,1024]{1,0:T(8,128)(2,1)} %add_convert_fusion), channel_id=1, source_target_pairs={{0,16},{16,0},{1,17},{17,1},{2,18},{18,2},{3,19},{19,3},{4,20},{20... | collective-permute-start | bytes 1572872 | tf_op jit(solution)/shard_map/ppermute | solution.py:432
  100.3 1.0 copy-start.1
  105.3 15.7 %all-to-all-start.3 = ((f32[32,8,128]{2,1,0:T(8,128)}), f32[32,8,128]{2,1,0:T(8,128)S(1)}, u32[]{:S(2)}, u32[]{:S(2)}) async-start(f32[32,8,128]{2,1,0:T(8,128)} %get-tuple-element.64), calls=%async_computation.3 | async-start | bytes 262144 | tf_op jit(solution)/shard_map/all_to_all | solution.py:452
  108.0 8.9 %collective-permute-start.9 = (bf16[16,1024]{1,0:T(8,128)(2,1)}, bf16[16,1024]{1,0:T(8,128)(2,1)S(1)}, u32[]{:S(2)}, u32[]{:S(2)}) collective-permute-start(bf16[16,1024]{1,0:T(8,128)(2,1)} %get-tuple-element.61), channel_id=1, source_target_pairs={{0,1},{1,2},{2,3},{3,4},{4,5},{5,6},{6,7},{7,8},{8,9},{9,10},{10,1... | collective-permute-start | bytes 98312 | tf_op jit(solution)/shard_map/ppermute | solution.py:444
  109.9 7.1 %collective-permute-start.10 = (bf16[16,1024]{1,0:T(8,128)(2,1)}, bf16[16,1024]{1,0:T(8,128)(2,1)S(1)}, u32[]{:S(2)}, u32[]{:S(2)}) collective-permute-start(bf16[16,1024]{1,0:T(8,128)(2,1)} %get-tuple-element.63), channel_id=1, source_target_pairs={{1,0},{2,1},{3,2},{4,3},{5,4},{6,5},{7,6},{8,7},{9,8},{10,9},{11,1... | collective-permute-start | bytes 98312 | tf_op jit(solution)/shard_map/ppermute | solution.py:444
  116.9 0.6 copy-start.14
  116.9 0.6 copy-start.15
  121.0 0.7 copy-start.10
  123.3 12.9 %all-to-all-start.4 = ((f32[32,8,128]{2,1,0:T(8,128)}), f32[32,8,128]{2,1,0:T(8,128)S(1)}, u32[]{:S(2)}, u32[]{:S(2)}) async-start(f32[32,8,128]{2,1,0:T(8,128)} %spread.1), calls=%async_computation.4 | async-start | bytes 262144 | tf_op jit(solution)/shard_map/all_to_all | solution.py:454
  127.6 0.8 copy-start.11

commit v4 on v3

--- a/solution.py
+++ b/solution.py
@@ -87,7 +87,7 @@
         copy.wait()
 
 
-def call(kernel, name, scalars, inputs, outs, scratch=(), after=(), resident=(), flops=0, moved=0, limit=60):
+def call(kernel, name, scalars, inputs, outs, scratch=(), after=(), resident=(), flops=0, moved=0, limit=63):
     hbm = pl.BlockSpec(memory_space=pl.ANY)
     vmem = pl.BlockSpec(memory_space=pltpu.VMEM)
     smem = pl.BlockSpec(memory_space=pltpu.SMEM)
@@ -401,7 +401,7 @@
             pltpu.VMEM((2, rows, 128), f32),
             pltpu.VMEM((part, width), f32),
         ],
-        compiler_params=pltpu.CompilerParams(vmem_limit_bytes=60 * MIB),
+        compiler_params=pltpu.CompilerParams(vmem_limit_bytes=63 * MIB),
         cost_estimate=pl.CostEstimate(
             flops=20 * rows * width,
             bytes_accessed=(16 + 2 * len(grads)) * rows * width,
@@ -609,7 +609,7 @@
         "adam_up", here, index, up_master, up_grads,
         up_mean_code, up_mean_scale, up_square_code, up_square_scale,
     )
-    conv_total = sum_everywhere(conv_terms, [grad_frames])
+    conv_total = sum_everywhere(conv_terms, [up_next[0], grad_left, grad_right])
     return (grad_frames, conv_total) + up_next + down_next
 
 

time: 138 us -> 134 us (0.971)
  local copies, waits for them, and re-layouts: 6.3 us -> 2.13 us
  waiting for transfers between devices: 30.4 us -> 32.2 us
  starting transfers between devices: 45.5 us -> 43.9 us
    all_to_all x1, waiting for transfers between devices: 0.01 us -> 4.3 us  [sum_everywhere(): lax.all_to_all(spread, axes, 0, 0, tiled=True).reshape(taps, strips * lanes)]
    unnamed x33 -> x15, local copies, waits for them, and re-layouts: 6.3 us -> 2.13 us
    ppermute x4, waiting for transfers between devices: 7.03 us -> 3.57 us  [halo(): return (lax.ppermute(tail, axes, right), lax.ppermute(head, axes, left))]
    all_to_all x1, starting transfers between devices: 4.32 us -> 2.57 us  [sum_everywhere(): lax.all_to_all(spread, axes, 0, 0, tiled=True).reshape(taps, strips * lanes)]
  transfers between devices with their start and end apart: 18 -> 18, of which waited for: 6 -> 6; matrix products, arithmetic and copies ran while one was open for 1% -> 1% of each run, Pallas kernels for 33% -> 32%
where the time goes in v4:
time: 134 us; the launch traced here: 133 us
  Pallas kernels  52.4 us (39%)
  starting transfers between devices  43.9 us (33%)
  waiting for transfers between devices  32.2 us (24%)
  local copies, waits for them, and re-layouts  2.13 us (2%)
  other arithmetic  1.39 us (1%)
    pallas_call x10, Pallas kernels, call(): pl.pallas_call(functools.partial(staged, kernel, counts, spans), out_shap...  37.1 us
    pallas_call x2, Pallas kernels, adam(): pl.pallas_call(functools.partial(adam_kernel, here, len(grads) - 2), grid...  15.3 us
    all_to_all x2, starting transfers between devices, by_expert(): lax.all_to_all(cells, 'expert', 0, 0, tiled=True).reshape(slots, width)  13 us
    all_to_all x2, waiting for transfers between devices, by_expert(): lax.all_to_all(cells, 'expert', 0, 0, tiled=True).reshape(slots, width)  11.4 us
    ppermute x4, starting transfers between devices, halo(): return (lax.ppermute(tail, axes, right), lax.ppermute(head, axes, left))  10.7 us
    all_to_all x1, starting transfers between devices, to_senders(): return lax.all_to_all(cells, axes, 0, 0, tiled=True).reshape(rows.shape)  7.13 us
    all_to_all x1, waiting for transfers between devices, to_senders(): return lax.all_to_all(cells, axes, 0, 0, tiled=True).reshape(rows.shape)  6.49 us
    ppermute x4, starting transfers between devices, to_chip(): lax.ppermute(values, 'chip', [(i, (i + shift) % chips) for i in range(chi...  6.48 us
  transfers between devices with their start and end apart: 18, of which 6 were waited for; matrix products, arithmetic and copies ran while one was open for 1% of the time, Pallas kernels for 32%

profile of v4, /device:TPU:0, one launch (start us, length us, event | category | flops | bytes accessed | tf_op | source)
XLA Modules:
  0.0 132.9 jit_solution(17023057742068533564)
XLA Ops:
  0.7 2.7 %prepare.1 = (bf16[16,1024]{1,0:T(8,128)(2,1)}, bf16[16,1024]{1,0:T(8,128)(2,1)}, bf16[256,128]{1,0:T(8,128)(2,1)}, bf16[256,1024]{1,0:T(8,128)(2,1)}, bf16[256,1024]{1,0:T(8,128)(2,1)}) custom-call(s32[1]{0:T(128)} %bitcast.refs_0_.index_ref, s32[1,128]{1,0:T(1,128)} %bitcast.70, bf16[128,1024]{1,0:T(8,128)(2,1)} %refs_5_.1, bf16[128,1024]{1,0:T(8,128)(2,1)} %refs_4_.4, ...), custom_call_target="tpu_custom_call" | custom-call | flops 67108864 | bytes 1048576 | tf_op jit(solution)/shard_map/prepare/pallas_call | solution.py:105
  3.4 7.3 %all-to-all-start.1 = ((bf16[8,32,1024]{2,1,0:T(8,128)(2,1)}), bf16[8,32,1024]{2,1,0:T(8,128)(2,1)}, u32[]{:S(2)}, u32[]{:S(2)}) async-start(bf16[8,32,1024]{2,1,0:T(8,128)(2,1)} %bitcast.62), calls=%async_computation.1 | async-start | bytes 1048576 | tf_op jit(solution)/shard_map/all_to_all | solution.py:420
  10.6 1.5 %collective-permute-start.2 = (bf16[256,1024]{1,0:T(8,128)(2,1)}, bf16[256,1024]{1,0:T(8,128)(2,1)S(1)}, u32[]{:S(2)}, u32[]{:S(2)}) collective-permute-start(bf16[256,1024]{1,0:T(8,128)(2,1)} %get-tuple-element.48), channel_id=1, source_target_pairs={{0,16},{16,0},{1,17},{17,1},{2,18},{18,2},{3,19},{19,3},{4,20},{20... | collective-permute-start | bytes 1572872 | tf_op jit(solution)/shard_map/ppermute | solution.py:432
  12.2 2.0 %collective-permute-start = (bf16[16,1024]{1,0:T(8,128)(2,1)}, bf16[16,1024]{1,0:T(8,128)(2,1)S(1)}, u32[]{:S(2)}, u32[]{:S(2)}) collective-permute-start(bf16[16,1024]{1,0:T(8,128)(2,1)} %get-tuple-element.46), channel_id=1, source_target_pairs={{0,1},{1,2},{2,3},{3,4},{4,5},{5,6},{6,7},{7,8},{8,9},{9,10},{10,1... | collective-permute-start | bytes 98312 | tf_op jit(solution)/shard_map/ppermute | solution.py:444
  14.2 3.3 %collective-permute-start.1 = (bf16[16,1024]{1,0:T(8,128)(2,1)}, bf16[16,1024]{1,0:T(8,128)(2,1)S(1)}, u32[]{:S(2)}, u32[]{:S(2)}) collective-permute-start(bf16[16,1024]{1,0:T(8,128)(2,1)} %get-tuple-element.47), channel_id=1, source_target_pairs={{1,0},{2,1},{3,2},{4,3},{5,4},{6,5},{7,6},{8,7},{9,8},{10,9},{11,1... | collective-permute-start | bytes 98312 | tf_op jit(solution)/shard_map/ppermute | solution.py:444
  17.5 3.3 %cast_near.1 = (bf16[256,1024]{1,0:T(8,128)(2,1)}, bf16[512,1024]{1,0:T(8,128)(2,1)}) custom-call(s32[1]{0:T(128)} %bitcast.refs_0_.index_ref, f32[256,2048]{1,0:T(8,128)} %bitcast.49, f32[512,1024]{1,0:T(8,128)} %bitcast.51, bf16[256,128]{1,0:T(8,128)(2,1)} %get-tuple-element.45.refs_3_.refs_5_.refs_1_), custom_call_target="tpu_custom_call" | custom-call | bytes 6291456 | tf_op jit(solution)/shard_map/cast_near/pallas_call | solution.py:105
  20.8 3.6 %collective-permute-done.refs_1_.refs_3_ = bf16[16,1024]{1,0:T(8,128)(2,1)S(1)} collective-permute-done((bf16[16,1024]{1,0:T(8,128)(2,1)}, bf16[16,1024]{1,0:T(8,128)(2,1)S(1)}, u32[]{:S(2)}, u32[]{:S(2)}) %collective-permute-start) | collective-permute-done | bytes 32800 | tf_op jit(solution)/shard_map/ppermute | solution.py:444
  24.4 0.0 collective-permute-done.1.refs_3_.refs_5_
  24.4 0.2 collective-permute-done.2.refs_6_.refs_4_
  24.6 0.4 copy-done.3
  25.0 0.0 copy-done.4
  25.0 0.4 copy-done
  25.4 3.8 %convolve.1 = (f32[128,1024]{1,0:T(8,128)}, bf16[256,1024]{1,0:T(8,128)(2,1)}) custom-call(s32[1]{0:T(128)} %bitcast.refs_0_.index_ref, bf16[16,1024]{1,0:T(8,128)(2,1)} %copy-done.3, bf16[128,1024]{1,0:T(8,128)(2,1)} %refs_4_.4, bf16[16,1024]{1,0:T(8,128)(2,1)} %copy-done.4, f32[32,1024]{1,0:T(8,128)} %refs_4_.5, ...), custom_call_target="tpu_custom_call" | custom-call | flops 67108864 | bytes 2097152 | tf_op jit(solution)/shard_map/convolve/pallas_call | solution.py:105
  29.2 5.7 %all-to-all-start = ((bf16[8,32,1024]{2,1,0:T(8,128)(2,1)}), bf16[8,32,1024]{2,1,0:T(8,128)(2,1)}, u32[]{:S(2)}, u32[]{:S(2)}) async-start(bf16[8,32,1024]{2,1,0:T(8,128)(2,1)} %bitcast.63), calls=%async_computation | async-start | bytes 1048576 | tf_op jit(solution)/shard_map/all_to_all | solution.py:420
  34.9 0.5 collective-permute-start.4
  35.4 0.1 collective-permute-start.5
  35.5 1.5 %collective-permute-start.6 = (bf16[256,1024]{1,0:T(8,128)(2,1)}, bf16[256,1024]{1,0:T(8,128)(2,1)S(1)}, u32[]{:S(2)}, u32[]{:S(2)}) collective-permute-start(bf16[256,1024]{1,0:T(8,128)(2,1)} %bitcast.7.refs_6_.refs_3_), channel_id=1, source_target_pairs={{0,16},{16,0},{1,17},{17,1},{2,18},{18,2},{3,19},{19,3},{4,20},{20... | collective-permute-start | bytes 1572872 | tf_op jit(solution)/shard_map/ppermute | solution.py:432
  37.0 11.4 %all-to-all-done = bf16[8,32,1024]{2,1,0:T(8,128)(2,1)} async-done(((bf16[8,32,1024]{2,1,0:T(8,128)(2,1)}), bf16[8,32,1024]{2,1,0:T(8,128)(2,1)}, u32[]{:S(2)}, u32[]{:S(2)}) %all-to-all-start) | async-done | bytes 524320 | tf_op jit(solution)/shard_map/all_to_all | solution.py:420
  48.5 1.5 %collective-permute-start.3 = (bf16[256,1024]{1,0:T(8,128)(2,1)}, bf16[256,1024]{1,0:T(8,128)(2,1)}, u32[]{:S(2)}, u32[]{:S(2)}) collective-permute-start(bf16[256,1024]{1,0:T(8,128)(2,1)} %bitcast.5.refs_1_), channel_id=1, source_target_pairs={{0,16},{16,0},{1,17},{17,1},{2,18},{18,2},{3,19},{19,3},{4,20},{20... | collective-permute-start | bytes 1572872 | tf_op jit(solution)/shard_map/ppermute | solution.py:432
  50.0 5.1 %own_group.1 = (bf16[256,1024]{1,0:T(8,128)(2,1)}, bf16[256,1024]{1,0:T(8,128)(2,1)}, bf16[256,1024]{1,0:T(8,128)(2,1)}) custom-call(s32[1]{0:T(128)} %bitcast.refs_0_.index_ref, bf16[256,1024]{1,0:T(8,128)(2,1)} %bitcast.5.refs_1_, bf16[256,1024]{1,0:T(8,128)(2,1)} %get-tuple-element.52.refs_2_, bf16[256,1024]{1,0:T(8,128)(2,1)} %collective-permute-done.4.refs_3_, ...), custom_call_target="tpu_custom_call" | custom-call | flops 1610612736 | bytes 8388608 | tf_op jit(solution)/shard_map/own_group/pallas_call | solution.py:105
  55.1 0.0 copy-start.1
  55.1 6.2 %collective-permute-done.3.refs_1_.refs_2_ = bf16[256,1024]{1,0:T(8,128)(2,1)} collective-permute-done((bf16[256,1024]{1,0:T(8,128)(2,1)}, bf16[256,1024]{1,0:T(8,128)(2,1)}, u32[]{:S(2)}, u32[]{:S(2)}) %collective-permute-start.3) | collective-permute-done | bytes 524320 | tf_op jit(solution)/shard_map/ppermute | solution.py:432
  61.3 5.4 %far_group.1 = (bf16[256,1024]{1,0:T(8,128)(2,1)}, bf16[256,1024]{1,0:T(8,128)(2,1)}, bf16[512,1024]{1,0:T(8,128)(2,1)}) custom-call(s32[1]{0:T(128)} %bitcast.refs_0_.index_ref, bf16[256,1024]{1,0:T(8,128)(2,1)} %collective-permute-done.3.refs_1_.refs_2_, bf16[256,1024]{1,0:T(8,128)(2,1)} %get-tuple-element.52.refs_2_, ...), custom_call_target="tpu_custom_call" | custom-call | flops 1610612736 | bytes 8388608 | tf_op jit(solution)/shard_map/far_group/pallas_call | solution.py:105
  66.8 7.1 %all-to-all-start.2 = ((bf16[16,32,1024]{2,1,0:T(8,128)(2,1)}), bf16[16,32,1024]{2,1,0:T(8,128)(2,1)}, u32[]{:S(2)}, u32[]{:S(2)}) async-start(bf16[16,32,1024]{2,1,0:T(8,128)(2,1)} %bitcast.59), calls=%async_computation.2 | async-start | bytes 2097152 | tf_op jit(solution)/shard_map/all_to_all | solution.py:427
  73.9 3.9 %up_grad.1 = (bf16[512,1024]{1,0:T(8,128)(2,1)}, bf16[512,1024]{1,0:T(8,128)(2,1)}) custom-call(s32[1]{0:T(128)} %bitcast.refs_0_.index_ref, bf16[256,1024]{1,0:T(8,128)(2,1)} %bitcast.5.refs_1_, bf16[256,1024]{1,0:T(8,128)(2,1)} %collective-permute-done.3.refs_1_.refs_2_, bf16[256,1024]{1,0:T(8,128)(2,1)} %get-tuple-element.65.refs_3_, ...), custom_call_target="tpu_custom_call" | custom-call | flops 1073741824 | bytes 8388608 | tf_op jit(solution)/shard_map/up_grad/pallas_call | solution.py:105
  77.8 0.1 collective-permute-start.11
  77.8 3.8 %down_grad.1 = (bf16[512,1024]{1,0:T(8,128)(2,1)}, bf16[512,1024]{1,0:T(8,128)(2,1)}) custom-call(s32[1]{0:T(128)} %bitcast.refs_0_.index_ref, bf16[256,1024]{1,0:T(8,128)(2,1)} %get-tuple-element.56.refs_1_, bf16[256,1024]{1,0:T(8,128)(2,1)} %get-tuple-element.57.refs_2_, bf16[256,1024]{1,0:T(8,128)(2,1)} %bitcast.7.refs_6_.refs_3_, bf16[256,1024]{1,0:T(8,128)(2,1)} %copy-done.1), custom_call_target="tpu_custom_call" | custom-call | flops 1073741824 | bytes 8388608 | tf_op jit(solution)/shard_map/down_grad/pallas_call | solution.py:105
  81.7 0.6 collective-permute-start.8
  82.2 1.4 %add_convert_fusion = bf16[256,1024]{1,0:T(8,128)(2,1)S(1)} fusion(bf16[512,1024]{1,0:T(8,128)(2,1)} %collective-permute-done.11.refs_1_, bf16[512,1024]{1,0:T(8,128)(2,1)} %get-tuple-element.67.refs_0_), kind=kLoop, calls=%fused_computation | loop fusion | flops 1048576 | bytes 1572864 | tf_op jit(solution)/shard_map/convert_element_type | solution.py:569
  83.6 1.9 %collective-permute-start.12 = (bf16[256,1024]{1,0:T(8,128)(2,1)S(1)}, bf16[256,1024]{1,0:T(8,128)(2,1)}, u32[]{:S(2)}, u32[]{:S(2)}) collective-permute-start(bf16[256,1024]{1,0:T(8,128)(2,1)S(1)} %add_convert_fusion), channel_id=1, source_target_pairs={{0,16},{16,0},{1,17},{17,1},{2,18},{18,2},{3,19},{19,3},{4,20},{20... | collective-permute-start | bytes 1572872 | tf_op jit(solution)/shard_map/ppermute | solution.py:432
  85.6 0.0 collective-permute-done.8.refs_1_
  85.6 7.6 %adam_down.1 = (f32[512,1024]{1,0:T(8,128)}, bf16[512,1024]{1,0:T(8,128)(2,1)}, f32[8,512]{1,0:T(8,128)}, bf16[512,1024]{1,0:T(8,128)(2,1)}, f32[8,512]{1,0:T(8,128)}) custom-call(s32[1]{0:T(128)} %bitcast.refs_0_.index_ref, f32[512,1024]{1,0:T(8,128)} %bitcast.52, bf16[512,1024]{1,0:T(8,128)(2,1)} %bitcast.57, f32[8,512]{1,0:T(8,128)} %bitcast.66, ...), custom_call_target="tpu_custom_call" | custom-call | flops 10485760 | bytes 10485760 | tf_op jit(solution)/shard_map/adam_down/pallas_call | solution.py:393
  93.2 6.5 %all-to-all-done.2 = bf16[16,32,1024]{2,1,0:T(8,128)(2,1)} async-done(((bf16[16,32,1024]{2,1,0:T(8,128)(2,1)}), bf16[16,32,1024]{2,1,0:T(8,128)(2,1)}, u32[]{:S(2)}, u32[]{:S(2)}) %all-to-all-start.2) | async-done | bytes 1048608 | tf_op jit(solution)/shard_map/all_to_all | solution.py:427
  99.7 4.0 %taps.1 = (bf16[128,1024]{1,0:T(8,128)(2,1)}, bf16[16,1024]{1,0:T(8,128)(2,1)}, bf16[16,1024]{1,0:T(8,128)(2,1)}, f32[32,8,128]{2,1,0:T(8,128)}) custom-call(s32[1]{0:T(128)} %bitcast.refs_0_.index_ref, bf16[256,128]{1,0:T(8,128)(2,1)} %get-tuple-element.45.refs_3_.refs_5_.refs_1_, f32[128,1024]{1,0:T(8,128)} %get-tuple-element.50.refs_2_, ...), custom_call_target="tpu_custom_call" | custom-call | flops 67108864 | bytes 2097152 | tf_op jit(solution)/shard_map/taps/pallas_call | solution.py:105
  103.7 2.8 %all-to-all-start.3 = ((f32[32,8,128]{2,1,0:T(8,128)}), f32[32,8,128]{2,1,0:T(8,128)S(1)}, u32[]{:S(2)}, u32[]{:S(2)}) async-start(f32[32,8,128]{2,1,0:T(8,128)} %get-tuple-element.64), calls=%async_computation.3 | async-start | bytes 262144 | tf_op jit(solution)/shard_map/all_to_all | solution.py:452
  106.5 1.8 %collective-permute-start.9 = (bf16[16,1024]{1,0:T(8,128)(2,1)}, bf16[16,1024]{1,0:T(8,128)(2,1)S(1)}, u32[]{:S(2)}, u32[]{:S(2)}) collective-permute-start(bf16[16,1024]{1,0:T(8,128)(2,1)} %get-tuple-element.61), channel_id=1, source_target_pairs={{0,1},{1,2},{2,3},{3,4},{4,5},{5,6},{6,7},{7,8},{8,9},{9,10},{10,1... | collective-permute-start | bytes 98312 | tf_op jit(solution)/shard_map/ppermute | solution.py:444
  108.3 3.6 %collective-permute-start.10 = (bf16[16,1024]{1,0:T(8,128)(2,1)}, bf16[16,1024]{1,0:T(8,128)(2,1)S(1)}, u32[]{:S(2)}, u32[]{:S(2)}) collective-permute-start(bf16[16,1024]{1,0:T(8,128)(2,1)} %get-tuple-element.63), channel_id=1, source_target_pairs={{1,0},{2,1},{3,2},{4,3},{5,4},{6,5},{7,6},{8,7},{9,8},{10,9},{11,1... | collective-permute-start | bytes 98312 | tf_op jit(solution)/shard_map/ppermute | solution.py:444
  111.9 0.0 collective-permute-done.12.refs_2_
  111.9 7.7 %adam_up.1 = (f32[256,2048]{1,0:T(8,128)}, bf16[256,2048]{1,0:T(8,128)(2,1)}, f32[16,256]{1,0:T(8,128)}, bf16[256,2048]{1,0:T(8,128)(2,1)}, f32[16,256]{1,0:T(8,128)}) custom-call(s32[1]{0:T(128)} %bitcast.refs_0_.index_ref, f32[256,2048]{1,0:T(8,128)} %bitcast.50, bf16[256,2048]{1,0:T(8,128)(2,1)} %bitcast.60, f32[16,256]{1,0:T(8,128)} %bitcast.68, ...), custom_call_target="tpu_custom_call" | custom-call | flops 10485760 | bytes 11534336 | tf_op jit(solution)/shard_map/adam_up/pallas_call | solution.py:393
  119.7 0.0 copy-start.2
  119.7 0.5 copy-done.5
  120.2 0.0 copy-done.6
  120.2 0.1 copy-done.2
  120.3 1.6 %spread.1 = f32[32,8,128]{2,1,0:T(8,128)} custom-call(f32[32,8,128]{2,1,0:T(8,128)} %copy-done.2, f32[1,256,2048]{2,1,0:T(8,128)} %bitcast.53, bf16[16,1024]{1,0:T(8,128)(2,1)} %copy-done.5, bf16[16,1024]{1,0:T(8,128)(2,1)} %copy-done.6), custom_call_target="tpu_custom_call" | custom-call | tf_op jit(solution)/shard_map/spread/pallas_call | solution.py:105
  121.9 2.6 %all-to-all-start.4 = ((f32[32,8,128]{2,1,0:T(8,128)}), f32[32,8,128]{2,1,0:T(8,128)S(1)}, u32[]{:S(2)}, u32[]{:S(2)}) async-start(f32[32,8,128]{2,1,0:T(8,128)} %spread.1), calls=%async_computation.4 | async-start | bytes 262144 | tf_op jit(solution)/shard_map/all_to_all | solution.py:454
  124.5 3.4 %frames.1 = bf16[128,1024]{1,0:T(8,128)(2,1)} custom-call(s32[1]{0:T(128)} %bitcast.refs_0_.index_ref, bf16[16,1024]{1,0:T(8,128)(2,1)} %copy-done.5, bf16[128,1024]{1,0:T(8,128)(2,1)} %get-tuple-element.62.refs_2_, bf16[16,1024]{1,0:T(8,128)(2,1)} %copy-done.6, f32[32,1024]{1,0:T(8,128)} %refs_4_.5, bf16[128,1024]{1,0:T(8,128)(2,1)} %refs_5_.1), custom_call_target="tpu_custom_call" | custom-call | flops 67108864 | bytes 1048576 | tf_op jit(solution)/shard_map/frames/pallas_call | solution.py:105
  127.9 4.3 %all-to-all-done.4 = f32[32,8,128]{2,1,0:T(8,128)S(1)} async-done(((f32[32,8,128]{2,1,0:T(8,128)}), f32[32,8,128]{2,1,0:T(8,128)S(1)}, u32[]{:S(2)}, u32[]{:S(2)}) %all-to-all-start.4) | async-done | bytes 131104 | tf_op jit(solution)/shard_map/all_to_all | solution.py:454
  132.2 0.7 copy.28
  (16 shorter events, 0.0 us)
Async XLA Ops:
  3.4 25.8 %all-to-all-start.1 = ((bf16[8,32,1024]{2,1,0:T(8,128)(2,1)}), bf16[8,32,1024]{2,1,0:T(8,128)(2,1)}, u32[]{:S(2)}, u32[]{:S(2)}) async-start(bf16[8,32,1024]{2,1,0:T(8,128)(2,1)} %bitcast.62), calls=%async_computation.1 | async-start | bytes 1048576 | tf_op jit(solution)/shard_map/all_to_all | solution.py:420
  10.6 13.9 %collective-permute-start.2 = (bf16[256,1024]{1,0:T(8,128)(2,1)}, bf16[256,1024]{1,0:T(8,128)(2,1)S(1)}, u32[]{:S(2)}, u32[]{:S(2)}) collective-permute-start(bf16[256,1024]{1,0:T(8,128)(2,1)} %get-tuple-element.48), channel_id=1, source_target_pairs={{0,16},{16,0},{1,17},{17,1},{2,18},{18,2},{3,19},{19,3},{4,20},{20... | collective-permute-start | bytes 1572872 | tf_op jit(solution)/shard_map/ppermute | solution.py:432
  12.2 12.2 %collective-permute-start = (bf16[16,1024]{1,0:T(8,128)(2,1)}, bf16[16,1024]{1,0:T(8,128)(2,1)S(1)}, u32[]{:S(2)}, u32[]{:S(2)}) collective-permute-start(bf16[16,1024]{1,0:T(8,128)(2,1)} %get-tuple-element.46), channel_id=1, source_target_pairs={{0,1},{1,2},{2,3},{3,4},{4,5},{5,6},{6,7},{7,8},{8,9},{9,10},{10,1... | collective-permute-start | bytes 98312 | tf_op jit(solution)/shard_map/ppermute | solution.py:444
  14.2 10.2 %collective-permute-start.1 = (bf16[16,1024]{1,0:T(8,128)(2,1)}, bf16[16,1024]{1,0:T(8,128)(2,1)S(1)}, u32[]{:S(2)}, u32[]{:S(2)}) collective-permute-start(bf16[16,1024]{1,0:T(8,128)(2,1)} %get-tuple-element.47), channel_id=1, source_target_pairs={{1,0},{2,1},{3,2},{4,3},{5,4},{6,5},{7,6},{8,7},{9,8},{10,9},{11,1... | collective-permute-start | bytes 98312 | tf_op jit(solution)/shard_map/ppermute | solution.py:444
  24.4 0.6 copy-start.3
  24.4 0.6 copy-start.4
  24.6 0.8 copy-start
  29.2 19.3 %all-to-all-start = ((bf16[8,32,1024]{2,1,0:T(8,128)(2,1)}), bf16[8,32,1024]{2,1,0:T(8,128)(2,1)}, u32[]{:S(2)}, u32[]{:S(2)}) async-start(bf16[8,32,1024]{2,1,0:T(8,128)(2,1)} %bitcast.63), calls=%async_computation | async-start | bytes 1048576 | tf_op jit(solution)/shard_map/all_to_all | solution.py:420
  34.9 15.1 %collective-permute-start.7 = (bf16[512,1024]{1,0:T(8,128)(2,1)}, bf16[512,1024]{1,0:T(8,128)(2,1)}, u32[]{:S(2)}, u32[]{:S(2)}) collective-permute-start(bf16[512,1024]{1,0:T(8,128)(2,1)} %get-tuple-element.49.refs_7_), channel_id=1, source_target_pairs={{0,8},{8,0},{1,9},{9,1},{2,10},{10,2},{3,11},{11,3},{4,12},{12,4},... | collective-permute-start | bytes 3145736 | tf_op jit(solution)/shard_map/ppermute | solution.py:436
  34.9 15.0 %collective-permute-start.4 = (bf16[256,1024]{1,0:T(8,128)(2,1)}, bf16[256,1024]{1,0:T(8,128)(2,1)}, u32[]{:S(2)}, u32[]{:S(2)}) collective-permute-start(bf16[256,1024]{1,0:T(8,128)(2,1)} %get-tuple-element.52.refs_2_), channel_id=1, source_target_pairs={{0,8},{8,0},{1,9},{9,1},{2,10},{10,2},{3,11},{11,3},{4,12},{12,4},... | collective-permute-start | bytes 1572872 | tf_op jit(solution)/shard_map/ppermute | solution.py:436
  35.4 14.5 %collective-permute-start.5 = (bf16[256,1024]{1,0:T(8,128)(2,1)}, bf16[256,1024]{1,0:T(8,128)(2,1)}, u32[]{:S(2)}, u32[]{:S(2)}) collective-permute-start(bf16[256,1024]{1,0:T(8,128)(2,1)} %copy-done), channel_id=1, source_target_pairs={{0,8},{8,0},{1,9},{9,1},{2,10},{10,2},{3,11},{11,3},{4,12},{12,4},... | collective-permute-start | bytes 1572872 | tf_op jit(solution)/shard_map/ppermute | solution.py:436
  35.5 19.6 %collective-permute-start.6 = (bf16[256,1024]{1,0:T(8,128)(2,1)}, bf16[256,1024]{1,0:T(8,128)(2,1)S(1)}, u32[]{:S(2)}, u32[]{:S(2)}) collective-permute-start(bf16[256,1024]{1,0:T(8,128)(2,1)} %bitcast.7.refs_6_.refs_3_), channel_id=1, source_target_pairs={{0,16},{16,0},{1,17},{17,1},{2,18},{18,2},{3,19},{19,3},{4,20},{20... | collective-permute-start | bytes 1572872 | tf_op jit(solution)/shard_map/ppermute | solution.py:432
  48.5 12.9 %collective-permute-start.3 = (bf16[256,1024]{1,0:T(8,128)(2,1)}, bf16[256,1024]{1,0:T(8,128)(2,1)}, u32[]{:S(2)}, u32[]{:S(2)}) collective-permute-start(bf16[256,1024]{1,0:T(8,128)(2,1)} %bitcast.5.refs_1_), channel_id=1, source_target_pairs={{0,16},{16,0},{1,17},{17,1},{2,18},{18,2},{3,19},{19,3},{4,20},{20... | collective-permute-start | bytes 1572872 | tf_op jit(solution)/shard_map/ppermute | solution.py:432
  55.1 6.2 %copy-start.1 = (bf16[256,1024]{1,0:T(8,128)(2,1)}, bf16[256,1024]{1,0:T(8,128)(2,1)S(1)}, u32[]{:S(2)}) copy-start(bf16[256,1024]{1,0:T(8,128)(2,1)S(1)} %collective-permute-done.6.refs_6_.refs_4_) | copy-start | bytes 1572868
  66.8 32.9 %all-to-all-start.2 = ((bf16[16,32,1024]{2,1,0:T(8,128)(2,1)}), bf16[16,32,1024]{2,1,0:T(8,128)(2,1)}, u32[]{:S(2)}, u32[]{:S(2)}) async-start(bf16[16,32,1024]{2,1,0:T(8,128)(2,1)} %bitcast.59), calls=%async_computation.2 | async-start | bytes 2097152 | tf_op jit(solution)/shard_map/all_to_all | solution.py:427
  77.8 4.5 %collective-permute-start.11 = (bf16[512,1024]{1,0:T(8,128)(2,1)}, bf16[512,1024]{1,0:T(8,128)(2,1)}, u32[]{:S(2)}, u32[]{:S(2)}) collective-permute-start(bf16[512,1024]{1,0:T(8,128)(2,1)} %get-tuple-element.68), channel_id=1, source_target_pairs={{0,8},{8,0},{1,9},{9,1},{2,10},{10,2},{3,11},{11,3},{4,12},{12,4},... | collective-permute-start | bytes 3145736 | tf_op jit(solution)/shard_map/ppermute | solution.py:436
  81.7 3.9 %collective-permute-start.8 = (bf16[512,1024]{1,0:T(8,128)(2,1)}, bf16[512,1024]{1,0:T(8,128)(2,1)}, u32[]{:S(2)}, u32[]{:S(2)}) collective-permute-start(bf16[512,1024]{1,0:T(8,128)(2,1)} %get-tuple-element.59), channel_id=1, source_target_pairs={{0,8},{8,0},{1,9},{9,1},{2,10},{10,2},{3,11},{11,3},{4,12},{12,4},... | collective-permute-start | bytes 3145736 | tf_op jit(solution)/shard_map/ppermute | solution.py:436
  83.6 28.2 %collective-permute-start.12 = (bf16[256,1024]{1,0:T(8,128)(2,1)S(1)}, bf16[256,1024]{1,0:T(8,128)(2,1)}, u32[]{:S(2)}, u32[]{:S(2)}) collective-permute-start(bf16[256,1024]{1,0:T(8,128)(2,1)S(1)} %add_convert_fusion), channel_id=1, source_target_pairs={{0,16},{16,0},{1,17},{17,1},{2,18},{18,2},{3,19},{19,3},{4,20},{20... | collective-permute-start | bytes 1572872 | tf_op jit(solution)/shard_map/ppermute | solution.py:432
  103.7 15.9 %all-to-all-start.3 = ((f32[32,8,128]{2,1,0:T(8,128)}), f32[32,8,128]{2,1,0:T(8,128)S(1)}, u32[]{:S(2)}, u32[]{:S(2)}) async-start(f32[32,8,128]{2,1,0:T(8,128)} %get-tuple-element.64), calls=%async_computation.3 | async-start | bytes 262144 | tf_op jit(solution)/shard_map/all_to_all | solution.py:452
  106.5 13.1 %collective-permute-start.9 = (bf16[16,1024]{1,0:T(8,128)(2,1)}, bf16[16,1024]{1,0:T(8,128)(2,1)S(1)}, u32[]{:S(2)}, u32[]{:S(2)}) collective-permute-start(bf16[16,1024]{1,0:T(8,128)(2,1)} %get-tuple-element.61), channel_id=1, source_target_pairs={{0,1},{1,2},{2,3},{3,4},{4,5},{5,6},{6,7},{7,8},{8,9},{9,10},{10,1... | collective-permute-start | bytes 98312 | tf_op jit(solution)/shard_map/ppermute | solution.py:444
  108.3 11.3 %collective-permute-start.10 = (bf16[16,1024]{1,0:T(8,128)(2,1)}, bf16[16,1024]{1,0:T(8,128)(2,1)S(1)}, u32[]{:S(2)}, u32[]{:S(2)}) collective-permute-start(bf16[16,1024]{1,0:T(8,128)(2,1)} %get-tuple-element.63), channel_id=1, source_target_pairs={{1,0},{2,1},{3,2},{4,3},{5,4},{6,5},{7,6},{8,7},{9,8},{10,9},{11,1... | collective-permute-start | bytes 98312 | tf_op jit(solution)/shard_map/ppermute | solution.py:444
  119.6 0.6 copy-start.5
  119.6 0.6 copy-start.6
  119.7 0.7 copy-start.2
  121.9 10.3 %all-to-all-start.4 = ((f32[32,8,128]{2,1,0:T(8,128)}), f32[32,8,128]{2,1,0:T(8,128)S(1)}, u32[]{:S(2)}, u32[]{:S(2)}) async-start(f32[32,8,128]{2,1,0:T(8,128)} %spread.1), calls=%async_computation.4 | async-start | bytes 262144 | tf_op jit(solution)/shard_map/all_to_all | solution.py:454

commit v5 on v4

--- a/solution.py
+++ b/solution.py
@@ -18,7 +18,7 @@
 
 f32 = jnp.float32
 bf16 = jnp.bfloat16
-MIB = 1 << 20
+VMEM_BYTES = 127 << 19
 
 
 def swish_parts(values):
@@ -56,7 +56,7 @@
     for count in counts:
         groups.append(refs[:count])
         refs = refs[count:]
-    scalars, resident, sources, _, targets, held, made, scratch = groups
+    scalars, sources, _, targets, held, made, scratch = groups
     in_sems, out_sems = refs
     arriving = []
     for index, source in enumerate(sources):
@@ -77,7 +77,7 @@
         leaving[index] = pltpu.make_async_copy(made[index], targets[index], out_sems.at[index])
         leaving[index].start()
 
-    kernel(scalars + resident, take, made, give, scratch)
+    kernel(scalars, take, made, give, scratch)
     for index in range(len(targets)):
         if index not in leaving:
             give(index)
@@ -87,9 +87,8 @@
         copy.wait()
 
 
-def call(kernel, name, scalars, inputs, outs, scratch=(), after=(), resident=(), flops=0, moved=0, limit=63):
+def call(kernel, name, scalars, inputs, outs, scratch=(), after=(), flops=0, moved=0):
     hbm = pl.BlockSpec(memory_space=pl.ANY)
-    vmem = pl.BlockSpec(memory_space=pltpu.VMEM)
     smem = pl.BlockSpec(memory_space=pltpu.SMEM)
     pairs = [item if isinstance(item, tuple) else (item, None) for item in inputs]
     arrays = [array for array, _ in pairs]
@@ -99,24 +98,21 @@
         for array, span in pairs
     ]
     made = [pltpu.VMEM(shape, kind) for shape, kind in outs]
-    counts = (
-        len(scalars), len(resident), len(arrays), len(after), len(outs), len(held), len(made), len(scratch)
-    )
+    counts = (len(scalars), len(arrays), len(after), len(outs), len(held), len(made), len(scratch))
     return pl.pallas_call(
         functools.partial(staged, kernel, counts, spans),
         out_shape=[jax.ShapeDtypeStruct(shape, kind) for shape, kind in outs],
         in_specs=[smem] * len(scalars)
-        + [vmem] * len(resident)
         + [hbm] * (len(arrays) + len(after)),
         out_specs=[hbm] * len(outs),
         scratch_shapes=held
         + made
         + list(scratch)
         + [pltpu.SemaphoreType.DMA((len(arrays),)), pltpu.SemaphoreType.DMA((len(outs),))],
-        compiler_params=pltpu.CompilerParams(vmem_limit_bytes=limit * MIB),
+        compiler_params=pltpu.CompilerParams(vmem_limit_bytes=VMEM_BYTES),
         cost_estimate=pl.CostEstimate(flops=flops, bytes_accessed=moved, transcendentals=0),
         name=name,
-    )(*scalars, *resident, *arrays, *after)
+    )(*scalars, *arrays, *after)
 
 
 def prepare_kernel(here, experts, capacity, scalars, take, made, give, scratch):
@@ -172,20 +168,55 @@
     return total
 
 
-def conv_kernel(here, scalars, take, made, give, scratch):
+def conv_kernel(scalars, take, made, give, scratch):
+    (total_ref,) = made
+    pad_ref, shift_ref = scratch
+    frames, taps_ref = take(0), take(1)
+    length, width = frames.shape
+    side = taps_ref.shape[0] // 2
+    pad_ref[:side, :] = jnp.zeros((side, 128), f32)
+    pad_ref[side + length :, :] = jnp.zeros((side + 8, 128), f32)
+
+    def lanes(step, carry):
+        cols = at(step, 128)
+        pad_ref[side : side + length, :] = frames[:, cols].astype(f32)
+        weights = [taps_ref[tap : tap + 1, cols] for tap in range(taps_ref.shape[0])]
+        total_ref[:, cols] = slide(pad_ref, shift_ref, weights, length)
+        return carry
+
+    lax.fori_loop(0, width // 128, lanes, 0)
+
+
+def edge_kernel(here, scalars, take, made, give, scratch):
     slope_ref, out_ref = made
     pad_ref, shift_ref, feat_ref = scratch
     place = here(scalars[0])
-    left, frames, right, taps_ref = take(0), take(1), take(2), take(3)
+    left, right, total_ref, taps_ref = take(0), take(1), take(2), take(3)
     length, width = feat_ref.shape
+    side = left.shape[0]
+    count = taps_ref.shape[0]
+    pad_ref[: 4 * side + 8, :] = jnp.zeros((4 * side + 8, 128), f32)
 
     def lanes(step, carry):
         cols = at(step, 128)
-        fill_padded(pad_ref, place, left, frames, right, cols)
-        weights = [taps_ref[tap : tap + 1, cols] for tap in range(taps_ref.shape[0])]
-        active, slope = swish_parts(slide(pad_ref, shift_ref, weights, length))
-        slope_ref[:, cols] = slope
-        feat_ref[:, cols] = active.astype(bf16)
+        weights = [taps_ref[tap : tap + 1, cols] for tap in range(count)]
+        pad_ref[0:side, :] = left[:, cols].astype(f32) * place.first
+        head = slide(pad_ref, shift_ref, weights[:side] + [None] * side, side)
+        pad_ref[0:side, :] = jnp.zeros((side, 128), f32)
+        pad_ref[2 * side : 3 * side, :] = right[:, cols].astype(f32) * place.last
+        tail = slide(pad_ref, shift_ref, [None] * (side + 1) + weights[side + 1 :], side)
+        pad_ref[2 * side : 3 * side, :] = jnp.zeros((side, 128), f32)
+        for rows, extra in (
+            (slice(0, side), head),
+            (slice(side, length - side), None),
+            (slice(length - side, length), tail),
+        ):
+            total = total_ref[rows, cols]
+            if extra is not None:
+                total = total + extra
+            active, slope = swish_parts(total)
+            slope_ref[rows, cols] = slope
+            feat_ref[rows, cols] = active.astype(bf16)
         return carry
 
     lax.fori_loop(0, width // 128, lanes, 0)
@@ -334,7 +365,7 @@
 ):
     keep_ref, theirs_ref, far_refs, refs = refs[0], refs[1], refs[2 : 2 + sums], refs[2 + sums :]
     next_ref, mean_next_ref, mean_top_ref, square_next_ref, square_top_ref = refs[:5]
-    scales_ref, tops_ref, grad_ref = refs[5:]
+    split_ref, spread_ref, tops_ref, grad_ref = refs[5:]
     rows, width = master_ref.shape
     blocks = mean_scale_ref.shape[0]
     size = width // blocks
@@ -344,8 +375,17 @@
 
     @pl.when(step == 0)
     def _():
-        scales_ref[0, :, :blocks] = mean_scale_ref[...].T
-        scales_ref[1, :, :blocks] = square_scale_ref[...].T
+        lane = lax.broadcasted_iota(jnp.int32, (128, width), 0)
+        entry = lax.broadcasted_iota(jnp.int32, (128, width), 1)
+        chosen = (lax.rem(lane, blocks) == entry // size) & (lane < 3 * blocks)
+        spread_ref[...] = chosen.astype(f32).astype(bf16)
+        split_ref[...] = jnp.zeros_like(split_ref)
+        for kind, scale_ref in enumerate((mean_scale_ref, square_scale_ref)):
+            rest = scale_ref[...]
+            for term in range(3):
+                piece = rest.astype(bf16).astype(f32)
+                split_ref[kind, :, term * blocks : (term + 1) * blocks] = piece.T
+                rest = rest - piece
 
     place = here(index_ref)
     near = slice(0, width) if units == width else at(place.chip, units)
@@ -354,16 +394,20 @@
         grad_ref[:, at(place.came[index + 1], units)] = far_ref[...].astype(f32)
 
     part = at(step, rows)
-    mean_scales = scales_ref[0, part, :]
-    square_scales = scales_ref[1, part, :]
+    mean_scales, square_scales = [
+        jnp.dot(
+            split_ref[kind, part, :].astype(bf16), spread_ref[...], preferred_element_type=f32
+        )
+        for kind in range(2)
+    ]
     for block in range(blocks):
         cols = slice(block * size, (block + 1) * size)
         grad = grad_ref[:, cols]
         mean = beta_one * (
-            mean_ref[:, cols].astype(f32) * mean_scales[:, block : block + 1]
+            mean_ref[:, cols].astype(f32) * mean_scales[:, cols]
         ) + (1.0 - beta_one) * grad
         square = beta_two * (
-            square_ref[:, cols].astype(f32) * square_scales[:, block : block + 1]
+            square_ref[:, cols].astype(f32) * square_scales[:, cols]
         ) + (1.0 - beta_two) * (grad * grad)
         root = jnp.sqrt(square * (1.0 / bias_two)) + adam_eps
         next_ref[:, cols] = master_ref[:, cols] - (learn_rate / bias_one) * (mean / root)
@@ -398,10 +442,11 @@
         out_specs=[tile, tile, whole, tile, whole],
         scratch_shapes=[
             pltpu.VMEM((2, rows, 128), f32),
+            pltpu.VMEM((128, width), bf16),
             pltpu.VMEM((2, rows, 128), f32),
             pltpu.VMEM((part, width), f32),
         ],
-        compiler_params=pltpu.CompilerParams(vmem_limit_bytes=63 * MIB),
+        compiler_params=pltpu.CompilerParams(vmem_limit_bytes=VMEM_BYTES),
         cost_estimate=pl.CostEstimate(
             flops=20 * rows * width,
             bytes_accessed=(16 + 2 * len(grads)) * rows * width,
@@ -514,11 +559,22 @@
     for arrived in far_ups:
         ups = ups + [arrived, to_core(arrived)]
     grads_in = by_expert(send_grads)
+    (inner,) = call(
+        conv_kernel,
+        "convolve",
+        [],
+        [frames, conv_weight],
+        [((length, width), f32)],
+        scratch=strips,
+        after=[down_own],
+        flops=2 * slots * length * width,
+        moved=8 * slots * width,
+    )
     slope, send_rows = call(
-        functools.partial(conv_kernel, here),
-        "convolve",
+        functools.partial(edge_kernel, here),
+        "edges",
         [index],
-        [left, frames, right, conv_weight, place],
+        [left, right, inner, conv_weight, place],
         [((length, width), f32), row_shape],
         after=far_ups + [down_own],
         scratch=strips + [pltpu.VMEM((length, width), bf16)],

time: 134 us -> 132 us (0.985)
  waiting for transfers between devices: 32.2 us -> 28.7 us
  Pallas kernels: 52.4 us -> 54.3 us
    ppermute x4, waiting for transfers between devices: 3.57 us -> 0.29 us  [halo(): return (lax.ppermute(tail, axes, right), lax.ppermute(head, axes, left))]
    pallas_call x10 -> x11, Pallas kernels: 37.1 us -> 39.7 us  [call(): pl.pallas_call(functools.partial(staged, kernel, counts, spans), out_shap...]
  transfers between devices with their start and end apart: 18 -> 18, of which waited for: 6 -> 6; matrix products, arithmetic and copies ran while one was open for 1% -> 2% of each run, Pallas kernels for 32% -> 34%
where the time goes in v5:
time: 132 us; the launch traced here: 131 us
  Pallas kernels  54.3 us (41%)
  starting transfers between devices  43.4 us (33%)
  waiting for transfers between devices  28.7 us (22%)
  other arithmetic  2.19 us (2%)
  local copies, waits for them, and re-layouts  1.68 us (1%)
    pallas_call x11, Pallas kernels, call(): pl.pallas_call(functools.partial(staged, kernel, counts, spans), out_shap...  39.7 us
    pallas_call x2, Pallas kernels, adam(): pl.pallas_call(functools.partial(adam_kernel, here, len(grads) - 2), grid...  14.5 us
    all_to_all x2, starting transfers between devices, by_expert(): lax.all_to_all(cells, 'expert', 0, 0, tiled=True).reshape(slots, width)  12.7 us
    all_to_all x2, waiting for transfers between devices, by_expert(): lax.all_to_all(cells, 'expert', 0, 0, tiled=True).reshape(slots, width)  12 us
    ppermute x4, starting transfers between devices, halo(): return (lax.ppermute(tail, axes, right), lax.ppermute(head, axes, left))  10.7 us
    all_to_all x1, starting transfers between devices, to_senders(): return lax.all_to_all(cells, axes, 0, 0, tiled=True).reshape(rows.shape)  6.98 us
    ppermute x4, starting transfers between devices, to_chip(): lax.ppermute(values, 'chip', [(i, (i + shift) % chips) for i in range(chi...  6.43 us
    ppermute x4, waiting for transfers between devices, to_chip(): lax.ppermute(values, 'chip', [(i, (i + shift) % chips) for i in range(chi...  6.14 us
  transfers between devices with their start and end apart: 18, of which 6 were waited for; matrix products, arithmetic and copies ran while one was open for 2% of the time, Pallas kernels for 34%

profile of v5, /device:TPU:0, one launch (start us, length us, event | category | flops | bytes accessed | tf_op | source)
XLA Modules:
  0.0 131.1 jit_solution(5344964183518896038)
XLA Ops:
  0.7 2.7 %prepare.1 = (bf16[16,1024]{1,0:T(8,128)(2,1)}, bf16[16,1024]{1,0:T(8,128)(2,1)}, bf16[256,128]{1,0:T(8,128)(2,1)}, bf16[256,1024]{1,0:T(8,128)(2,1)}, bf16[256,1024]{1,0:T(8,128)(2,1)}) custom-call(s32[1]{0:T(128)} %bitcast.refs_0_.index_ref, s32[1,128]{1,0:T(1,128)} %bitcast.70, bf16[128,1024]{1,0:T(8,128)(2,1)} %refs_5_.1, bf16[128,1024]{1,0:T(8,128)(2,1)} %refs_4_.4, ...), custom_call_target="tpu_custom_call" | custom-call | flops 67108864 | bytes 1048576 | tf_op jit(solution)/shard_map/prepare/pallas_call | solution.py:102
  3.4 7.3 %all-to-all-start.1 = ((bf16[8,32,1024]{2,1,0:T(8,128)(2,1)}), bf16[8,32,1024]{2,1,0:T(8,128)(2,1)}, u32[]{:S(2)}, u32[]{:S(2)}) async-start(bf16[8,32,1024]{2,1,0:T(8,128)(2,1)} %bitcast.62), calls=%async_computation.1 | async-start | bytes 1048576 | tf_op jit(solution)/shard_map/all_to_all | solution.py:465
  10.6 1.5 %collective-permute-start.2 = (bf16[256,1024]{1,0:T(8,128)(2,1)}, bf16[256,1024]{1,0:T(8,128)(2,1)}, u32[]{:S(2)}, u32[]{:S(2)}) collective-permute-start(bf16[256,1024]{1,0:T(8,128)(2,1)} %get-tuple-element.49), channel_id=1, source_target_pairs={{0,16},{16,0},{1,17},{17,1},{2,18},{18,2},{3,19},{19,3},{4,20},{20... | collective-permute-start | bytes 1572872 | tf_op jit(solution)/shard_map/ppermute | solution.py:477
  12.2 2.0 %collective-permute-start = (bf16[16,1024]{1,0:T(8,128)(2,1)}, bf16[16,1024]{1,0:T(8,128)(2,1)S(1)}, u32[]{:S(2)}, u32[]{:S(2)}) collective-permute-start(bf16[16,1024]{1,0:T(8,128)(2,1)} %get-tuple-element.46), channel_id=1, source_target_pairs={{0,1},{1,2},{2,3},{3,4},{4,5},{5,6},{6,7},{7,8},{8,9},{9,10},{10,1... | collective-permute-start | bytes 98312 | tf_op jit(solution)/shard_map/ppermute | solution.py:489
  14.2 3.3 %collective-permute-start.1 = (bf16[16,1024]{1,0:T(8,128)(2,1)}, bf16[16,1024]{1,0:T(8,128)(2,1)S(1)}, u32[]{:S(2)}, u32[]{:S(2)}) collective-permute-start(bf16[16,1024]{1,0:T(8,128)(2,1)} %get-tuple-element.47), channel_id=1, source_target_pairs={{1,0},{2,1},{3,2},{4,3},{5,4},{6,5},{7,6},{8,7},{9,8},{10,9},{11,1... | collective-permute-start | bytes 98312 | tf_op jit(solution)/shard_map/ppermute | solution.py:489
  17.5 3.3 %cast_near.1 = (bf16[256,1024]{1,0:T(8,128)(2,1)}, bf16[512,1024]{1,0:T(8,128)(2,1)}) custom-call(s32[1]{0:T(128)} %bitcast.refs_0_.index_ref, f32[256,2048]{1,0:T(8,128)} %bitcast.49, f32[512,1024]{1,0:T(8,128)} %bitcast.51, bf16[256,128]{1,0:T(8,128)(2,1)} %get-tuple-element.45.refs_3_.refs_5_.refs_1_), custom_call_target="tpu_custom_call" | custom-call | bytes 6291456 | tf_op jit(solution)/shard_map/cast_near/pallas_call | solution.py:102
  20.8 3.3 %convolve.1.refs_3_ = f32[128,1024]{1,0:T(8,128)} custom-call(bf16[128,1024]{1,0:T(8,128)(2,1)} %refs_4_.4, f32[32,1024]{1,0:T(8,128)} %refs_4_.5, bf16[512,1024]{1,0:T(8,128)(2,1)} %get-tuple-element.48.refs_2_.refs_7_), custom_call_target="tpu_custom_call" | custom-call | flops 67108864 | bytes 2097152 | tf_op jit(solution)/shard_map/convolve/pallas_call | solution.py:102
  24.1 0.3 collective-permute-done.refs_1_.refs_3_
  24.4 0.0 collective-permute-done.1.refs_2_.refs_5_
  24.4 0.3 collective-permute-done.2.refs_6_.refs_4_
  24.7 0.3 copy-done.1
  25.0 0.0 copy-done.2
  25.0 3.2 %edges.1 = (f32[128,1024]{1,0:T(8,128)}, bf16[256,1024]{1,0:T(8,128)(2,1)}) custom-call(s32[1]{0:T(128)} %bitcast.refs_0_.index_ref, bf16[16,1024]{1,0:T(8,128)(2,1)} %copy-done.1, bf16[16,1024]{1,0:T(8,128)(2,1)} %copy-done.2, f32[128,1024]{1,0:T(8,128)} %convolve.1.refs_3_, f32[32,1024]{1,0:T(8,128)} %refs_4_.5, ...), custom_call_target="tpu_custom_call" | custom-call | flops 67108864 | bytes 2097152 | tf_op jit(solution)/shard_map/edges/pallas_call | solution.py:102
  28.2 5.4 %all-to-all-start = ((bf16[8,32,1024]{2,1,0:T(8,128)(2,1)}), bf16[8,32,1024]{2,1,0:T(8,128)(2,1)}, u32[]{:S(2)}, u32[]{:S(2)}) async-start(bf16[8,32,1024]{2,1,0:T(8,128)(2,1)} %bitcast.63), calls=%async_computation | async-start | bytes 1048576 | tf_op jit(solution)/shard_map/all_to_all | solution.py:465
  33.6 0.0 collective-permute-start.7
  33.6 0.5 collective-permute-start.4
  34.1 0.1 collective-permute-start.5
  34.2 1.5 %collective-permute-start.6 = (bf16[256,1024]{1,0:T(8,128)(2,1)}, bf16[256,1024]{1,0:T(8,128)(2,1)}, u32[]{:S(2)}, u32[]{:S(2)}) collective-permute-start(bf16[256,1024]{1,0:T(8,128)(2,1)} %bitcast.7.refs_6_.refs_3_), channel_id=1, source_target_pairs={{0,16},{16,0},{1,17},{17,1},{2,18},{18,2},{3,19},{19,3},{4,20},{20... | collective-permute-start | bytes 1572872 | tf_op jit(solution)/shard_map/ppermute | solution.py:477
  35.7 12.0 %all-to-all-done = bf16[8,32,1024]{2,1,0:T(8,128)(2,1)} async-done(((bf16[8,32,1024]{2,1,0:T(8,128)(2,1)}), bf16[8,32,1024]{2,1,0:T(8,128)(2,1)}, u32[]{:S(2)}, u32[]{:S(2)}) %all-to-all-start) | async-done | bytes 524320 | tf_op jit(solution)/shard_map/all_to_all | solution.py:465
  47.7 1.5 %collective-permute-start.3 = (bf16[256,1024]{1,0:T(8,128)(2,1)}, bf16[256,1024]{1,0:T(8,128)(2,1)}, u32[]{:S(2)}, u32[]{:S(2)}) collective-permute-start(bf16[256,1024]{1,0:T(8,128)(2,1)} %bitcast.5.refs_1_), channel_id=1, source_target_pairs={{0,16},{16,0},{1,17},{17,1},{2,18},{18,2},{3,19},{19,3},{4,20},{20... | collective-permute-start | bytes 1572872 | tf_op jit(solution)/shard_map/ppermute | solution.py:477
  49.2 0.0 collective-permute-done.4.refs_3_
  49.2 5.1 %own_group.1 = (bf16[256,1024]{1,0:T(8,128)(2,1)}, bf16[256,1024]{1,0:T(8,128)(2,1)}, bf16[256,1024]{1,0:T(8,128)(2,1)}) custom-call(s32[1]{0:T(128)} %bitcast.refs_0_.index_ref, bf16[256,1024]{1,0:T(8,128)(2,1)} %bitcast.5.refs_1_, bf16[256,1024]{1,0:T(8,128)(2,1)} %get-tuple-element.52.refs_2_, bf16[256,1024]{1,0:T(8,128)(2,1)} %collective-permute-done.4.refs_3_, ...), custom_call_target="tpu_custom_call" | custom-call | flops 1610612736 | bytes 8388608 | tf_op jit(solution)/shard_map/own_group/pallas_call | solution.py:102
  54.3 0.0 collective-permute-done.6.refs_6_.refs_4_
  54.3 5.9 %collective-permute-done.3.refs_1_.refs_2_ = bf16[256,1024]{1,0:T(8,128)(2,1)} collective-permute-done((bf16[256,1024]{1,0:T(8,128)(2,1)}, bf16[256,1024]{1,0:T(8,128)(2,1)}, u32[]{:S(2)}, u32[]{:S(2)}) %collective-permute-start.3) | collective-permute-done | bytes 524320 | tf_op jit(solution)/shard_map/ppermute | solution.py:477
  60.1 5.4 %far_group.1 = (bf16[256,1024]{1,0:T(8,128)(2,1)}, bf16[256,1024]{1,0:T(8,128)(2,1)}, bf16[512,1024]{1,0:T(8,128)(2,1)}) custom-call(s32[1]{0:T(128)} %bitcast.refs_0_.index_ref, bf16[256,1024]{1,0:T(8,128)(2,1)} %collective-permute-done.3.refs_1_.refs_2_, bf16[256,1024]{1,0:T(8,128)(2,1)} %get-tuple-element.52.refs_2_, ...), custom_call_target="tpu_custom_call" | custom-call | flops 1610612736 | bytes 8388608 | tf_op jit(solution)/shard_map/far_group/pallas_call | solution.py:102
  65.6 7.0 %all-to-all-start.2 = ((bf16[16,32,1024]{2,1,0:T(8,128)(2,1)}), bf16[16,32,1024]{2,1,0:T(8,128)(2,1)}, u32[]{:S(2)}, u32[]{:S(2)}) async-start(bf16[16,32,1024]{2,1,0:T(8,128)(2,1)} %bitcast.59), calls=%async_computation.2 | async-start | bytes 2097152 | tf_op jit(solution)/shard_map/all_to_all | solution.py:472
  72.6 3.8 %up_grad.1 = (bf16[512,1024]{1,0:T(8,128)(2,1)}, bf16[512,1024]{1,0:T(8,128)(2,1)}) custom-call(s32[1]{0:T(128)} %bitcast.refs_0_.index_ref, bf16[256,1024]{1,0:T(8,128)(2,1)} %bitcast.5.refs_1_, bf16[256,1024]{1,0:T(8,128)(2,1)} %collective-permute-done.3.refs_1_.refs_2_, bf16[256,1024]{1,0:T(8,128)(2,1)} %get-tuple-element.65.refs_3_, ...), custom_call_target="tpu_custom_call" | custom-call | flops 1073741824 | bytes 8388608 | tf_op jit(solution)/shard_map/up_grad/pallas_call | solution.py:102
  76.4 0.1 collective-permute-start.11
  76.5 3.8 %down_grad.1 = (bf16[512,1024]{1,0:T(8,128)(2,1)}, bf16[512,1024]{1,0:T(8,128)(2,1)}) custom-call(s32[1]{0:T(128)} %bitcast.refs_0_.index_ref, bf16[256,1024]{1,0:T(8,128)(2,1)} %get-tuple-element.56.refs_1_, bf16[256,1024]{1,0:T(8,128)(2,1)} %get-tuple-element.57.refs_2_, bf16[256,1024]{1,0:T(8,128)(2,1)} %bitcast.7.refs_6_.refs_3_, ...), custom_call_target="tpu_custom_call" | custom-call | flops 1073741824 | bytes 8388608 | tf_op jit(solution)/shard_map/down_grad/pallas_call | solution.py:102
  80.3 0.6 collective-permute-start.8
  80.9 2.2 %add_convert_fusion = bf16[256,1024]{1,0:T(8,128)(2,1)} fusion(bf16[512,1024]{1,0:T(8,128)(2,1)} %collective-permute-done.11.refs_1_, bf16[512,1024]{1,0:T(8,128)(2,1)} %get-tuple-element.67.refs_0_), kind=kLoop, calls=%fused_computation | loop fusion | flops 1048576 | bytes 1572864 | tf_op jit(solution)/shard_map/convert_element_type | solution.py:625
  83.1 1.9 %collective-permute-start.12 = (bf16[256,1024]{1,0:T(8,128)(2,1)}, bf16[256,1024]{1,0:T(8,128)(2,1)}, u32[]{:S(2)}, u32[]{:S(2)}) collective-permute-start(bf16[256,1024]{1,0:T(8,128)(2,1)} %add_convert_fusion), channel_id=1, source_target_pairs={{0,16},{16,0},{1,17},{17,1},{2,18},{18,2},{3,19},{19,3},{4,20},{20... | collective-permute-start | bytes 1572872 | tf_op jit(solution)/shard_map/ppermute | solution.py:477
  85.0 7.3 %adam_down.1 = (f32[512,1024]{1,0:T(8,128)}, bf16[512,1024]{1,0:T(8,128)(2,1)}, f32[8,512]{1,0:T(8,128)}, bf16[512,1024]{1,0:T(8,128)(2,1)}, f32[8,512]{1,0:T(8,128)}) custom-call(s32[1]{0:T(128)} %bitcast.refs_0_.index_ref, f32[512,1024]{1,0:T(8,128)} %bitcast.52, bf16[512,1024]{1,0:T(8,128)(2,1)} %bitcast.57, f32[8,512]{1,0:T(8,128)} %bitcast.66, ...), custom_call_target="tpu_custom_call" | custom-call | flops 10485760 | bytes 10485760 | tf_op jit(solution)/shard_map/adam_down/pallas_call | solution.py:437
  92.3 6.0 %all-to-all-done.2 = bf16[16,32,1024]{2,1,0:T(8,128)(2,1)} async-done(((bf16[16,32,1024]{2,1,0:T(8,128)(2,1)}), bf16[16,32,1024]{2,1,0:T(8,128)(2,1)}, u32[]{:S(2)}, u32[]{:S(2)}) %all-to-all-start.2) | async-done | bytes 1048608 | tf_op jit(solution)/shard_map/all_to_all | solution.py:472
  98.3 4.0 %taps.1 = (bf16[128,1024]{1,0:T(8,128)(2,1)}, bf16[16,1024]{1,0:T(8,128)(2,1)}, bf16[16,1024]{1,0:T(8,128)(2,1)}, f32[32,8,128]{2,1,0:T(8,128)}) custom-call(s32[1]{0:T(128)} %bitcast.refs_0_.index_ref, bf16[256,128]{1,0:T(8,128)(2,1)} %get-tuple-element.45.refs_3_.refs_5_.refs_1_, f32[128,1024]{1,0:T(8,128)} %get-tuple-element.50.refs_2_, ...), custom_call_target="tpu_custom_call" | custom-call | flops 67108864 | bytes 2097152 | tf_op jit(solution)/shard_map/taps/pallas_call | solution.py:102
  102.3 2.8 %all-to-all-start.3 = ((f32[32,8,128]{2,1,0:T(8,128)}), f32[32,8,128]{2,1,0:T(8,128)S(1)}, u32[]{:S(2)}, u32[]{:S(2)}) async-start(f32[32,8,128]{2,1,0:T(8,128)} %get-tuple-element.64), calls=%async_computation.3 | async-start | bytes 262144 | tf_op jit(solution)/shard_map/all_to_all | solution.py:497
  105.1 1.8 %collective-permute-start.9 = (bf16[16,1024]{1,0:T(8,128)(2,1)}, bf16[16,1024]{1,0:T(8,128)(2,1)S(1)}, u32[]{:S(2)}, u32[]{:S(2)}) collective-permute-start(bf16[16,1024]{1,0:T(8,128)(2,1)} %get-tuple-element.61), channel_id=1, source_target_pairs={{0,1},{1,2},{2,3},{3,4},{4,5},{5,6},{6,7},{7,8},{8,9},{9,10},{10,1... | collective-permute-start | bytes 98312 | tf_op jit(solution)/shard_map/ppermute | solution.py:489
  107.0 3.6 %collective-permute-start.10 = (bf16[16,1024]{1,0:T(8,128)(2,1)}, bf16[16,1024]{1,0:T(8,128)(2,1)S(1)}, u32[]{:S(2)}, u32[]{:S(2)}) collective-permute-start(bf16[16,1024]{1,0:T(8,128)(2,1)} %get-tuple-element.63), channel_id=1, source_target_pairs={{1,0},{2,1},{3,2},{4,3},{5,4},{6,5},{7,6},{8,7},{9,8},{10,9},{11,1... | collective-permute-start | bytes 98312 | tf_op jit(solution)/shard_map/ppermute | solution.py:489
  110.5 7.2 %adam_up.1 = (f32[256,2048]{1,0:T(8,128)}, bf16[256,2048]{1,0:T(8,128)(2,1)}, f32[16,256]{1,0:T(8,128)}, bf16[256,2048]{1,0:T(8,128)(2,1)}, f32[16,256]{1,0:T(8,128)}) custom-call(s32[1]{0:T(128)} %bitcast.refs_0_.index_ref, f32[256,2048]{1,0:T(8,128)} %bitcast.50, bf16[256,2048]{1,0:T(8,128)(2,1)} %bitcast.60, f32[16,256]{1,0:T(8,128)} %bitcast.68, ...), custom_call_target="tpu_custom_call" | custom-call | flops 10485760 | bytes 11534336 | tf_op jit(solution)/shard_map/adam_up/pallas_call | solution.py:437
  117.8 0.0 copy-start
  117.8 0.5 copy-done.3
  118.4 0.0 copy-done.4
  118.4 0.1 copy-done
  118.5 1.6 %spread.1 = f32[32,8,128]{2,1,0:T(8,128)} custom-call(f32[32,8,128]{2,1,0:T(8,128)} %copy-done, f32[1,256,2048]{2,1,0:T(8,128)} %bitcast.53, bf16[16,1024]{1,0:T(8,128)(2,1)} %copy-done.3, bf16[16,1024]{1,0:T(8,128)(2,1)} %copy-done.4), custom_call_target="tpu_custom_call" | custom-call | tf_op jit(solution)/shard_map/spread/pallas_call | solution.py:102
  120.1 2.6 %all-to-all-start.4 = ((f32[32,8,128]{2,1,0:T(8,128)}), f32[32,8,128]{2,1,0:T(8,128)S(1)}, u32[]{:S(2)}, u32[]{:S(2)}) async-start(f32[32,8,128]{2,1,0:T(8,128)} %spread.1), calls=%async_computation.4 | async-start | bytes 262144 | tf_op jit(solution)/shard_map/all_to_all | solution.py:499
  122.7 3.4 %frames.1 = bf16[128,1024]{1,0:T(8,128)(2,1)} custom-call(s32[1]{0:T(128)} %bitcast.refs_0_.index_ref, bf16[16,1024]{1,0:T(8,128)(2,1)} %copy-done.3, bf16[128,1024]{1,0:T(8,128)(2,1)} %get-tuple-element.62.refs_2_, bf16[16,1024]{1,0:T(8,128)(2,1)} %copy-done.4, f32[32,1024]{1,0:T(8,128)} %refs_4_.5, bf16[128,1024]{1,0:T(8,128)(2,1)} %refs_5_.1), custom_call_target="tpu_custom_call" | custom-call | flops 67108864 | bytes 1048576 | tf_op jit(solution)/shard_map/frames/pallas_call | solution.py:102
  126.1 4.3 %all-to-all-done.4 = f32[32,8,128]{2,1,0:T(8,128)S(1)} async-done(((f32[32,8,128]{2,1,0:T(8,128)}), f32[32,8,128]{2,1,0:T(8,128)S(1)}, u32[]{:S(2)}, u32[]{:S(2)}) %all-to-all-start.4) | async-done | bytes 131104 | tf_op jit(solution)/shard_map/all_to_all | solution.py:499
  130.4 0.7 copy.28
  (13 shorter events, 0.0 us)
Async XLA Ops:
  3.4 24.8 %all-to-all-start.1 = ((bf16[8,32,1024]{2,1,0:T(8,128)(2,1)}), bf16[8,32,1024]{2,1,0:T(8,128)(2,1)}, u32[]{:S(2)}, u32[]{:S(2)}) async-start(bf16[8,32,1024]{2,1,0:T(8,128)(2,1)} %bitcast.62), calls=%async_computation.1 | async-start | bytes 1048576 | tf_op jit(solution)/shard_map/all_to_all | solution.py:465
  10.6 14.1 %collective-permute-start.2 = (bf16[256,1024]{1,0:T(8,128)(2,1)}, bf16[256,1024]{1,0:T(8,128)(2,1)}, u32[]{:S(2)}, u32[]{:S(2)}) collective-permute-start(bf16[256,1024]{1,0:T(8,128)(2,1)} %get-tuple-element.49), channel_id=1, source_target_pairs={{0,16},{16,0},{1,17},{17,1},{2,18},{18,2},{3,19},{19,3},{4,20},{20... | collective-permute-start | bytes 1572872 | tf_op jit(solution)/shard_map/ppermute | solution.py:477
  12.2 12.2 %collective-permute-start = (bf16[16,1024]{1,0:T(8,128)(2,1)}, bf16[16,1024]{1,0:T(8,128)(2,1)S(1)}, u32[]{:S(2)}, u32[]{:S(2)}) collective-permute-start(bf16[16,1024]{1,0:T(8,128)(2,1)} %get-tuple-element.46), channel_id=1, source_target_pairs={{0,1},{1,2},{2,3},{3,4},{4,5},{5,6},{6,7},{7,8},{8,9},{9,10},{10,1... | collective-permute-start | bytes 98312 | tf_op jit(solution)/shard_map/ppermute | solution.py:489
  14.2 10.2 %collective-permute-start.1 = (bf16[16,1024]{1,0:T(8,128)(2,1)}, bf16[16,1024]{1,0:T(8,128)(2,1)S(1)}, u32[]{:S(2)}, u32[]{:S(2)}) collective-permute-start(bf16[16,1024]{1,0:T(8,128)(2,1)} %get-tuple-element.47), channel_id=1, source_target_pairs={{1,0},{2,1},{3,2},{4,3},{5,4},{6,5},{7,6},{8,7},{9,8},{10,9},{11,1... | collective-permute-start | bytes 98312 | tf_op jit(solution)/shard_map/ppermute | solution.py:489
  24.4 0.6 copy-start.1
  24.4 0.6 copy-start.2
  28.2 19.5 %all-to-all-start = ((bf16[8,32,1024]{2,1,0:T(8,128)(2,1)}), bf16[8,32,1024]{2,1,0:T(8,128)(2,1)}, u32[]{:S(2)}, u32[]{:S(2)}) async-start(bf16[8,32,1024]{2,1,0:T(8,128)(2,1)} %bitcast.63), calls=%async_computation | async-start | bytes 1048576 | tf_op jit(solution)/shard_map/all_to_all | solution.py:465
  33.6 15.6 %collective-permute-start.7 = (bf16[512,1024]{1,0:T(8,128)(2,1)}, bf16[512,1024]{1,0:T(8,128)(2,1)}, u32[]{:S(2)}, u32[]{:S(2)}) collective-permute-start(bf16[512,1024]{1,0:T(8,128)(2,1)} %get-tuple-element.48.refs_2_.refs_7_), channel_id=1, source_target_pairs={{0,8},{8,0},{1,9},{9,1},{2,10},{10,2},{3,11},{11,3},{4,12},{12,4},... | collective-permute-start | bytes 3145736 | tf_op jit(solution)/shard_map/ppermute | solution.py:481
  33.6 15.6 %collective-permute-start.4 = (bf16[256,1024]{1,0:T(8,128)(2,1)}, bf16[256,1024]{1,0:T(8,128)(2,1)}, u32[]{:S(2)}, u32[]{:S(2)}) collective-permute-start(bf16[256,1024]{1,0:T(8,128)(2,1)} %get-tuple-element.52.refs_2_), channel_id=1, source_target_pairs={{0,8},{8,0},{1,9},{9,1},{2,10},{10,2},{3,11},{11,3},{4,12},{12,4},... | collective-permute-start | bytes 1572872 | tf_op jit(solution)/shard_map/ppermute | solution.py:481
  34.1 15.1 %collective-permute-start.5 = (bf16[256,1024]{1,0:T(8,128)(2,1)}, bf16[256,1024]{1,0:T(8,128)(2,1)}, u32[]{:S(2)}, u32[]{:S(2)}) collective-permute-start(bf16[256,1024]{1,0:T(8,128)(2,1)} %collective-permute-done.2.refs_6_.refs_4_), channel_id=1, source_target_pairs={{0,8},{8,0},{1,9},{9,1},{2,10},{10,2},{3,11},{11,3},{4,12},{12,4},... | collective-permute-start | bytes 1572872 | tf_op jit(solution)/shard_map/ppermute | solution.py:481
  34.2 20.1 %collective-permute-start.6 = (bf16[256,1024]{1,0:T(8,128)(2,1)}, bf16[256,1024]{1,0:T(8,128)(2,1)}, u32[]{:S(2)}, u32[]{:S(2)}) collective-permute-start(bf16[256,1024]{1,0:T(8,128)(2,1)} %bitcast.7.refs_6_.refs_3_), channel_id=1, source_target_pairs={{0,16},{16,0},{1,17},{17,1},{2,18},{18,2},{3,19},{19,3},{4,20},{20... | collective-permute-start | bytes 1572872 | tf_op jit(solution)/shard_map/ppermute | solution.py:477
  47.7 12.5 %collective-permute-start.3 = (bf16[256,1024]{1,0:T(8,128)(2,1)}, bf16[256,1024]{1,0:T(8,128)(2,1)}, u32[]{:S(2)}, u32[]{:S(2)}) collective-permute-start(bf16[256,1024]{1,0:T(8,128)(2,1)} %bitcast.5.refs_1_), channel_id=1, source_target_pairs={{0,16},{16,0},{1,17},{17,1},{2,18},{18,2},{3,19},{19,3},{4,20},{20... | collective-permute-start | bytes 1572872 | tf_op jit(solution)/shard_map/ppermute | solution.py:477
  65.6 32.7 %all-to-all-start.2 = ((bf16[16,32,1024]{2,1,0:T(8,128)(2,1)}), bf16[16,32,1024]{2,1,0:T(8,128)(2,1)}, u32[]{:S(2)}, u32[]{:S(2)}) async-start(bf16[16,32,1024]{2,1,0:T(8,128)(2,1)} %bitcast.59), calls=%async_computation.2 | async-start | bytes 2097152 | tf_op jit(solution)/shard_map/all_to_all | solution.py:472
  76.4 4.5 %collective-permute-start.11 = (bf16[512,1024]{1,0:T(8,128)(2,1)}, bf16[512,1024]{1,0:T(8,128)(2,1)}, u32[]{:S(2)}, u32[]{:S(2)}) collective-permute-start(bf16[512,1024]{1,0:T(8,128)(2,1)} %get-tuple-element.68), channel_id=1, source_target_pairs={{0,8},{8,0},{1,9},{9,1},{2,10},{10,2},{3,11},{11,3},{4,12},{12,4},... | collective-permute-start | bytes 3145736 | tf_op jit(solution)/shard_map/ppermute | solution.py:481
  80.3 4.6 %collective-permute-start.8 = (bf16[512,1024]{1,0:T(8,128)(2,1)}, bf16[512,1024]{1,0:T(8,128)(2,1)}, u32[]{:S(2)}, u32[]{:S(2)}) collective-permute-start(bf16[512,1024]{1,0:T(8,128)(2,1)} %get-tuple-element.59), channel_id=1, source_target_pairs={{0,8},{8,0},{1,9},{9,1},{2,10},{10,2},{3,11},{11,3},{4,12},{12,4},... | collective-permute-start | bytes 3145736 | tf_op jit(solution)/shard_map/ppermute | solution.py:481
  83.1 27.4 %collective-permute-start.12 = (bf16[256,1024]{1,0:T(8,128)(2,1)}, bf16[256,1024]{1,0:T(8,128)(2,1)}, u32[]{:S(2)}, u32[]{:S(2)}) collective-permute-start(bf16[256,1024]{1,0:T(8,128)(2,1)} %add_convert_fusion), channel_id=1, source_target_pairs={{0,16},{16,0},{1,17},{17,1},{2,18},{18,2},{3,19},{19,3},{4,20},{20... | collective-permute-start | bytes 1572872 | tf_op jit(solution)/shard_map/ppermute | solution.py:477
  102.3 15.5 %all-to-all-start.3 = ((f32[32,8,128]{2,1,0:T(8,128)}), f32[32,8,128]{2,1,0:T(8,128)S(1)}, u32[]{:S(2)}, u32[]{:S(2)}) async-start(f32[32,8,128]{2,1,0:T(8,128)} %get-tuple-element.64), calls=%async_computation.3 | async-start | bytes 262144 | tf_op jit(solution)/shard_map/all_to_all | solution.py:497
  105.1 12.6 %collective-permute-start.9 = (bf16[16,1024]{1,0:T(8,128)(2,1)}, bf16[16,1024]{1,0:T(8,128)(2,1)S(1)}, u32[]{:S(2)}, u32[]{:S(2)}) collective-permute-start(bf16[16,1024]{1,0:T(8,128)(2,1)} %get-tuple-element.61), channel_id=1, source_target_pairs={{0,1},{1,2},{2,3},{3,4},{4,5},{5,6},{6,7},{7,8},{8,9},{9,10},{10,1... | collective-permute-start | bytes 98312 | tf_op jit(solution)/shard_map/ppermute | solution.py:489
  107.0 10.8 %collective-permute-start.10 = (bf16[16,1024]{1,0:T(8,128)(2,1)}, bf16[16,1024]{1,0:T(8,128)(2,1)S(1)}, u32[]{:S(2)}, u32[]{:S(2)}) collective-permute-start(bf16[16,1024]{1,0:T(8,128)(2,1)} %get-tuple-element.63), channel_id=1, source_target_pairs={{1,0},{2,1},{3,2},{4,3},{5,4},{6,5},{7,6},{8,7},{9,8},{10,9},{11,1... | collective-permute-start | bytes 98312 | tf_op jit(solution)/shard_map/ppermute | solution.py:489
  117.8 0.6 copy-start.3
  117.8 0.6 copy-start.4
  117.8 0.7 copy-start
  120.1 10.3 %all-to-all-start.4 = ((f32[32,8,128]{2,1,0:T(8,128)}), f32[32,8,128]{2,1,0:T(8,128)S(1)}, u32[]{:S(2)}, u32[]{:S(2)}) async-start(f32[32,8,128]{2,1,0:T(8,128)} %spread.1), calls=%async_computation.4 | async-start | bytes 262144 | tf_op jit(solution)/shard_map/all_to_all | solution.py:499

commit v6 on v5

--- a/solution.py
+++ b/solution.py
@@ -215,7 +215,7 @@
             if extra is not None:
                 total = total + extra
             active, slope = swish_parts(total)
-            slope_ref[rows, cols] = slope
+            slope_ref[rows, cols] = slope.astype(bf16)
             feat_ref[rows, cols] = active.astype(bf16)
         return carry
 
@@ -315,7 +315,7 @@
     for chip in range(back_ref.shape[0] // slots):
         features = features + across(spots, back_ref[chip * slots : (chip + 1) * slots, :])
     features = features.astype(bf16).astype(f32)
-    grad = (features * take(1)[...]).astype(bf16)
+    grad = (features * take(1)[...].astype(f32)).astype(bf16)
     grad_ref[...] = grad
     head_ref[...] = grad[:side]
     tail_ref[...] = grad[length - side :]
@@ -325,15 +325,17 @@
     left, frames, right = take(2), take(3), take(4)
     shift_ref[0:8, :] = jnp.zeros((8, 128), f32)
     shift_ref[8 + length :, :] = jnp.zeros((8, 128), f32)
-    for step in range(width // 128):
+    strips = width // 128
+    for step in range(strips):
         cols = slice(step * 128, (step + 1) * 128)
         fill_padded(pad_ref, place, left, frames, right, cols)
         shift_ref[8 : 8 + length, :] = grad_ref[:, cols].astype(f32)
         for rest in range(8):
             moved = shift_ref[8 - rest : 8 - rest + length + 8, :]
-            for tap in range(rest, terms_ref.shape[0], 8):
+            for tap in range(rest, terms_ref.shape[0] // strips * 8, 8):
                 product = moved * pad_ref[tap - rest : tap - rest + length + 8, :]
-                terms_ref[tap, step : step + 1, :] = jnp.sum(product, axis=0, keepdims=True)
+                tile = tap // 8 * strips + step
+                terms_ref[tile, rest : rest + 1, :] = jnp.sum(product, axis=0, keepdims=True)
 
 
 def frames_kernel(here, scalars, take, made, give, scratch):
@@ -489,14 +491,16 @@
     return lax.ppermute(tail, axes, right), lax.ppermute(head, axes, left)
 
 
-def sum_everywhere(terms, after):
+def sum_everywhere(terms, strips, after):
     axes = ("chip", "core", "expert")
     count = math.prod(lax.axis_size(axis) for axis in axes)
-    taps, strips, lanes = terms.shape
-    cells = terms.reshape(count, taps * strips // count, lanes)
+    tiles, rows, lanes = terms.shape
+    cells = terms.reshape(count, tiles * rows // count, lanes)
     parts = lax.all_to_all(cells, axes, 0, 0, tiled=True)
     (spread,) = call(spread_kernel, "spread", [], [parts], [(cells.shape, f32)], after=after)
-    return lax.all_to_all(spread, axes, 0, 0, tiled=True).reshape(taps, strips * lanes)
+    total = lax.all_to_all(spread, axes, 0, 0, tiled=True)
+    total = total.reshape(tiles // strips, strips, rows, lanes).transpose(0, 2, 1, 3)
+    return total.reshape(tiles // strips * rows, strips * lanes)
 
 
 def body(
@@ -575,7 +579,7 @@
         "edges",
         [index],
         [left, right, inner, conv_weight, place],
-        [((length, width), f32), row_shape],
+        [((length, width), bf16), row_shape],
         after=far_ups + [down_own],
         scratch=strips + [pltpu.VMEM((length, width), bf16)],
         flops=2 * slots * length * width,
@@ -644,7 +648,7 @@
         "taps",
         [index],
         [place, slope, left, frames, right, returned],
-        [((length, width), bf16), ((side, width), bf16), ((side, width), bf16), ((taps, width // 128, 128), f32)],
+        [((length, width), bf16), ((side, width), bf16), ((side, width), bf16), ((taps // 8 * (width // 128), 8, 128), f32)],
         after=[down_next[0]],
         scratch=strips,
         flops=2 * slots * length * width,
@@ -665,7 +669,7 @@
         "adam_up", here, index, up_master, up_grads,
         up_mean_code, up_mean_scale, up_square_code, up_square_scale,
     )
-    conv_total = sum_everywhere(conv_terms, [up_next[0], grad_left, grad_right])
+    conv_total = sum_everywhere(conv_terms, width // 128, [up_next[0], grad_left, grad_right])
     return (grad_frames, conv_total) + up_next + down_next
 
 

time: 132 us -> 132 us (level)
  no operation moved by 1% of the time
where the time goes in v6:
time: 132 us; the launch traced here: 131 us
  Pallas kernels  54.2 us (41%)
  starting transfers between devices  43.4 us (33%)
  waiting for transfers between devices  28.8 us (22%)
  other arithmetic  2.19 us (2%)
  local copies, waits for them, and re-layouts  1.64 us (1%)
    pallas_call x11, Pallas kernels, call(): pl.pallas_call(functools.partial(staged, kernel, counts, spans), out_shap...  39.6 us
    pallas_call x2, Pallas kernels, adam(): pl.pallas_call(functools.partial(adam_kernel, here, len(grads) - 2), grid...  14.5 us
    all_to_all x2, starting transfers between devices, by_expert(): lax.all_to_all(cells, 'expert', 0, 0, tiled=True).reshape(slots, width)  12.7 us
    all_to_all x2, waiting for transfers between devices, by_expert(): lax.all_to_all(cells, 'expert', 0, 0, tiled=True).reshape(slots, width)  12 us
    ppermute x4, starting transfers between devices, halo(): return (lax.ppermute(tail, axes, right), lax.ppermute(head, axes, left))  10.7 us
    all_to_all x1, starting transfers between devices, to_senders(): return lax.all_to_all(cells, axes, 0, 0, tiled=True).reshape(rows.shape)  6.99 us
    ppermute x4, starting transfers between devices, to_chip(): lax.ppermute(values, 'chip', [(i, (i + shift) % chips) for i in range(chi...  6.41 us
    ppermute x4, waiting for transfers between devices, to_chip(): lax.ppermute(values, 'chip', [(i, (i + shift) % chips) for i in range(chi...  6.16 us
  transfers between devices with their start and end apart: 18, of which 6 were waited for; matrix products, arithmetic and copies ran while one was open for 2% of the time, Pallas kernels for 34%

profile of v6, /device:TPU:0, one launch (start us, length us, event | category | flops | bytes accessed | tf_op | source)
XLA Modules:
  0.0 131.0 jit_solution(3159821810413989874)
XLA Ops:
  0.7 2.7 %prepare.1 = (bf16[16,1024]{1,0:T(8,128)(2,1)}, bf16[16,1024]{1,0:T(8,128)(2,1)}, bf16[256,128]{1,0:T(8,128)(2,1)}, bf16[256,1024]{1,0:T(8,128)(2,1)}, bf16[256,1024]{1,0:T(8,128)(2,1)}) custom-call(s32[1]{0:T(128)} %bitcast.refs_0_.index_ref, s32[1,128]{1,0:T(1,128)} %bitcast.70, bf16[128,1024]{1,0:T(8,128)(2,1)} %refs_5_.1, bf16[128,1024]{1,0:T(8,128)(2,1)} %refs_4_.4, ...), custom_call_target="tpu_custom_call" | custom-call | flops 67108864 | bytes 1048576 | tf_op jit(solution)/shard_map/prepare/pallas_call | solution.py:102
  3.4 7.3 %all-to-all-start.1 = ((bf16[8,32,1024]{2,1,0:T(8,128)(2,1)}), bf16[8,32,1024]{2,1,0:T(8,128)(2,1)}, u32[]{:S(2)}, u32[]{:S(2)}) async-start(bf16[8,32,1024]{2,1,0:T(8,128)(2,1)} %bitcast.63), calls=%async_computation.1 | async-start | bytes 1048576 | tf_op jit(solution)/shard_map/all_to_all | solution.py:467
  10.6 1.5 %collective-permute-start.2 = (bf16[256,1024]{1,0:T(8,128)(2,1)}, bf16[256,1024]{1,0:T(8,128)(2,1)}, u32[]{:S(2)}, u32[]{:S(2)}) collective-permute-start(bf16[256,1024]{1,0:T(8,128)(2,1)} %get-tuple-element.49), channel_id=1, source_target_pairs={{0,16},{16,0},{1,17},{17,1},{2,18},{18,2},{3,19},{19,3},{4,20},{20... | collective-permute-start | bytes 1572872 | tf_op jit(solution)/shard_map/ppermute | solution.py:479
  12.2 2.0 %collective-permute-start = (bf16[16,1024]{1,0:T(8,128)(2,1)}, bf16[16,1024]{1,0:T(8,128)(2,1)S(1)}, u32[]{:S(2)}, u32[]{:S(2)}) collective-permute-start(bf16[16,1024]{1,0:T(8,128)(2,1)} %get-tuple-element.46), channel_id=1, source_target_pairs={{0,1},{1,2},{2,3},{3,4},{4,5},{5,6},{6,7},{7,8},{8,9},{9,10},{10,1... | collective-permute-start | bytes 98312 | tf_op jit(solution)/shard_map/ppermute | solution.py:491
  14.2 3.3 %collective-permute-start.1 = (bf16[16,1024]{1,0:T(8,128)(2,1)}, bf16[16,1024]{1,0:T(8,128)(2,1)S(1)}, u32[]{:S(2)}, u32[]{:S(2)}) collective-permute-start(bf16[16,1024]{1,0:T(8,128)(2,1)} %get-tuple-element.47), channel_id=1, source_target_pairs={{1,0},{2,1},{3,2},{4,3},{5,4},{6,5},{7,6},{8,7},{9,8},{10,9},{11,1... | collective-permute-start | bytes 98312 | tf_op jit(solution)/shard_map/ppermute | solution.py:491
  17.5 3.3 %cast_near.1 = (bf16[256,1024]{1,0:T(8,128)(2,1)}, bf16[512,1024]{1,0:T(8,128)(2,1)}) custom-call(s32[1]{0:T(128)} %bitcast.refs_0_.index_ref, f32[256,2048]{1,0:T(8,128)} %bitcast.50, f32[512,1024]{1,0:T(8,128)} %bitcast.52, bf16[256,128]{1,0:T(8,128)(2,1)} %get-tuple-element.45.refs_3_.refs_5_.refs_1_), custom_call_target="tpu_custom_call" | custom-call | bytes 6291456 | tf_op jit(solution)/shard_map/cast_near/pallas_call | solution.py:102
  20.8 3.3 %convolve.1.refs_3_ = f32[128,1024]{1,0:T(8,128)} custom-call(bf16[128,1024]{1,0:T(8,128)(2,1)} %refs_4_.4, f32[32,1024]{1,0:T(8,128)} %refs_4_.5, bf16[512,1024]{1,0:T(8,128)(2,1)} %get-tuple-element.48.refs_2_.refs_7_), custom_call_target="tpu_custom_call" | custom-call | flops 67108864 | bytes 2097152 | tf_op jit(solution)/shard_map/convolve/pallas_call | solution.py:102
  24.1 0.3 collective-permute-done.refs_1_.refs_3_
  24.4 0.0 collective-permute-done.1.refs_2_.refs_5_
  24.4 0.3 collective-permute-done.2.refs_6_.refs_4_
  24.7 0.3 copy-done.1
  25.0 0.0 copy-done.2
  25.0 3.2 %edges.1 = (bf16[128,1024]{1,0:T(8,128)(2,1)}, bf16[256,1024]{1,0:T(8,128)(2,1)}) custom-call(s32[1]{0:T(128)} %bitcast.refs_0_.index_ref, bf16[16,1024]{1,0:T(8,128)(2,1)} %copy-done.1, bf16[16,1024]{1,0:T(8,128)(2,1)} %copy-done.2, f32[128,1024]{1,0:T(8,128)} %convolve.1.refs_3_, f32[32,1024]{1,0:T(8,128)} %refs_4_.5, ...), custom_call_target="tpu_custom_call" | custom-call | flops 67108864 | bytes 2097152 | tf_op jit(solution)/shard_map/edges/pallas_call | solution.py:102
  28.2 5.4 %all-to-all-start = ((bf16[8,32,1024]{2,1,0:T(8,128)(2,1)}), bf16[8,32,1024]{2,1,0:T(8,128)(2,1)}, u32[]{:S(2)}, u32[]{:S(2)}) async-start(bf16[8,32,1024]{2,1,0:T(8,128)(2,1)} %bitcast.64), calls=%async_computation | async-start | bytes 1048576 | tf_op jit(solution)/shard_map/all_to_all | solution.py:467
  33.6 0.0 collective-permute-start.7
  33.6 0.5 collective-permute-start.4
  34.1 0.1 collective-permute-start.5
  34.2 1.5 %collective-permute-start.6 = (bf16[256,1024]{1,0:T(8,128)(2,1)}, bf16[256,1024]{1,0:T(8,128)(2,1)}, u32[]{:S(2)}, u32[]{:S(2)}) collective-permute-start(bf16[256,1024]{1,0:T(8,128)(2,1)} %bitcast.7.refs_6_.refs_3_), channel_id=1, source_target_pairs={{0,16},{16,0},{1,17},{17,1},{2,18},{18,2},{3,19},{19,3},{4,20},{20... | collective-permute-start | bytes 1572872 | tf_op jit(solution)/shard_map/ppermute | solution.py:479
  35.7 12.0 %all-to-all-done = bf16[8,32,1024]{2,1,0:T(8,128)(2,1)} async-done(((bf16[8,32,1024]{2,1,0:T(8,128)(2,1)}), bf16[8,32,1024]{2,1,0:T(8,128)(2,1)}, u32[]{:S(2)}, u32[]{:S(2)}) %all-to-all-start) | async-done | bytes 524320 | tf_op jit(solution)/shard_map/all_to_all | solution.py:467
  47.7 1.5 %collective-permute-start.3 = (bf16[256,1024]{1,0:T(8,128)(2,1)}, bf16[256,1024]{1,0:T(8,128)(2,1)}, u32[]{:S(2)}, u32[]{:S(2)}) collective-permute-start(bf16[256,1024]{1,0:T(8,128)(2,1)} %bitcast.5.refs_1_), channel_id=1, source_target_pairs={{0,16},{16,0},{1,17},{17,1},{2,18},{18,2},{3,19},{19,3},{4,20},{20... | collective-permute-start | bytes 1572872 | tf_op jit(solution)/shard_map/ppermute | solution.py:479
  49.2 0.0 collective-permute-done.4.refs_3_
  49.2 0.0 collective-permute-done.5.refs_5_
  49.2 5.1 %own_group.1 = (bf16[256,1024]{1,0:T(8,128)(2,1)}, bf16[256,1024]{1,0:T(8,128)(2,1)}, bf16[256,1024]{1,0:T(8,128)(2,1)}) custom-call(s32[1]{0:T(128)} %bitcast.refs_0_.index_ref, bf16[256,1024]{1,0:T(8,128)(2,1)} %bitcast.5.refs_1_, bf16[256,1024]{1,0:T(8,128)(2,1)} %get-tuple-element.52.refs_2_, bf16[256,1024]{1,0:T(8,128)(2,1)} %collective-permute-done.4.refs_3_, ...), custom_call_target="tpu_custom_call" | custom-call | flops 1610612736 | bytes 8388608 | tf_op jit(solution)/shard_map/own_group/pallas_call | solution.py:102
  54.3 5.9 %collective-permute-done.3.refs_1_.refs_2_ = bf16[256,1024]{1,0:T(8,128)(2,1)} collective-permute-done((bf16[256,1024]{1,0:T(8,128)(2,1)}, bf16[256,1024]{1,0:T(8,128)(2,1)}, u32[]{:S(2)}, u32[]{:S(2)}) %collective-permute-start.3) | collective-permute-done | bytes 524320 | tf_op jit(solution)/shard_map/ppermute | solution.py:479
  60.1 5.4 %far_group.1 = (bf16[256,1024]{1,0:T(8,128)(2,1)}, bf16[256,1024]{1,0:T(8,128)(2,1)}, bf16[512,1024]{1,0:T(8,128)(2,1)}) custom-call(s32[1]{0:T(128)} %bitcast.refs_0_.index_ref, bf16[256,1024]{1,0:T(8,128)(2,1)} %collective-permute-done.3.refs_1_.refs_2_, bf16[256,1024]{1,0:T(8,128)(2,1)} %get-tuple-element.52.refs_2_, ...), custom_call_target="tpu_custom_call" | custom-call | flops 1610612736 | bytes 8388608 | tf_op jit(solution)/shard_map/far_group/pallas_call | solution.py:102
  65.6 7.0 %all-to-all-start.2 = ((bf16[16,32,1024]{2,1,0:T(8,128)(2,1)}), bf16[16,32,1024]{2,1,0:T(8,128)(2,1)}, u32[]{:S(2)}, u32[]{:S(2)}) async-start(bf16[16,32,1024]{2,1,0:T(8,128)(2,1)} %bitcast.60), calls=%async_computation.2 | async-start | bytes 2097152 | tf_op jit(solution)/shard_map/all_to_all | solution.py:474
  72.6 3.8 %up_grad.1 = (bf16[512,1024]{1,0:T(8,128)(2,1)}, bf16[512,1024]{1,0:T(8,128)(2,1)}) custom-call(s32[1]{0:T(128)} %bitcast.refs_0_.index_ref, bf16[256,1024]{1,0:T(8,128)(2,1)} %bitcast.5.refs_1_, bf16[256,1024]{1,0:T(8,128)(2,1)} %collective-permute-done.3.refs_1_.refs_2_, bf16[256,1024]{1,0:T(8,128)(2,1)} %get-tuple-element.65.refs_3_, ...), custom_call_target="tpu_custom_call" | custom-call | flops 1073741824 | bytes 8388608 | tf_op jit(solution)/shard_map/up_grad/pallas_call | solution.py:102
  76.4 0.1 collective-permute-start.11
  76.5 3.8 %down_grad.1 = (bf16[512,1024]{1,0:T(8,128)(2,1)}, bf16[512,1024]{1,0:T(8,128)(2,1)}) custom-call(s32[1]{0:T(128)} %bitcast.refs_0_.index_ref, bf16[256,1024]{1,0:T(8,128)(2,1)} %get-tuple-element.56.refs_1_, bf16[256,1024]{1,0:T(8,128)(2,1)} %get-tuple-element.57.refs_2_, bf16[256,1024]{1,0:T(8,128)(2,1)} %bitcast.7.refs_6_.refs_3_, ...), custom_call_target="tpu_custom_call" | custom-call | flops 1073741824 | bytes 8388608 | tf_op jit(solution)/shard_map/down_grad/pallas_call | solution.py:102
  80.3 0.6 collective-permute-start.8
  80.9 2.2 %add_convert_fusion = bf16[256,1024]{1,0:T(8,128)(2,1)} fusion(bf16[512,1024]{1,0:T(8,128)(2,1)} %collective-permute-done.11.refs_1_, bf16[512,1024]{1,0:T(8,128)(2,1)} %get-tuple-element.67.refs_0_), kind=kLoop, calls=%fused_computation | loop fusion | flops 1048576 | bytes 1572864 | tf_op jit(solution)/shard_map/convert_element_type | solution.py:629
  83.1 1.9 %collective-permute-start.12 = (bf16[256,1024]{1,0:T(8,128)(2,1)}, bf16[256,1024]{1,0:T(8,128)(2,1)}, u32[]{:S(2)}, u32[]{:S(2)}) collective-permute-start(bf16[256,1024]{1,0:T(8,128)(2,1)} %add_convert_fusion), channel_id=1, source_target_pairs={{0,16},{16,0},{1,17},{17,1},{2,18},{18,2},{3,19},{19,3},{4,20},{20... | collective-permute-start | bytes 1572872 | tf_op jit(solution)/shard_map/ppermute | solution.py:479
  84.9 7.3 %adam_down.1 = (f32[512,1024]{1,0:T(8,128)}, bf16[512,1024]{1,0:T(8,128)(2,1)}, f32[8,512]{1,0:T(8,128)}, bf16[512,1024]{1,0:T(8,128)(2,1)}, f32[8,512]{1,0:T(8,128)}) custom-call(s32[1]{0:T(128)} %bitcast.refs_0_.index_ref, f32[512,1024]{1,0:T(8,128)} %bitcast.53, bf16[512,1024]{1,0:T(8,128)(2,1)} %bitcast.58, f32[8,512]{1,0:T(8,128)} %bitcast.66, ...), custom_call_target="tpu_custom_call" | custom-call | flops 10485760 | bytes 10485760 | tf_op jit(solution)/shard_map/adam_down/pallas_call | solution.py:439
  92.3 6.0 %all-to-all-done.2 = bf16[16,32,1024]{2,1,0:T(8,128)(2,1)} async-done(((bf16[16,32,1024]{2,1,0:T(8,128)(2,1)}), bf16[16,32,1024]{2,1,0:T(8,128)(2,1)}, u32[]{:S(2)}, u32[]{:S(2)}) %all-to-all-start.2) | async-done | bytes 1048608 | tf_op jit(solution)/shard_map/all_to_all | solution.py:474
  98.3 4.0 %taps.1 = (bf16[128,1024]{1,0:T(8,128)(2,1)}, bf16[16,1024]{1,0:T(8,128)(2,1)}, bf16[16,1024]{1,0:T(8,128)(2,1)}, f32[32,8,128]{2,1,0:T(8,128)}) custom-call(s32[1]{0:T(128)} %bitcast.refs_0_.index_ref, bf16[256,128]{1,0:T(8,128)(2,1)} %get-tuple-element.45.refs_3_.refs_5_.refs_1_, bf16[128,1024]{1,0:T(8,128)(2,1)} %get-tuple-element.50.refs_2_, ...), custom_call_target="tpu_custom_call" | custom-call | flops 67108864 | bytes 2097152 | tf_op jit(solution)/shard_map/taps/pallas_call | solution.py:102
  102.3 2.8 %all-to-all-start.3 = ((f32[32,8,128]{2,1,0:T(8,128)}), f32[32,8,128]{2,1,0:T(8,128)S(1)}, u32[]{:S(2)}, u32[]{:S(2)}) async-start(f32[32,8,128]{2,1,0:T(8,128)} %get-tuple-element.64), calls=%async_computation.3 | async-start | bytes 262144 | tf_op jit(solution)/shard_map/all_to_all | solution.py:499
  105.1 1.8 %collective-permute-start.9 = (bf16[16,1024]{1,0:T(8,128)(2,1)}, bf16[16,1024]{1,0:T(8,128)(2,1)S(1)}, u32[]{:S(2)}, u32[]{:S(2)}) collective-permute-start(bf16[16,1024]{1,0:T(8,128)(2,1)} %get-tuple-element.61), channel_id=1, source_target_pairs={{0,1},{1,2},{2,3},{3,4},{4,5},{5,6},{6,7},{7,8},{8,9},{9,10},{10,1... | collective-permute-start | bytes 98312 | tf_op jit(solution)/shard_map/ppermute | solution.py:491
  106.9 3.6 %collective-permute-start.10 = (bf16[16,1024]{1,0:T(8,128)(2,1)}, bf16[16,1024]{1,0:T(8,128)(2,1)S(1)}, u32[]{:S(2)}, u32[]{:S(2)}) collective-permute-start(bf16[16,1024]{1,0:T(8,128)(2,1)} %get-tuple-element.63), channel_id=1, source_target_pairs={{1,0},{2,1},{3,2},{4,3},{5,4},{6,5},{7,6},{8,7},{9,8},{10,9},{11,1... | collective-permute-start | bytes 98312 | tf_op jit(solution)/shard_map/ppermute | solution.py:491
  110.5 7.2 %adam_up.1 = (f32[256,2048]{1,0:T(8,128)}, bf16[256,2048]{1,0:T(8,128)(2,1)}, f32[16,256]{1,0:T(8,128)}, bf16[256,2048]{1,0:T(8,128)(2,1)}, f32[16,256]{1,0:T(8,128)}) custom-call(s32[1]{0:T(128)} %bitcast.refs_0_.index_ref, f32[256,2048]{1,0:T(8,128)} %bitcast.51, bf16[256,2048]{1,0:T(8,128)(2,1)} %bitcast.61, f32[16,256]{1,0:T(8,128)} %bitcast.68, ...), custom_call_target="tpu_custom_call" | custom-call | flops 10485760 | bytes 11534336 | tf_op jit(solution)/shard_map/adam_up/pallas_call | solution.py:439
  117.7 0.0 copy-start
  117.7 0.5 copy-done.3
  118.3 0.0 copy-done.4
  118.3 0.1 copy-done
  118.4 1.6 %spread.1 = f32[32,8,128]{2,1,0:T(8,128)} custom-call(f32[32,8,128]{2,1,0:T(8,128)} %copy-done, f32[1,256,2048]{2,1,0:T(8,128)} %bitcast.54, bf16[16,1024]{1,0:T(8,128)(2,1)} %copy-done.3, bf16[16,1024]{1,0:T(8,128)(2,1)} %copy-done.4), custom_call_target="tpu_custom_call" | custom-call | tf_op jit(solution)/shard_map/spread/pallas_call | solution.py:102
  120.0 2.6 %all-to-all-start.4 = ((f32[32,8,128]{2,1,0:T(8,128)}), f32[32,8,128]{2,1,0:T(8,128)S(1)}, u32[]{:S(2)}, u32[]{:S(2)}) async-start(f32[32,8,128]{2,1,0:T(8,128)} %spread.1), calls=%async_computation.4 | async-start | bytes 262144 | tf_op jit(solution)/shard_map/all_to_all | solution.py:501
  122.6 3.4 %frames.1 = bf16[128,1024]{1,0:T(8,128)(2,1)} custom-call(s32[1]{0:T(128)} %bitcast.refs_0_.index_ref, bf16[16,1024]{1,0:T(8,128)(2,1)} %copy-done.3, bf16[128,1024]{1,0:T(8,128)(2,1)} %get-tuple-element.62.refs_2_, bf16[16,1024]{1,0:T(8,128)(2,1)} %copy-done.4, f32[32,1024]{1,0:T(8,128)} %refs_4_.5, bf16[128,1024]{1,0:T(8,128)(2,1)} %refs_5_.1), custom_call_target="tpu_custom_call" | custom-call | flops 67108864 | bytes 1048576 | tf_op jit(solution)/shard_map/frames/pallas_call | solution.py:102
  126.0 4.3 %all-to-all-done.4 = f32[32,8,128]{2,1,0:T(8,128)S(1)} async-done(((f32[32,8,128]{2,1,0:T(8,128)}), f32[32,8,128]{2,1,0:T(8,128)S(1)}, u32[]{:S(2)}, u32[]{:S(2)}) %all-to-all-start.4) | async-done | bytes 131104 | tf_op jit(solution)/shard_map/all_to_all | solution.py:501
  130.3 0.7 copy.27
  (13 shorter events, 0.0 us)
Async XLA Ops:
  3.4 24.8 %all-to-all-start.1 = ((bf16[8,32,1024]{2,1,0:T(8,128)(2,1)}), bf16[8,32,1024]{2,1,0:T(8,128)(2,1)}, u32[]{:S(2)}, u32[]{:S(2)}) async-start(bf16[8,32,1024]{2,1,0:T(8,128)(2,1)} %bitcast.63), calls=%async_computation.1 | async-start | bytes 1048576 | tf_op jit(solution)/shard_map/all_to_all | solution.py:467
  10.6 14.1 %collective-permute-start.2 = (bf16[256,1024]{1,0:T(8,128)(2,1)}, bf16[256,1024]{1,0:T(8,128)(2,1)}, u32[]{:S(2)}, u32[]{:S(2)}) collective-permute-start(bf16[256,1024]{1,0:T(8,128)(2,1)} %get-tuple-element.49), channel_id=1, source_target_pairs={{0,16},{16,0},{1,17},{17,1},{2,18},{18,2},{3,19},{19,3},{4,20},{20... | collective-permute-start | bytes 1572872 | tf_op jit(solution)/shard_map/ppermute | solution.py:479
  12.2 12.2 %collective-permute-start = (bf16[16,1024]{1,0:T(8,128)(2,1)}, bf16[16,1024]{1,0:T(8,128)(2,1)S(1)}, u32[]{:S(2)}, u32[]{:S(2)}) collective-permute-start(bf16[16,1024]{1,0:T(8,128)(2,1)} %get-tuple-element.46), channel_id=1, source_target_pairs={{0,1},{1,2},{2,3},{3,4},{4,5},{5,6},{6,7},{7,8},{8,9},{9,10},{10,1... | collective-permute-start | bytes 98312 | tf_op jit(solution)/shard_map/ppermute | solution.py:491
  14.2 10.2 %collective-permute-start.1 = (bf16[16,1024]{1,0:T(8,128)(2,1)}, bf16[16,1024]{1,0:T(8,128)(2,1)S(1)}, u32[]{:S(2)}, u32[]{:S(2)}) collective-permute-start(bf16[16,1024]{1,0:T(8,128)(2,1)} %get-tuple-element.47), channel_id=1, source_target_pairs={{1,0},{2,1},{3,2},{4,3},{5,4},{6,5},{7,6},{8,7},{9,8},{10,9},{11,1... | collective-permute-start | bytes 98312 | tf_op jit(solution)/shard_map/ppermute | solution.py:491
  24.4 0.6 copy-start.1
  24.4 0.6 copy-start.2
  28.2 19.5 %all-to-all-start = ((bf16[8,32,1024]{2,1,0:T(8,128)(2,1)}), bf16[8,32,1024]{2,1,0:T(8,128)(2,1)}, u32[]{:S(2)}, u32[]{:S(2)}) async-start(bf16[8,32,1024]{2,1,0:T(8,128)(2,1)} %bitcast.64), calls=%async_computation | async-start | bytes 1048576 | tf_op jit(solution)/shard_map/all_to_all | solution.py:467
  33.6 15.6 %collective-permute-start.7 = (bf16[512,1024]{1,0:T(8,128)(2,1)}, bf16[512,1024]{1,0:T(8,128)(2,1)}, u32[]{:S(2)}, u32[]{:S(2)}) collective-permute-start(bf16[512,1024]{1,0:T(8,128)(2,1)} %get-tuple-element.48.refs_2_.refs_7_), channel_id=1, source_target_pairs={{0,8},{8,0},{1,9},{9,1},{2,10},{10,2},{3,11},{11,3},{4,12},{12,4},... | collective-permute-start | bytes 3145736 | tf_op jit(solution)/shard_map/ppermute | solution.py:483
  33.6 15.6 %collective-permute-start.4 = (bf16[256,1024]{1,0:T(8,128)(2,1)}, bf16[256,1024]{1,0:T(8,128)(2,1)}, u32[]{:S(2)}, u32[]{:S(2)}) collective-permute-start(bf16[256,1024]{1,0:T(8,128)(2,1)} %get-tuple-element.52.refs_2_), channel_id=1, source_target_pairs={{0,8},{8,0},{1,9},{9,1},{2,10},{10,2},{3,11},{11,3},{4,12},{12,4},... | collective-permute-start | bytes 1572872 | tf_op jit(solution)/shard_map/ppermute | solution.py:483
  34.1 15.1 %collective-permute-start.5 = (bf16[256,1024]{1,0:T(8,128)(2,1)}, bf16[256,1024]{1,0:T(8,128)(2,1)}, u32[]{:S(2)}, u32[]{:S(2)}) collective-permute-start(bf16[256,1024]{1,0:T(8,128)(2,1)} %collective-permute-done.2.refs_6_.refs_4_), channel_id=1, source_target_pairs={{0,8},{8,0},{1,9},{9,1},{2,10},{10,2},{3,11},{11,3},{4,12},{12,4},... | collective-permute-start | bytes 1572872 | tf_op jit(solution)/shard_map/ppermute | solution.py:483
  34.2 20.1 %collective-permute-start.6 = (bf16[256,1024]{1,0:T(8,128)(2,1)}, bf16[256,1024]{1,0:T(8,128)(2,1)}, u32[]{:S(2)}, u32[]{:S(2)}) collective-permute-start(bf16[256,1024]{1,0:T(8,128)(2,1)} %bitcast.7.refs_6_.refs_3_), channel_id=1, source_target_pairs={{0,16},{16,0},{1,17},{17,1},{2,18},{18,2},{3,19},{19,3},{4,20},{20... | collective-permute-start | bytes 1572872 | tf_op jit(solution)/shard_map/ppermute | solution.py:479
  47.7 12.5 %collective-permute-start.3 = (bf16[256,1024]{1,0:T(8,128)(2,1)}, bf16[256,1024]{1,0:T(8,128)(2,1)}, u32[]{:S(2)}, u32[]{:S(2)}) collective-permute-start(bf16[256,1024]{1,0:T(8,128)(2,1)} %bitcast.5.refs_1_), channel_id=1, source_target_pairs={{0,16},{16,0},{1,17},{17,1},{2,18},{18,2},{3,19},{19,3},{4,20},{20... | collective-permute-start | bytes 1572872 | tf_op jit(solution)/shard_map/ppermute | solution.py:479
  65.6 32.7 %all-to-all-start.2 = ((bf16[16,32,1024]{2,1,0:T(8,128)(2,1)}), bf16[16,32,1024]{2,1,0:T(8,128)(2,1)}, u32[]{:S(2)}, u32[]{:S(2)}) async-start(bf16[16,32,1024]{2,1,0:T(8,128)(2,1)} %bitcast.60), calls=%async_computation.2 | async-start | bytes 2097152 | tf_op jit(solution)/shard_map/all_to_all | solution.py:474
  76.4 4.5 %collective-permute-start.11 = (bf16[512,1024]{1,0:T(8,128)(2,1)}, bf16[512,1024]{1,0:T(8,128)(2,1)}, u32[]{:S(2)}, u32[]{:S(2)}) collective-permute-start(bf16[512,1024]{1,0:T(8,128)(2,1)} %get-tuple-element.68), channel_id=1, source_target_pairs={{0,8},{8,0},{1,9},{9,1},{2,10},{10,2},{3,11},{11,3},{4,12},{12,4},... | collective-permute-start | bytes 3145736 | tf_op jit(solution)/shard_map/ppermute | solution.py:483
  80.3 4.6 %collective-permute-start.8 = (bf16[512,1024]{1,0:T(8,128)(2,1)}, bf16[512,1024]{1,0:T(8,128)(2,1)}, u32[]{:S(2)}, u32[]{:S(2)}) collective-permute-start(bf16[512,1024]{1,0:T(8,128)(2,1)} %get-tuple-element.59), channel_id=1, source_target_pairs={{0,8},{8,0},{1,9},{9,1},{2,10},{10,2},{3,11},{11,3},{4,12},{12,4},... | collective-permute-start | bytes 3145736 | tf_op jit(solution)/shard_map/ppermute | solution.py:483
  83.1 27.4 %collective-permute-start.12 = (bf16[256,1024]{1,0:T(8,128)(2,1)}, bf16[256,1024]{1,0:T(8,128)(2,1)}, u32[]{:S(2)}, u32[]{:S(2)}) collective-permute-start(bf16[256,1024]{1,0:T(8,128)(2,1)} %add_convert_fusion), channel_id=1, source_target_pairs={{0,16},{16,0},{1,17},{17,1},{2,18},{18,2},{3,19},{19,3},{4,20},{20... | collective-permute-start | bytes 1572872 | tf_op jit(solution)/shard_map/ppermute | solution.py:479
  102.3 15.4 %all-to-all-start.3 = ((f32[32,8,128]{2,1,0:T(8,128)}), f32[32,8,128]{2,1,0:T(8,128)S(1)}, u32[]{:S(2)}, u32[]{:S(2)}) async-start(f32[32,8,128]{2,1,0:T(8,128)} %get-tuple-element.64), calls=%async_computation.3 | async-start | bytes 262144 | tf_op jit(solution)/shard_map/all_to_all | solution.py:499
  105.1 12.6 %collective-permute-start.9 = (bf16[16,1024]{1,0:T(8,128)(2,1)}, bf16[16,1024]{1,0:T(8,128)(2,1)S(1)}, u32[]{:S(2)}, u32[]{:S(2)}) collective-permute-start(bf16[16,1024]{1,0:T(8,128)(2,1)} %get-tuple-element.61), channel_id=1, source_target_pairs={{0,1},{1,2},{2,3},{3,4},{4,5},{5,6},{6,7},{7,8},{8,9},{9,10},{10,1... | collective-permute-start | bytes 98312 | tf_op jit(solution)/shard_map/ppermute | solution.py:491
  106.9 10.8 %collective-permute-start.10 = (bf16[16,1024]{1,0:T(8,128)(2,1)}, bf16[16,1024]{1,0:T(8,128)(2,1)S(1)}, u32[]{:S(2)}, u32[]{:S(2)}) collective-permute-start(bf16[16,1024]{1,0:T(8,128)(2,1)} %get-tuple-element.63), channel_id=1, source_target_pairs={{1,0},{2,1},{3,2},{4,3},{5,4},{6,5},{7,6},{8,7},{9,8},{10,9},{11,1... | collective-permute-start | bytes 98312 | tf_op jit(solution)/shard_map/ppermute | solution.py:491
  117.7 0.6 copy-start.3
  117.7 0.6 copy-start.4
  117.7 0.7 copy-start
  120.0 10.3 %all-to-all-start.4 = ((f32[32,8,128]{2,1,0:T(8,128)}), f32[32,8,128]{2,1,0:T(8,128)S(1)}, u32[]{:S(2)}, u32[]{:S(2)}) async-start(f32[32,8,128]{2,1,0:T(8,128)} %spread.1), calls=%async_computation.4 | async-start | bytes 262144 | tf_op jit(solution)/shard_map/all_to_all | solution.py:501

commit v7 on v6

--- a/solution.py
+++ b/solution.py
@@ -232,7 +232,7 @@
     up_refs = [take(1 + shard) for shard in range(len(place.shards))]
     depth = up_refs[0].shape[0]
     units = hidden_ref.shape[1]
-    chunk = 256
+    chunk = 512
 
     def step(index, carry):
         cols = at(index, chunk)

time: 132 us -> 132 us (level)
  no operation moved by 1% of the time
where the time goes in v7:
time: 132 us; the launch traced here: 131 us
  Pallas kernels  54.2 us (41%)
  starting transfers between devices  43.4 us (33%)
  waiting for transfers between devices  28.7 us (22%)
  other arithmetic  2.19 us (2%)
  local copies, waits for them, and re-layouts  1.64 us (1%)
    pallas_call x11, Pallas kernels, call(): pl.pallas_call(functools.partial(staged, kernel, counts, spans), out_shap...  39.6 us
    pallas_call x2, Pallas kernels, adam(): pl.pallas_call(functools.partial(adam_kernel, here, len(grads) - 2), grid...  14.5 us
    all_to_all x2, starting transfers between devices, by_expert(): lax.all_to_all(cells, 'expert', 0, 0, tiled=True).reshape(slots, width)  12.7 us
    all_to_all x2, waiting for transfers between devices, by_expert(): lax.all_to_all(cells, 'expert', 0, 0, tiled=True).reshape(slots, width)  12 us
    ppermute x4, starting transfers between devices, halo(): return (lax.ppermute(tail, axes, right), lax.ppermute(head, axes, left))  10.7 us
    all_to_all x1, starting transfers between devices, to_senders(): return lax.all_to_all(cells, axes, 0, 0, tiled=True).reshape(rows.shape)  6.99 us
    ppermute x4, starting transfers between devices, to_chip(): lax.ppermute(values, 'chip', [(i, (i + shift) % chips) for i in range(chi...  6.41 us
    ppermute x4, waiting for transfers between devices, to_chip(): lax.ppermute(values, 'chip', [(i, (i + shift) % chips) for i in range(chi...  6.15 us
  transfers between devices with their start and end apart: 18, of which 6 were waited for; matrix products, arithmetic and copies ran while one was open for 2% of the time, Pallas kernels for 34%

profile of v7, /device:TPU:0, one launch (start us, length us, event | category | flops | bytes accessed | tf_op | source)
XLA Modules:
  0.0 131.0 jit_solution(3750995735671316554)
XLA Ops:
  0.7 2.7 %prepare.1 = (bf16[16,1024]{1,0:T(8,128)(2,1)}, bf16[16,1024]{1,0:T(8,128)(2,1)}, bf16[256,128]{1,0:T(8,128)(2,1)}, bf16[256,1024]{1,0:T(8,128)(2,1)}, bf16[256,1024]{1,0:T(8,128)(2,1)}) custom-call(s32[1]{0:T(128)} %bitcast.refs_0_.index_ref, s32[1,128]{1,0:T(1,128)} %bitcast.70, bf16[128,1024]{1,0:T(8,128)(2,1)} %refs_5_.1, bf16[128,1024]{1,0:T(8,128)(2,1)} %refs_4_.4, ...), custom_call_target="tpu_custom_call" | custom-call | flops 67108864 | bytes 1048576 | tf_op jit(solution)/shard_map/prepare/pallas_call | solution.py:102
  3.4 7.3 %all-to-all-start.1 = ((bf16[8,32,1024]{2,1,0:T(8,128)(2,1)}), bf16[8,32,1024]{2,1,0:T(8,128)(2,1)}, u32[]{:S(2)}, u32[]{:S(2)}) async-start(bf16[8,32,1024]{2,1,0:T(8,128)(2,1)} %bitcast.63), calls=%async_computation.1 | async-start | bytes 1048576 | tf_op jit(solution)/shard_map/all_to_all | solution.py:467
  10.6 1.5 %collective-permute-start.2 = (bf16[256,1024]{1,0:T(8,128)(2,1)}, bf16[256,1024]{1,0:T(8,128)(2,1)}, u32[]{:S(2)}, u32[]{:S(2)}) collective-permute-start(bf16[256,1024]{1,0:T(8,128)(2,1)} %get-tuple-element.49), channel_id=1, source_target_pairs={{0,16},{16,0},{1,17},{17,1},{2,18},{18,2},{3,19},{19,3},{4,20},{20... | collective-permute-start | bytes 1572872 | tf_op jit(solution)/shard_map/ppermute | solution.py:479
  12.2 2.0 %collective-permute-start = (bf16[16,1024]{1,0:T(8,128)(2,1)}, bf16[16,1024]{1,0:T(8,128)(2,1)S(1)}, u32[]{:S(2)}, u32[]{:S(2)}) collective-permute-start(bf16[16,1024]{1,0:T(8,128)(2,1)} %get-tuple-element.46), channel_id=1, source_target_pairs={{0,1},{1,2},{2,3},{3,4},{4,5},{5,6},{6,7},{7,8},{8,9},{9,10},{10,1... | collective-permute-start | bytes 98312 | tf_op jit(solution)/shard_map/ppermute | solution.py:491
  14.2 3.3 %collective-permute-start.1 = (bf16[16,1024]{1,0:T(8,128)(2,1)}, bf16[16,1024]{1,0:T(8,128)(2,1)S(1)}, u32[]{:S(2)}, u32[]{:S(2)}) collective-permute-start(bf16[16,1024]{1,0:T(8,128)(2,1)} %get-tuple-element.47), channel_id=1, source_target_pairs={{1,0},{2,1},{3,2},{4,3},{5,4},{6,5},{7,6},{8,7},{9,8},{10,9},{11,1... | collective-permute-start | bytes 98312 | tf_op jit(solution)/shard_map/ppermute | solution.py:491
  17.5 3.3 %cast_near.1 = (bf16[256,1024]{1,0:T(8,128)(2,1)}, bf16[512,1024]{1,0:T(8,128)(2,1)}) custom-call(s32[1]{0:T(128)} %bitcast.refs_0_.index_ref, f32[256,2048]{1,0:T(8,128)} %bitcast.50, f32[512,1024]{1,0:T(8,128)} %bitcast.52, bf16[256,128]{1,0:T(8,128)(2,1)} %get-tuple-element.45.refs_3_.refs_5_.refs_1_), custom_call_target="tpu_custom_call" | custom-call | bytes 6291456 | tf_op jit(solution)/shard_map/cast_near/pallas_call | solution.py:102
  20.8 3.3 %convolve.1.refs_3_ = f32[128,1024]{1,0:T(8,128)} custom-call(bf16[128,1024]{1,0:T(8,128)(2,1)} %refs_4_.4, f32[32,1024]{1,0:T(8,128)} %refs_4_.5, bf16[512,1024]{1,0:T(8,128)(2,1)} %get-tuple-element.48.refs_2_.refs_7_), custom_call_target="tpu_custom_call" | custom-call | flops 67108864 | bytes 2097152 | tf_op jit(solution)/shard_map/convolve/pallas_call | solution.py:102
  24.1 0.3 collective-permute-done.refs_1_.refs_3_
  24.4 0.0 collective-permute-done.1.refs_2_.refs_5_
  24.4 0.3 collective-permute-done.2.refs_6_.refs_4_
  24.7 0.3 copy-done.1
  25.0 0.0 copy-done.2
  25.0 3.2 %edges.1 = (bf16[128,1024]{1,0:T(8,128)(2,1)}, bf16[256,1024]{1,0:T(8,128)(2,1)}) custom-call(s32[1]{0:T(128)} %bitcast.refs_0_.index_ref, bf16[16,1024]{1,0:T(8,128)(2,1)} %copy-done.1, bf16[16,1024]{1,0:T(8,128)(2,1)} %copy-done.2, f32[128,1024]{1,0:T(8,128)} %convolve.1.refs_3_, f32[32,1024]{1,0:T(8,128)} %refs_4_.5, ...), custom_call_target="tpu_custom_call" | custom-call | flops 67108864 | bytes 2097152 | tf_op jit(solution)/shard_map/edges/pallas_call | solution.py:102
  28.2 5.4 %all-to-all-start = ((bf16[8,32,1024]{2,1,0:T(8,128)(2,1)}), bf16[8,32,1024]{2,1,0:T(8,128)(2,1)}, u32[]{:S(2)}, u32[]{:S(2)}) async-start(bf16[8,32,1024]{2,1,0:T(8,128)(2,1)} %bitcast.64), calls=%async_computation | async-start | bytes 1048576 | tf_op jit(solution)/shard_map/all_to_all | solution.py:467
  33.6 0.0 collective-permute-start.7
  33.6 0.5 collective-permute-start.4
  34.1 0.1 collective-permute-start.5
  34.2 1.5 %collective-permute-start.6 = (bf16[256,1024]{1,0:T(8,128)(2,1)}, bf16[256,1024]{1,0:T(8,128)(2,1)}, u32[]{:S(2)}, u32[]{:S(2)}) collective-permute-start(bf16[256,1024]{1,0:T(8,128)(2,1)} %bitcast.7.refs_6_.refs_3_), channel_id=1, source_target_pairs={{0,16},{16,0},{1,17},{17,1},{2,18},{18,2},{3,19},{19,3},{4,20},{20... | collective-permute-start | bytes 1572872 | tf_op jit(solution)/shard_map/ppermute | solution.py:479
  35.7 12.0 %all-to-all-done = bf16[8,32,1024]{2,1,0:T(8,128)(2,1)} async-done(((bf16[8,32,1024]{2,1,0:T(8,128)(2,1)}), bf16[8,32,1024]{2,1,0:T(8,128)(2,1)}, u32[]{:S(2)}, u32[]{:S(2)}) %all-to-all-start) | async-done | bytes 524320 | tf_op jit(solution)/shard_map/all_to_all | solution.py:467
  47.7 1.5 %collective-permute-start.3 = (bf16[256,1024]{1,0:T(8,128)(2,1)}, bf16[256,1024]{1,0:T(8,128)(2,1)}, u32[]{:S(2)}, u32[]{:S(2)}) collective-permute-start(bf16[256,1024]{1,0:T(8,128)(2,1)} %bitcast.5.refs_1_), channel_id=1, source_target_pairs={{0,16},{16,0},{1,17},{17,1},{2,18},{18,2},{3,19},{19,3},{4,20},{20... | collective-permute-start | bytes 1572872 | tf_op jit(solution)/shard_map/ppermute | solution.py:479
  49.2 0.0 collective-permute-done.4.refs_3_
  49.2 0.0 collective-permute-done.5.refs_5_
  49.2 5.1 %own_group.1 = (bf16[256,1024]{1,0:T(8,128)(2,1)}, bf16[256,1024]{1,0:T(8,128)(2,1)}, bf16[256,1024]{1,0:T(8,128)(2,1)}) custom-call(s32[1]{0:T(128)} %bitcast.refs_0_.index_ref, bf16[256,1024]{1,0:T(8,128)(2,1)} %bitcast.5.refs_1_, bf16[256,1024]{1,0:T(8,128)(2,1)} %get-tuple-element.52.refs_2_, bf16[256,1024]{1,0:T(8,128)(2,1)} %collective-permute-done.4.refs_3_, ...), custom_call_target="tpu_custom_call" | custom-call | flops 1610612736 | bytes 8388608 | tf_op jit(solution)/shard_map/own_group/pallas_call | solution.py:102
  54.3 5.9 %collective-permute-done.3.refs_1_.refs_2_ = bf16[256,1024]{1,0:T(8,128)(2,1)} collective-permute-done((bf16[256,1024]{1,0:T(8,128)(2,1)}, bf16[256,1024]{1,0:T(8,128)(2,1)}, u32[]{:S(2)}, u32[]{:S(2)}) %collective-permute-start.3) | collective-permute-done | bytes 524320 | tf_op jit(solution)/shard_map/ppermute | solution.py:479
  60.1 5.4 %far_group.1 = (bf16[256,1024]{1,0:T(8,128)(2,1)}, bf16[256,1024]{1,0:T(8,128)(2,1)}, bf16[512,1024]{1,0:T(8,128)(2,1)}) custom-call(s32[1]{0:T(128)} %bitcast.refs_0_.index_ref, bf16[256,1024]{1,0:T(8,128)(2,1)} %collective-permute-done.3.refs_1_.refs_2_, bf16[256,1024]{1,0:T(8,128)(2,1)} %get-tuple-element.52.refs_2_, ...), custom_call_target="tpu_custom_call" | custom-call | flops 1610612736 | bytes 8388608 | tf_op jit(solution)/shard_map/far_group/pallas_call | solution.py:102
  65.6 7.0 %all-to-all-start.2 = ((bf16[16,32,1024]{2,1,0:T(8,128)(2,1)}), bf16[16,32,1024]{2,1,0:T(8,128)(2,1)}, u32[]{:S(2)}, u32[]{:S(2)}) async-start(bf16[16,32,1024]{2,1,0:T(8,128)(2,1)} %bitcast.60), calls=%async_computation.2 | async-start | bytes 2097152 | tf_op jit(solution)/shard_map/all_to_all | solution.py:474
  72.6 3.8 %up_grad.1 = (bf16[512,1024]{1,0:T(8,128)(2,1)}, bf16[512,1024]{1,0:T(8,128)(2,1)}) custom-call(s32[1]{0:T(128)} %bitcast.refs_0_.index_ref, bf16[256,1024]{1,0:T(8,128)(2,1)} %bitcast.5.refs_1_, bf16[256,1024]{1,0:T(8,128)(2,1)} %collective-permute-done.3.refs_1_.refs_2_, bf16[256,1024]{1,0:T(8,128)(2,1)} %get-tuple-element.65.refs_3_, ...), custom_call_target="tpu_custom_call" | custom-call | flops 1073741824 | bytes 8388608 | tf_op jit(solution)/shard_map/up_grad/pallas_call | solution.py:102
  76.4 0.1 collective-permute-start.11
  76.5 3.8 %down_grad.1 = (bf16[512,1024]{1,0:T(8,128)(2,1)}, bf16[512,1024]{1,0:T(8,128)(2,1)}) custom-call(s32[1]{0:T(128)} %bitcast.refs_0_.index_ref, bf16[256,1024]{1,0:T(8,128)(2,1)} %get-tuple-element.56.refs_1_, bf16[256,1024]{1,0:T(8,128)(2,1)} %get-tuple-element.57.refs_2_, bf16[256,1024]{1,0:T(8,128)(2,1)} %bitcast.7.refs_6_.refs_3_, ...), custom_call_target="tpu_custom_call" | custom-call | flops 1073741824 | bytes 8388608 | tf_op jit(solution)/shard_map/down_grad/pallas_call | solution.py:102
  80.3 0.6 collective-permute-start.8
  80.9 2.2 %add_convert_fusion = bf16[256,1024]{1,0:T(8,128)(2,1)} fusion(bf16[512,1024]{1,0:T(8,128)(2,1)} %collective-permute-done.11.refs_1_, bf16[512,1024]{1,0:T(8,128)(2,1)} %get-tuple-element.67.refs_0_), kind=kLoop, calls=%fused_computation | loop fusion | flops 1048576 | bytes 1572864 | tf_op jit(solution)/shard_map/convert_element_type | solution.py:629
  83.1 1.9 %collective-permute-start.12 = (bf16[256,1024]{1,0:T(8,128)(2,1)}, bf16[256,1024]{1,0:T(8,128)(2,1)}, u32[]{:S(2)}, u32[]{:S(2)}) collective-permute-start(bf16[256,1024]{1,0:T(8,128)(2,1)} %add_convert_fusion), channel_id=1, source_target_pairs={{0,16},{16,0},{1,17},{17,1},{2,18},{18,2},{3,19},{19,3},{4,20},{20... | collective-permute-start | bytes 1572872 | tf_op jit(solution)/shard_map/ppermute | solution.py:479
  84.9 7.3 %adam_down.1 = (f32[512,1024]{1,0:T(8,128)}, bf16[512,1024]{1,0:T(8,128)(2,1)}, f32[8,512]{1,0:T(8,128)}, bf16[512,1024]{1,0:T(8,128)(2,1)}, f32[8,512]{1,0:T(8,128)}) custom-call(s32[1]{0:T(128)} %bitcast.refs_0_.index_ref, f32[512,1024]{1,0:T(8,128)} %bitcast.53, bf16[512,1024]{1,0:T(8,128)(2,1)} %bitcast.58, f32[8,512]{1,0:T(8,128)} %bitcast.66, ...), custom_call_target="tpu_custom_call" | custom-call | flops 10485760 | bytes 10485760 | tf_op jit(solution)/shard_map/adam_down/pallas_call | solution.py:439
  92.3 6.0 %all-to-all-done.2 = bf16[16,32,1024]{2,1,0:T(8,128)(2,1)} async-done(((bf16[16,32,1024]{2,1,0:T(8,128)(2,1)}), bf16[16,32,1024]{2,1,0:T(8,128)(2,1)}, u32[]{:S(2)}, u32[]{:S(2)}) %all-to-all-start.2) | async-done | bytes 1048608 | tf_op jit(solution)/shard_map/all_to_all | solution.py:474
  98.3 4.0 %taps.1 = (bf16[128,1024]{1,0:T(8,128)(2,1)}, bf16[16,1024]{1,0:T(8,128)(2,1)}, bf16[16,1024]{1,0:T(8,128)(2,1)}, f32[32,8,128]{2,1,0:T(8,128)}) custom-call(s32[1]{0:T(128)} %bitcast.refs_0_.index_ref, bf16[256,128]{1,0:T(8,128)(2,1)} %get-tuple-element.45.refs_3_.refs_5_.refs_1_, bf16[128,1024]{1,0:T(8,128)(2,1)} %get-tuple-element.50.refs_2_, ...), custom_call_target="tpu_custom_call" | custom-call | flops 67108864 | bytes 2097152 | tf_op jit(solution)/shard_map/taps/pallas_call | solution.py:102
  102.3 2.8 %all-to-all-start.3 = ((f32[32,8,128]{2,1,0:T(8,128)}), f32[32,8,128]{2,1,0:T(8,128)S(1)}, u32[]{:S(2)}, u32[]{:S(2)}) async-start(f32[32,8,128]{2,1,0:T(8,128)} %get-tuple-element.64), calls=%async_computation.3 | async-start | bytes 262144 | tf_op jit(solution)/shard_map/all_to_all | solution.py:499
  105.1 1.8 %collective-permute-start.9 = (bf16[16,1024]{1,0:T(8,128)(2,1)}, bf16[16,1024]{1,0:T(8,128)(2,1)S(1)}, u32[]{:S(2)}, u32[]{:S(2)}) collective-permute-start(bf16[16,1024]{1,0:T(8,128)(2,1)} %get-tuple-element.61), channel_id=1, source_target_pairs={{0,1},{1,2},{2,3},{3,4},{4,5},{5,6},{6,7},{7,8},{8,9},{9,10},{10,1... | collective-permute-start | bytes 98312 | tf_op jit(solution)/shard_map/ppermute | solution.py:491
  106.9 3.6 %collective-permute-start.10 = (bf16[16,1024]{1,0:T(8,128)(2,1)}, bf16[16,1024]{1,0:T(8,128)(2,1)S(1)}, u32[]{:S(2)}, u32[]{:S(2)}) collective-permute-start(bf16[16,1024]{1,0:T(8,128)(2,1)} %get-tuple-element.63), channel_id=1, source_target_pairs={{1,0},{2,1},{3,2},{4,3},{5,4},{6,5},{7,6},{8,7},{9,8},{10,9},{11,1... | collective-permute-start | bytes 98312 | tf_op jit(solution)/shard_map/ppermute | solution.py:491
  110.5 7.2 %adam_up.1 = (f32[256,2048]{1,0:T(8,128)}, bf16[256,2048]{1,0:T(8,128)(2,1)}, f32[16,256]{1,0:T(8,128)}, bf16[256,2048]{1,0:T(8,128)(2,1)}, f32[16,256]{1,0:T(8,128)}) custom-call(s32[1]{0:T(128)} %bitcast.refs_0_.index_ref, f32[256,2048]{1,0:T(8,128)} %bitcast.51, bf16[256,2048]{1,0:T(8,128)(2,1)} %bitcast.61, f32[16,256]{1,0:T(8,128)} %bitcast.68, ...), custom_call_target="tpu_custom_call" | custom-call | flops 10485760 | bytes 11534336 | tf_op jit(solution)/shard_map/adam_up/pallas_call | solution.py:439
  117.7 0.0 copy-start
  117.7 0.5 copy-done.3
  118.3 0.0 copy-done.4
  118.3 0.1 copy-done
  118.4 1.6 %spread.1 = f32[32,8,128]{2,1,0:T(8,128)} custom-call(f32[32,8,128]{2,1,0:T(8,128)} %copy-done, f32[1,256,2048]{2,1,0:T(8,128)} %bitcast.54, bf16[16,1024]{1,0:T(8,128)(2,1)} %copy-done.3, bf16[16,1024]{1,0:T(8,128)(2,1)} %copy-done.4), custom_call_target="tpu_custom_call" | custom-call | tf_op jit(solution)/shard_map/spread/pallas_call | solution.py:102
  120.0 2.6 %all-to-all-start.4 = ((f32[32,8,128]{2,1,0:T(8,128)}), f32[32,8,128]{2,1,0:T(8,128)S(1)}, u32[]{:S(2)}, u32[]{:S(2)}) async-start(f32[32,8,128]{2,1,0:T(8,128)} %spread.1), calls=%async_computation.4 | async-start | bytes 262144 | tf_op jit(solution)/shard_map/all_to_all | solution.py:501
  122.6 3.4 %frames.1 = bf16[128,1024]{1,0:T(8,128)(2,1)} custom-call(s32[1]{0:T(128)} %bitcast.refs_0_.index_ref, bf16[16,1024]{1,0:T(8,128)(2,1)} %copy-done.3, bf16[128,1024]{1,0:T(8,128)(2,1)} %get-tuple-element.62.refs_2_, bf16[16,1024]{1,0:T(8,128)(2,1)} %copy-done.4, f32[32,1024]{1,0:T(8,128)} %refs_4_.5, bf16[128,1024]{1,0:T(8,128)(2,1)} %refs_5_.1), custom_call_target="tpu_custom_call" | custom-call | flops 67108864 | bytes 1048576 | tf_op jit(solution)/shard_map/frames/pallas_call | solution.py:102
  126.0 4.3 %all-to-all-done.4 = f32[32,8,128]{2,1,0:T(8,128)S(1)} async-done(((f32[32,8,128]{2,1,0:T(8,128)}), f32[32,8,128]{2,1,0:T(8,128)S(1)}, u32[]{:S(2)}, u32[]{:S(2)}) %all-to-all-start.4) | async-done | bytes 131104 | tf_op jit(solution)/shard_map/all_to_all | solution.py:501
  130.3 0.7 copy.27
  (13 shorter events, 0.0 us)
Async XLA Ops:
  3.4 24.8 %all-to-all-start.1 = ((bf16[8,32,1024]{2,1,0:T(8,128)(2,1)}), bf16[8,32,1024]{2,1,0:T(8,128)(2,1)}, u32[]{:S(2)}, u32[]{:S(2)}) async-start(bf16[8,32,1024]{2,1,0:T(8,128)(2,1)} %bitcast.63), calls=%async_computation.1 | async-start | bytes 1048576 | tf_op jit(solution)/shard_map/all_to_all | solution.py:467
  10.6 14.1 %collective-permute-start.2 = (bf16[256,1024]{1,0:T(8,128)(2,1)}, bf16[256,1024]{1,0:T(8,128)(2,1)}, u32[]{:S(2)}, u32[]{:S(2)}) collective-permute-start(bf16[256,1024]{1,0:T(8,128)(2,1)} %get-tuple-element.49), channel_id=1, source_target_pairs={{0,16},{16,0},{1,17},{17,1},{2,18},{18,2},{3,19},{19,3},{4,20},{20... | collective-permute-start | bytes 1572872 | tf_op jit(solution)/shard_map/ppermute | solution.py:479
  12.2 12.2 %collective-permute-start = (bf16[16,1024]{1,0:T(8,128)(2,1)}, bf16[16,1024]{1,0:T(8,128)(2,1)S(1)}, u32[]{:S(2)}, u32[]{:S(2)}) collective-permute-start(bf16[16,1024]{1,0:T(8,128)(2,1)} %get-tuple-element.46), channel_id=1, source_target_pairs={{0,1},{1,2},{2,3},{3,4},{4,5},{5,6},{6,7},{7,8},{8,9},{9,10},{10,1... | collective-permute-start | bytes 98312 | tf_op jit(solution)/shard_map/ppermute | solution.py:491
  14.2 10.2 %collective-permute-start.1 = (bf16[16,1024]{1,0:T(8,128)(2,1)}, bf16[16,1024]{1,0:T(8,128)(2,1)S(1)}, u32[]{:S(2)}, u32[]{:S(2)}) collective-permute-start(bf16[16,1024]{1,0:T(8,128)(2,1)} %get-tuple-element.47), channel_id=1, source_target_pairs={{1,0},{2,1},{3,2},{4,3},{5,4},{6,5},{7,6},{8,7},{9,8},{10,9},{11,1... | collective-permute-start | bytes 98312 | tf_op jit(solution)/shard_map/ppermute | solution.py:491
  24.4 0.6 copy-start.1
  24.4 0.6 copy-start.2
  28.2 19.5 %all-to-all-start = ((bf16[8,32,1024]{2,1,0:T(8,128)(2,1)}), bf16[8,32,1024]{2,1,0:T(8,128)(2,1)}, u32[]{:S(2)}, u32[]{:S(2)}) async-start(bf16[8,32,1024]{2,1,0:T(8,128)(2,1)} %bitcast.64), calls=%async_computation | async-start | bytes 1048576 | tf_op jit(solution)/shard_map/all_to_all | solution.py:467
  33.6 15.6 %collective-permute-start.7 = (bf16[512,1024]{1,0:T(8,128)(2,1)}, bf16[512,1024]{1,0:T(8,128)(2,1)}, u32[]{:S(2)}, u32[]{:S(2)}) collective-permute-start(bf16[512,1024]{1,0:T(8,128)(2,1)} %get-tuple-element.48.refs_2_.refs_7_), channel_id=1, source_target_pairs={{0,8},{8,0},{1,9},{9,1},{2,10},{10,2},{3,11},{11,3},{4,12},{12,4},... | collective-permute-start | bytes 3145736 | tf_op jit(solution)/shard_map/ppermute | solution.py:483
  33.6 15.6 %collective-permute-start.4 = (bf16[256,1024]{1,0:T(8,128)(2,1)}, bf16[256,1024]{1,0:T(8,128)(2,1)}, u32[]{:S(2)}, u32[]{:S(2)}) collective-permute-start(bf16[256,1024]{1,0:T(8,128)(2,1)} %get-tuple-element.52.refs_2_), channel_id=1, source_target_pairs={{0,8},{8,0},{1,9},{9,1},{2,10},{10,2},{3,11},{11,3},{4,12},{12,4},... | collective-permute-start | bytes 1572872 | tf_op jit(solution)/shard_map/ppermute | solution.py:483
  34.1 15.1 %collective-permute-start.5 = (bf16[256,1024]{1,0:T(8,128)(2,1)}, bf16[256,1024]{1,0:T(8,128)(2,1)}, u32[]{:S(2)}, u32[]{:S(2)}) collective-permute-start(bf16[256,1024]{1,0:T(8,128)(2,1)} %collective-permute-done.2.refs_6_.refs_4_), channel_id=1, source_target_pairs={{0,8},{8,0},{1,9},{9,1},{2,10},{10,2},{3,11},{11,3},{4,12},{12,4},... | collective-permute-start | bytes 1572872 | tf_op jit(solution)/shard_map/ppermute | solution.py:483
  34.2 20.1 %collective-permute-start.6 = (bf16[256,1024]{1,0:T(8,128)(2,1)}, bf16[256,1024]{1,0:T(8,128)(2,1)}, u32[]{:S(2)}, u32[]{:S(2)}) collective-permute-start(bf16[256,1024]{1,0:T(8,128)(2,1)} %bitcast.7.refs_6_.refs_3_), channel_id=1, source_target_pairs={{0,16},{16,0},{1,17},{17,1},{2,18},{18,2},{3,19},{19,3},{4,20},{20... | collective-permute-start | bytes 1572872 | tf_op jit(solution)/shard_map/ppermute | solution.py:479
  47.7 12.5 %collective-permute-start.3 = (bf16[256,1024]{1,0:T(8,128)(2,1)}, bf16[256,1024]{1,0:T(8,128)(2,1)}, u32[]{:S(2)}, u32[]{:S(2)}) collective-permute-start(bf16[256,1024]{1,0:T(8,128)(2,1)} %bitcast.5.refs_1_), channel_id=1, source_target_pairs={{0,16},{16,0},{1,17},{17,1},{2,18},{18,2},{3,19},{19,3},{4,20},{20... | collective-permute-start | bytes 1572872 | tf_op jit(solution)/shard_map/ppermute | solution.py:479
  65.6 32.7 %all-to-all-start.2 = ((bf16[16,32,1024]{2,1,0:T(8,128)(2,1)}), bf16[16,32,1024]{2,1,0:T(8,128)(2,1)}, u32[]{:S(2)}, u32[]{:S(2)}) async-start(bf16[16,32,1024]{2,1,0:T(8,128)(2,1)} %bitcast.60), calls=%async_computation.2 | async-start | bytes 2097152 | tf_op jit(solution)/shard_map/all_to_all | solution.py:474
  76.4 4.5 %collective-permute-start.11 = (bf16[512,1024]{1,0:T(8,128)(2,1)}, bf16[512,1024]{1,0:T(8,128)(2,1)}, u32[]{:S(2)}, u32[]{:S(2)}) collective-permute-start(bf16[512,1024]{1,0:T(8,128)(2,1)} %get-tuple-element.68), channel_id=1, source_target_pairs={{0,8},{8,0},{1,9},{9,1},{2,10},{10,2},{3,11},{11,3},{4,12},{12,4},... | collective-permute-start | bytes 3145736 | tf_op jit(solution)/shard_map/ppermute | solution.py:483
  80.3 4.6 %collective-permute-start.8 = (bf16[512,1024]{1,0:T(8,128)(2,1)}, bf16[512,1024]{1,0:T(8,128)(2,1)}, u32[]{:S(2)}, u32[]{:S(2)}) collective-permute-start(bf16[512,1024]{1,0:T(8,128)(2,1)} %get-tuple-element.59), channel_id=1, source_target_pairs={{0,8},{8,0},{1,9},{9,1},{2,10},{10,2},{3,11},{11,3},{4,12},{12,4},... | collective-permute-start | bytes 3145736 | tf_op jit(solution)/shard_map/ppermute | solution.py:483
  83.1 27.4 %collective-permute-start.12 = (bf16[256,1024]{1,0:T(8,128)(2,1)}, bf16[256,1024]{1,0:T(8,128)(2,1)}, u32[]{:S(2)}, u32[]{:S(2)}) collective-permute-start(bf16[256,1024]{1,0:T(8,128)(2,1)} %add_convert_fusion), channel_id=1, source_target_pairs={{0,16},{16,0},{1,17},{17,1},{2,18},{18,2},{3,19},{19,3},{4,20},{20... | collective-permute-start | bytes 1572872 | tf_op jit(solution)/shard_map/ppermute | solution.py:479
  102.3 15.4 %all-to-all-start.3 = ((f32[32,8,128]{2,1,0:T(8,128)}), f32[32,8,128]{2,1,0:T(8,128)S(1)}, u32[]{:S(2)}, u32[]{:S(2)}) async-start(f32[32,8,128]{2,1,0:T(8,128)} %get-tuple-element.64), calls=%async_computation.3 | async-start | bytes 262144 | tf_op jit(solution)/shard_map/all_to_all | solution.py:499
  105.1 12.6 %collective-permute-start.9 = (bf16[16,1024]{1,0:T(8,128)(2,1)}, bf16[16,1024]{1,0:T(8,128)(2,1)S(1)}, u32[]{:S(2)}, u32[]{:S(2)}) collective-permute-start(bf16[16,1024]{1,0:T(8,128)(2,1)} %get-tuple-element.61), channel_id=1, source_target_pairs={{0,1},{1,2},{2,3},{3,4},{4,5},{5,6},{6,7},{7,8},{8,9},{9,10},{10,1... | collective-permute-start | bytes 98312 | tf_op jit(solution)/shard_map/ppermute | solution.py:491
  106.9 10.8 %collective-permute-start.10 = (bf16[16,1024]{1,0:T(8,128)(2,1)}, bf16[16,1024]{1,0:T(8,128)(2,1)S(1)}, u32[]{:S(2)}, u32[]{:S(2)}) collective-permute-start(bf16[16,1024]{1,0:T(8,128)(2,1)} %get-tuple-element.63), channel_id=1, source_target_pairs={{1,0},{2,1},{3,2},{4,3},{5,4},{6,5},{7,6},{8,7},{9,8},{10,9},{11,1... | collective-permute-start | bytes 98312 | tf_op jit(solution)/shard_map/ppermute | solution.py:491
  117.7 0.6 copy-start.3
  117.7 0.6 copy-start.4
  117.7 0.7 copy-start
  120.0 10.3 %all-to-all-start.4 = ((f32[32,8,128]{2,1,0:T(8,128)}), f32[32,8,128]{2,1,0:T(8,128)S(1)}, u32[]{:S(2)}, u32[]{:S(2)}) async-start(f32[32,8,128]{2,1,0:T(8,128)} %spread.1), calls=%async_computation.4 | async-start | bytes 262144 | tf_op jit(solution)/shard_map/all_to_all | solution.py:501
